TPU v7x, 256 devices: a whole 4x4x8 slice. The times are simulated.
256 devices in a mesh: lat: 8 (over z), lon: 16 (over y, x_lo, core), grp: 2 (over x_hi).
Axes of the slice: x: 4 (x_hi: 2, x_lo: 2; x = x_hi * 2 + x_lo), y: 4, z: 8, core: 2. Of those that a mesh axis runs over, the one named last changes fastest.
Arguments:
- columns: float32 [2, 278, 128, 2048], P('grp', None, 'lat', 'lon'), may hold values from -6 to 6
- east_courant: float32 [128, 2048], P('lat', 'lon'), may hold values from 0.05 to 0.45
- north_courant: float32 [128, 2048], P('lat', 'lon'), may hold values from 0.05 to 0.45
- assign: int32 [8, 16, 16], replicated, may hold values from 0 to 255, as said below
- block_cost: int32 [8, 16, 16], replicated, may hold values from 1 to 128, as said below
- w_in: bfloat16 [556, 384], replicated, may hold values from -0.25 to 0.25
- w_mid: bfloat16 [384, 384], replicated, may hold values from -0.3125 to 0.3125
- w_out: bfloat16 [384, 368], replicated, may hold values from -0.3125 to 0.3125
- energy: float32 [368], replicated, may hold values from -4 to 4
Outputs:
- new_columns: float32 [2, 278, 128, 2048], P('grp', None, 'lat', 'lon')
- gradients: float32 [502272], P('grp')
Inputs may be any that keep to these rules, and one draw needn't show every extreme that they name: For each band b, assign[b] holds every number 0 to 255 once. The blocks of one device that go to one physics device of its band number 0 or exactly 1. `block_cost`: every band has a block with all 128 columns live.
All inputs are finite; a program needn't handle non-finite values.
Results may differ from a plain program's by a relative error of at most 0.0019.
Values may be sent and summed in bfloat16 or wider, within the bound.
No kernel may reach another device: no remote copies, remote signals or barrier semaphores. Data moves between devices by JAX's collectives and lax.ppermute only.
A program may use at most 128 MiB of HBM per device.

v0:
```python
import math

import jax
import jax.numpy as jnp
from jax import lax
from jax.sharding import PartitionSpec as P

step_weight = 0.5


def passed_along(value, axis, steps):
    count = lax.axis_size(axis)
    pairs = [(source, (source + steps) % count) for source in range(count)]
    return lax.ppermute(value, axis, pairs)


def from_behind(block, axis, distance):
    devices = range(lax.axis_size(axis))
    route = [(i - distance, i) for i in devices if i - distance in devices]
    return lax.ppermute(block, axis, route)


def upwind(grid_field, east_courant, north_courant, top_band):
    flux_x = east_courant[None] * grid_field
    flux_y = north_courant[None] * grid_field
    row_ids = lax.broadcasted_iota(jnp.int32, flux_y.shape, 1)
    flux_y = jnp.where(jnp.logical_and(row_ids == flux_y.shape[1] - 1, top_band), 0.0, flux_y)
    west_rim = passed_along(flux_x[:, :, -1:], "lon", 1)
    inflow_x = jnp.concatenate([west_rim, flux_x[:, :, :-1]], axis=2)
    south_rim = from_behind(flux_y[:, -1:, :], "lat", 1)
    inflow_y = jnp.concatenate([south_rim, flux_y[:, :-1, :]], axis=1)
    return grid_field - flux_x + inflow_x - flux_y + inflow_y


def silu_slope(pre_act):
    sigmoid_value = jax.nn.sigmoid(pre_act)
    return sigmoid_value * (1.0 + pre_act * (1.0 - sigmoid_value))


def network(inputs, live_mask, w_in, w_mid, w_out, energy, loss_norm):
    pre_one = jnp.dot(w_in.T, inputs, preferred_element_type=jnp.float32)
    hidden_one = jax.nn.silu(pre_one).astype(jnp.bfloat16)
    pre_two = jnp.dot(w_mid.T, hidden_one, preferred_element_type=jnp.float32)
    hidden_two = jax.nn.silu(pre_two).astype(jnp.bfloat16)
    result = jnp.dot(w_out.T, hidden_two, preferred_element_type=jnp.float32).astype(jnp.bfloat16)
    column_energy = jnp.sum(energy[:, None] * result.astype(jnp.float32), axis=0) / math.sqrt(
        energy.shape[0]
    )
    g_result = (energy[:, None] * (live_mask * column_energy * loss_norm)[None, :]).astype(
        jnp.bfloat16
    )
    d_out = jnp.dot(hidden_two, g_result.T, preferred_element_type=jnp.float32)
    g_two = (
        jnp.dot(w_out, g_result, preferred_element_type=jnp.float32) * silu_slope(pre_two)
    ).astype(jnp.bfloat16)
    d_mid = jnp.dot(hidden_one, g_two.T, preferred_element_type=jnp.float32)
    g_one = (
        jnp.dot(w_mid, g_two, preferred_element_type=jnp.float32) * silu_slope(pre_one)
    ).astype(jnp.bfloat16)
    d_in = jnp.dot(inputs, g_one.T, preferred_element_type=jnp.float32)
    return (result, jnp.concatenate([d_in.reshape(-1), d_mid.reshape(-1), d_out.reshape(-1)]))


def on_device(columns, east_courant, north_courant, assign, block_cost, w_in, w_mid, w_out, energy):
    lon_count = lax.axis_size("lon")
    band_count = lax.axis_size("lat")
    grp_count = lax.axis_size("grp")
    band_index = lax.axis_index("lat")
    lon_index = lax.axis_index("lon")
    grp_index = lax.axis_index("grp")
    half_width = columns.shape[1]
    lat_rows = columns.shape[2]
    block_width = columns.shape[3]
    pair_cap = max(1, lat_rows // lon_count)
    stored = columns[0]
    is_physics = grp_index == 1
    top_band = band_index == band_count - 1
    state_field = upwind(stored, east_courant, north_courant, top_band)
    state_field = upwind(state_field, east_courant, north_courant, top_band)
    targets = lax.dynamic_index_in_dim(assign, band_index, 0, keepdims=False)
    band_cost = lax.dynamic_index_in_dim(block_cost, band_index, 0, keepdims=False)
    owner_ids = targets // lat_rows
    block_ids = lax.broadcasted_iota(jnp.int32, (lat_rows, lat_rows), 0)
    other_ids = lax.broadcasted_iota(jnp.int32, (lat_rows, lat_rows), 1)
    earlier = other_ids < block_ids
    same_owner = owner_ids[:, :, None] == owner_ids[:, None, :]
    ranks = jnp.sum(jnp.logical_and(same_owner, earlier[None]), axis=2)
    own_owner = lax.dynamic_index_in_dim(owner_ids, lon_index, 0, keepdims=False)
    own_rank = lax.dynamic_index_in_dim(ranks, lon_index, 0, keepdims=False)
    dest_ids = lax.broadcasted_iota(jnp.int32, (lon_count, pair_cap, lat_rows), 0)
    pair_ids = lax.broadcasted_iota(jnp.int32, (lon_count, pair_cap, lat_rows), 1)
    send_table = jnp.logical_and(
        own_owner[None, None, :] == dest_ids, own_rank[None, None, :] == pair_ids
    ).astype(jnp.bfloat16)
    slot_ids = lon_index * lat_rows + lax.broadcasted_iota(jnp.int32, (lat_rows,), 0)
    match = targets[None, :, :] == slot_ids[:, None, None]
    rank_pick = ranks[None, :, None, :] == lax.broadcasted_iota(jnp.int32, (1, 1, pair_cap, 1), 2)
    recv_table = jnp.any(jnp.logical_and(match[:, :, None, :], rank_pick), axis=3).astype(
        jnp.bfloat16
    )
    arrived = from_behind(state_field.astype(jnp.bfloat16), "grp", 1)
    outgoing = jnp.einsum(
        "dqk,fkc->dqfc", send_table, arrived, preferred_element_type=jnp.float32
    ).astype(jnp.bfloat16)
    received = lax.all_to_all(outgoing, "lon", split_axis=0, concat_axis=0, tiled=True)
    incoming = jnp.einsum(
        "sjq,jqfc->fsc", recv_table, received, preferred_element_type=jnp.float32
    ).astype(jnp.bfloat16)
    slot_cost = jnp.sum(jnp.where(match, band_cost[None], 0), axis=(1, 2))
    column_ids = lax.broadcasted_iota(jnp.int32, (lat_rows, block_width), 1)
    slot_live = (column_ids < slot_cost[:, None]).astype(jnp.float32)
    inputs = jnp.concatenate([incoming, stored.astype(jnp.bfloat16)], axis=0).reshape(
        -1, lat_rows * block_width
    )
    live_flat = slot_live.reshape(-1)
    loss_norm = 1.0 / math.sqrt(lat_rows * band_count * block_width * lon_count)
    outputs, gradient = network(
        inputs, live_flat * is_physics.astype(jnp.float32), w_in, w_mid, w_out, energy, loss_norm
    )
    result_blocks = outputs.reshape(-1, lat_rows, block_width)
    tendency = result_blocks[:half_width]
    backward = jnp.einsum(
        "sjq,fsc->jqfc", recv_table, tendency, preferred_element_type=jnp.float32
    ).astype(jnp.bfloat16)
    returned = lax.all_to_all(backward, "lon", split_axis=0, concat_axis=0, tiled=True)
    home_tend = jnp.einsum(
        "dqk,dqfc->fkc", send_table, returned, preferred_element_type=jnp.float32
    ).astype(jnp.bfloat16)
    at_home = from_behind(home_tend, "grp", -1)
    own_cost = lax.dynamic_index_in_dim(band_cost, lon_index, 0, keepdims=False)
    home_live = (column_ids < own_cost[:, None]).astype(jnp.float32)
    new_state = state_field + step_weight * home_live[None] * at_home.astype(jnp.float32)
    kept_rows = result_blocks[result_blocks.shape[0] - half_width :].astype(jnp.float32)
    new_memory = jnp.where(slot_live[None] > 0, kept_rows, stored)
    new_columns = jnp.where(is_physics, new_memory, new_state)[None]
    summed = lax.psum(gradient, ("lat", "lon", "grp"))
    half_size = summed.shape[0] // grp_count
    grad_half = lax.dynamic_slice_in_dim(summed, grp_index * half_size, half_size)
    return (new_columns, grad_half)


def solution(mesh):
    in_specs = (
        P("grp", None, "lat", "lon"),
        P("lat", "lon"),
        P("lat", "lon"),
        P(),
        P(),
        P(),
        P(),
        P(),
        P(),
    )
    out_specs = (P("grp", None, "lat", "lon"), P("grp"))
    return jax.shard_map(
        on_device, mesh=mesh, in_specs=in_specs, out_specs=out_specs, check_vma=False
    )
```

profile of v0, /device:TPU:1, one launch (start us, length us, event | category | flops | bytes accessed | tf_op | source)
XLA Modules:
  0.0 436.3 jit_solution(15564182540137779222)
XLA Ops:
  7.2 2.1 bitcast_multiply_fusion.7
  9.4 4.4 %collective-permute-start.1 = (f32[278,1,128]{2,1,0:T(1,128)S(1)}, f32[278,1,128]{2,1,0:T(1,128)S(1)}, u32[]{:S(2)}, u32[]{:S(2)}) collective-permute-start(f32[278,1,128]{2,1,0:T(1,128)S(1)} %slice.47), channel_id=1, source_target_pairs={{0,32},{32,64},{64,96},{96,128},{128,160},{160,192},{192,224},{1,3... | collective-permute-start | bytes 427016 | tf_op jit(solution)/shard_map/ppermute | solution.py:20
  13.8 2.1 slice.45
  15.9 2.8 copy.24
  18.7 2.1 collective-permute-start
  21.8 2.7 copy.25
  24.5 4.4 %multiply_select_fusion = (f32[278,16,128]{2,1,0:T(8,128)S(1)}, f32[278,16,128]{2,1,0:T(8,128)S(1)}) fusion(f32[16,128]{1,0:T(8,128)S(1)} %copy-done.14, pred[16]{0:T(512)(128)(4,1)S(1)} %compare_and_fusion, f32[278,15,128]{2,1,0:T(8,128)} %bitcast.148, f32[278,1,128]{2,1,0:T(1,128)S(1)} %collective-permute-done.1, f32[278,16,127]{2,1,0:T(8,128)} %bitcast.146, ...), kind=kLoop, calls=%fused_computation.41 | loop fusion | flops 6262784 | bytes 11403280 | tf_op jit(solution)/shard_map/jit(_where)/select_n | solution.py:27
  29.1 3.5 collective-permute-start.3
  34.2 2.1 slice.49
  36.2 2.7 copy.26
  38.9 2.6 collective-permute-start.2
  43.3 2.7 copy.27
  46.0 6.8 %fusion.56 = (bf16[278,16,128]{2,1,0:T(8,128)(2,1)}, f32[278,16,128]{2,1,0:T(8,128)}) fusion(f32[278,15,128]{2,1,0:T(8,128)} %bitcast.147, f32[278,1,128]{2,1,0:T(1,128)S(1)} %collective-permute-done.3, f32[278,16,128]{2,1,0:T(8,128)} %copy-done.3, f32[16,128]{1,0:T(8,128)S(1)} %copy-done.14, pred[16]{0:T(512)(128)(4,1)S(1)} %compare_and_fusion, ...), kind=kLoop, calls=%fused_computation.105 | loop fusion | flops 5693440 | bytes 10264592 | tf_op jit(solution)/shard_map/convert_element_type | solution.py:101
  52.8 5.7 %collective-permute-start.4 = (bf16[278,16,128]{2,1,0:T(8,128)(2,1)}, bf16[278,16,128]{2,1,0:T(8,128)(2,1)}, u32[]{:S(2)}, u32[]{:S(2)}) collective-permute-start(bf16[278,16,128]{2,1,0:T(8,128)(2,1)} %get-tuple-element.4), channel_id=1, source_target_pairs={{0,1},{2,3},{4,5},{6,7},{8,9},{10,11},{12,13},{14,15},{16,17},{18,... | collective-permute-start | bytes 3416072 | tf_op jit(solution)/shard_map/ppermute | solution.py:20
  59.7 17.7 %collective-permute-done.4 = bf16[278,16,128]{2,1,0:T(8,128)(2,1)} collective-permute-done((bf16[278,16,128]{2,1,0:T(8,128)(2,1)}, bf16[278,16,128]{2,1,0:T(8,128)(2,1)}, u32[]{:S(2)}, u32[]{:S(2)}) %collective-permute-start.4) | collective-permute-done | bytes 1138720 | tf_op jit(solution)/shard_map/ppermute | solution.py:20
  80.4 10.3 %all-to-all-start = ((bf16[16,1,278,128]{3,2,1,0:T(8,128)(2,1)}), bf16[16,1,278,128]{3,2,1,0:T(8,128)(2,1)}, u32[]{:S(2)}, u32[]{:S(2)}) async-start(bf16[16,1,278,128]{3,2,1,0:T(8,128)(2,1)} %copy.28), calls=%async_computation | async-start | bytes 2293760 | tf_op jit(solution)/shard_map/all_to_all | solution.py:105
  93.5 14.3 %all-to-all-done = bf16[16,1,278,128]{3,2,1,0:T(8,128)(2,1)} async-done(((bf16[16,1,278,128]{3,2,1,0:T(8,128)(2,1)}), bf16[16,1,278,128]{3,2,1,0:T(8,128)(2,1)}, u32[]{:S(2)}, u32[]{:S(2)}) %all-to-all-start) | async-done | bytes 1138720 | tf_op jit(solution)/shard_map/all_to_all | solution.py:105
  110.8 3.6 fusion.11
  114.4 3.0 fusion.5
  122.5 5.0 %all-to-all-start.1 = ((bf16[16,1,278,128]{3,2,1,0:T(8,128)(2,1)}), bf16[16,1,278,128]{3,2,1,0:T(8,128)(2,1)}, u32[]{:S(2)}, u32[]{:S(2)}) async-start(bf16[16,1,278,128]{3,2,1,0:T(8,128)(2,1)} %copy.31), calls=%async_computation.1 | async-start | bytes 2293760 | tf_op jit(solution)/shard_map/all_to_all | solution.py:125
  127.8 4.9 %fusion.1 = bf16[384,2048]{0,1:T(8,128)(2,1)} fusion(f32[2048,384]{1,0:T(8,128)} %get-tuple-element.15, bf16[384,368]{0,1:T(8,128)(2,1)S(1)} %copy-done.16, f32[2048]{0:T(1024)S(1)} %fusion.38, f32[368]{0:T(512)S(1)} %copy-done.17), kind=kOutput, calls=%fused_computation.3 | convolution fusion | flops 587399168 | bytes 5010880 | tf_op jit(solution)/shard_map/dot_general | solution.py:54
  132.8 6.6 %fusion.31 = f32[556,384]{1,0:T(8,128)} fusion(bf16[556,2048]{1,0:T(8,128)(2,1)} %bitcast.155, f32[2048,384]{1,0:T(8,128)} %get-tuple-element.13, bf16[384,2048]{0,1:T(8,128)(2,1)} %fusion.1, bf16[384,384]{1,0:T(8,128)(2,1)S(1)} %copy-done.15), kind=kOutput, calls=%fused_computation.56 | convolution fusion | flops 1485570048 | bytes 8144896 | tf_op jit(solution)/shard_map/dot_general | solution.py:60
  139.3 2.1 reshape.271
  141.5 2.9 fusion.60
  145.2 3.3 fusion.22
  148.6 2.5 reshape.273
  151.1 2.8 fusion.30
  155.2 2.6 pad_maximum_fusion.1
  158.7 3.5 copy.38
  162.2 260.1 %all-reduce.2.cloned.1.call-done = f32[502272]{0:T(1024)} async-done(((f32[502272]{0:T(1024)}), f32[502272]{0:T(1024)}) %all-reduce.2.cloned.1.call-update) | async-done | bytes 2009104 | tf_op jit(solution)/shard_map/psum | solution.py:136
  422.3 2.5 dynamic_slice.25
  424.7 4.7 %fusion.16 = f32[1,278,16,128]{3,2,1,0:T(8,128)} fusion(f32[280,16,128]{2,1,0:T(8,128)} %bitcast.151, f32[1,278,16,128]{3,2,1,0:T(8,128)S(1)} %copy-done.2, f32[278,16,128]{2,1,0:T(8,128)} %get-tuple-element.5, bf16[278,16,128]{2,1,0:T(8,128)(2,1)} %collective-permute-done.5, f32[16,128]{1,0:T(8,128)S(1)} %fusion.43, ...), kind=kLoop, calls=%fused_computation.28 | loop fusion | flops 2846720 | bytes 10258433 | tf_op jit(solution)/shard_map/broadcast_in_dim | solution.py:135
  (78 shorter events, 22.8 us)
Async XLA Ops:
  7.2 103.7 %copy-start = (bf16[556,384]{1,0:T(8,128)(2,1)S(1)}, bf16[556,384]{1,0:T(8,128)(2,1)}, u32[]{:S(2)}) copy-start(bf16[556,384]{1,0:T(8,128)(2,1)} %param.14) | copy-start | bytes 1281028
  9.3 4.5 %copy-start.5 = (f32[278,16,128]{2,1,0:T(8,128)}, f32[278,16,128]{2,1,0:T(8,128)S(1)}, u32[]{:S(2)}) copy-start(f32[278,16,128]{2,1,0:T(8,128)S(1)} %get-tuple-element.8) | copy-start | bytes 6832132
  9.3 4.5 %copy-start.7 = (f32[278,16,128]{2,1,0:T(8,128)}, f32[278,16,128]{2,1,0:T(8,128)S(1)}, u32[]{:S(2)}) copy-start(f32[278,16,128]{2,1,0:T(8,128)S(1)} %get-tuple-element.9) | copy-start | bytes 6832132
  9.4 15.0 %collective-permute-start.1 = (f32[278,1,128]{2,1,0:T(1,128)S(1)}, f32[278,1,128]{2,1,0:T(1,128)S(1)}, u32[]{:S(2)}, u32[]{:S(2)}) collective-permute-start(f32[278,1,128]{2,1,0:T(1,128)S(1)} %slice.47), channel_id=1, source_target_pairs={{0,32},{32,64},{64,96},{96,128},{128,160},{160,192},{192,224},{1,3... | collective-permute-start | bytes 427016 | tf_op jit(solution)/shard_map/ppermute | solution.py:20
  15.9 8.6 %copy-start.2 = (f32[1,278,16,128]{3,2,1,0:T(8,128)S(1)}, f32[1,278,16,128]{3,2,1,0:T(8,128)}, u32[]{:S(2)}) copy-start(f32[1,278,16,128]{3,2,1,0:T(8,128)} %param.9) | copy-start | bytes 6832132
  15.9 8.6 %copy-start.13 = (f32[16,128]{1,0:T(8,128)S(1)}, f32[16,128]{1,0:T(8,128)}, u32[]{:S(2)}) copy-start(f32[16,128]{1,0:T(8,128)} %param.10) | copy-start | bytes 24580
  15.9 8.6 %copy-start.14 = (f32[16,128]{1,0:T(8,128)S(1)}, f32[16,128]{1,0:T(8,128)}, u32[]{:S(2)}) copy-start(f32[16,128]{1,0:T(8,128)} %param.11) | copy-start | bytes 24580
  18.7 3.1 collective-permute-start
  28.9 3.9 copy-start.3
  28.9 3.9 copy-start.6
  29.1 16.9 %collective-permute-start.3 = (f32[278,1,128]{2,1,0:T(1,128)S(1)}, f32[278,1,128]{2,1,0:T(1,128)S(1)}, u32[]{:S(2)}, u32[]{:S(2)}) collective-permute-start(f32[278,1,128]{2,1,0:T(1,128)S(1)} %slice.51), channel_id=1, source_target_pairs={{0,32},{32,64},{64,96},{96,128},{128,160},{160,192},{192,224},{1,3... | collective-permute-start | bytes 427016 | tf_op jit(solution)/shard_map/ppermute | solution.py:20
  32.8 1.4 copy-start.4
  38.9 4.3 collective-permute-start.2
  52.8 24.7 %collective-permute-start.4 = (bf16[278,16,128]{2,1,0:T(8,128)(2,1)}, bf16[278,16,128]{2,1,0:T(8,128)(2,1)}, u32[]{:S(2)}, u32[]{:S(2)}) collective-permute-start(bf16[278,16,128]{2,1,0:T(8,128)(2,1)} %get-tuple-element.4), channel_id=1, source_target_pairs={{0,1},{2,3},{4,5},{6,7},{8,9},{10,11},{12,13},{14,15},{16,17},{18,... | collective-permute-start | bytes 3416072 | tf_op jit(solution)/shard_map/ppermute | solution.py:20
  80.4 27.3 %all-to-all-start = ((bf16[16,1,278,128]{3,2,1,0:T(8,128)(2,1)}), bf16[16,1,278,128]{3,2,1,0:T(8,128)(2,1)}, u32[]{:S(2)}, u32[]{:S(2)}) async-start(bf16[16,1,278,128]{3,2,1,0:T(8,128)(2,1)} %copy.28), calls=%async_computation | async-start | bytes 2293760 | tf_op jit(solution)/shard_map/all_to_all | solution.py:105
  107.8 1.8 copy-start.8
  110.8 3.6 copy-start.10
  110.8 3.6 copy-start.15
  114.4 3.0 copy-start.12
  114.4 3.0 copy-start.16
  114.4 3.0 copy-start.17
  117.4 1.1 copy-start.18
  122.5 28.6 %all-to-all-start.1 = ((bf16[16,1,278,128]{3,2,1,0:T(8,128)(2,1)}), bf16[16,1,278,128]{3,2,1,0:T(8,128)(2,1)}, u32[]{:S(2)}, u32[]{:S(2)}) async-start(bf16[16,1,278,128]{3,2,1,0:T(8,128)(2,1)} %copy.31), calls=%async_computation.1 | async-start | bytes 2293760 | tf_op jit(solution)/shard_map/all_to_all | solution.py:125
  127.5 294.7 %all-reduce.2.cloned.1.call-start = ((), (), s32[]{:S(2)}) async-start(), calls=%async_computation.2 | async-start | bytes 4022272 | tf_op jit(solution)/shard_map/psum | solution.py:136
  148.5 6.6 %copy-start.9 = (f32[147456]{0:T(1024)S(1)}, f32[147456]{0:T(1024)}, u32[]{:S(2)}) copy-start(f32[147456]{0:T(1024)} %reshape.272) | copy-start | bytes 1769476
  151.1 4.1 copy-start.11
  153.9 270.8 %collective-permute-start.5 = (bf16[278,16,128]{2,1,0:T(8,128)(2,1)}, bf16[278,16,128]{2,1,0:T(8,128)(2,1)}, u32[]{:S(2)}, u32[]{:S(2)}) collective-permute-start(bf16[278,16,128]{2,1,0:T(8,128)(2,1)} %fusion.30), channel_id=1, source_target_pairs={{1,0},{3,2},{5,4},{7,6},{9,8},{11,10},{13,12},{15,14},{17,16},{19,... | collective-permute-start | bytes 3416072 | tf_op jit(solution)/shard_map/ppermute | solution.py:20
  424.7 4.7 %copy-start.1 = (bf16[556,384]{1,0:T(8,128)(2,1)S(1)}, bf16[556,384]{1,0:T(8,128)(2,1)}, u32[]{:S(2)}) copy-start(bf16[556,384]{1,0:T(8,128)(2,1)} %param.14) | copy-start | bytes 1281028
Sparse Core Ops, SparseCore 0:
  157.9 264.2 all-reduce.1
where the time goes:
time: 438 us; the launch traced here: 436 us
  waiting for transfers between devices  295 us (67%)
  starting transfers between devices  35.2 us (8%)
  local copies, waits for them, and re-layouts  33.7 us (8%)
  matrix products  32 us (7%)
  other arithmetic  26.2 us (6%)
  between operations  14.4 us (3%)
    psum x1, waiting for transfers between devices, on_device(): summed = lax.psum(gradient, ('lat', 'lon', 'grp'))  260 us
    ppermute x4, waiting for transfers between devices, from_behind(): return lax.ppermute(block, axis, route)  17.7 us
    ppermute x4, starting transfers between devices, from_behind(): return lax.ppermute(block, axis, route)  15 us
    all_to_all x1, waiting for transfers between devices, on_device(): lax.all_to_all(outgoing, 'lon', split_axis=0, concat_axis=0, tiled=True)  14.3 us
    all_to_all x1, starting transfers between devices, on_device(): lax.all_to_all(outgoing, 'lon', split_axis=0, concat_axis=0, tiled=True)  10.3 us
    slice x4, local copies, waits for them, and re-layouts, upwind(): west_rim = passed_along(flux_x[:, :, -1:], 'lon', 1)  9.65 us
  transfers between devices with their start and end apart: 9, of which 5 were waited for; matrix products, arithmetic and copies ran while one was open for 12% of the time, Pallas kernels for 0%

commit v1 on v0

v1 whole, which is shorter than its diff:
```python
import functools
import math

import jax
import jax.numpy as jnp
from jax import lax
from jax.experimental import pallas as pl
from jax.experimental.pallas import tpu as pltpu
from jax.sharding import Mesh, PartitionSpec as P

f32 = jnp.float32
bf16 = jnp.bfloat16

FEAT = 278
FPAD = 288
PACK = 144
ROWS = 16
COLS = 128
HID = 384
OUT = 368
FLAT = FEAT * ROWS
MINE = ROWS * COLS // 2
LON = ("y", "x", "core")
VMEM_LIMIT = 50 * 1024 * 1024

NT = (((1,), (1,)), ((), ()))
TN = (((0,), (0,)), ((), ()))

A_ROWS = 680
B_ROWS = 288
OWNERS = 128
A_PIECE = 16
B_PIECE = 8
PIECE = A_PIECE + B_PIECE


def vmem_call(kernel, outs, scratch, n_smem, n_vmem, flops, size, name):
    return pl.pallas_call(
        kernel,
        out_shape=outs,
        in_specs=[pl.BlockSpec(memory_space=pltpu.SMEM)] * n_smem
        + [pl.BlockSpec(memory_space=pltpu.VMEM)] * n_vmem,
        out_specs=jax.tree.map(lambda _: pl.BlockSpec(memory_space=pltpu.VMEM), outs),
        scratch_shapes=scratch,
        compiler_params=pltpu.CompilerParams(vmem_limit_bytes=VMEM_LIMIT),
        cost_estimate=pl.CostEstimate(flops=flops, bytes_accessed=size, transcendentals=0),
        name=name,
    )


def lane_ids(shape):
    return lax.broadcasted_iota(jnp.int32, shape, len(shape) - 1)


def row_ids(shape):
    return lax.broadcasted_iota(jnp.int32, shape, len(shape) - 2)


def chunks():
    full = FEAT // 8
    return full, FEAT - full * 8


def coefficients(east, north, flags_ref):
    dyn = flags_ref[0]
    not_top = flags_ref[1]
    rows = row_ids(north.shape)
    north = jnp.where(rows == ROWS - 1, north * not_top, north) * dyn
    east = east * dyn
    keep = 1.0 - east - north
    west = jnp.where(lane_ids(east.shape) == 0, 0.0, pltpu.roll(east, 1, 1))
    south = jnp.where(rows == 0, 0.0, pltpu.roll(north, 1, 0))
    return east, north, keep, west, south


def step(q, keep, west, south):
    shaped = q.reshape(-1, ROWS, COLS)
    out = (
        keep[None] * shaped
        + west[None] * pltpu.roll(shaped, 1, 2)
        + south[None] * pltpu.roll(shaped, 1, 1)
    )
    return out


def rim_kernel(flags_ref, x_ref, east_ref, north_ref, rim_ref, north_out_ref):
    east, north, keep, west, south = coefficients(east_ref[...], north_ref[...], flags_ref)
    pick_rows = row_ids((16, COLS))
    last = lane_ids((16, COLS)) == COLS - 1

    def pick(k):
        return jnp.where(jnp.logical_and(pick_rows == k, last), 1.0, 0.0).astype(bf16)

    def piece(start, count):
        q = x_ref[pl.ds(start * ROWS, count * ROWS), :]
        shaped = q.reshape(count, ROWS, COLS)
        after = step(q, keep, west, south)
        flux_one = (east[None] * shaped).reshape(count * ROWS, COLS).astype(bf16)
        flux_two = (east[None] * after).reshape(count * ROWS, COLS).astype(bf16)
        flux_up = (north[None] * shaped).reshape(count * ROWS, COLS).astype(bf16)
        out = lax.dot_general(pick(0), flux_one, NT, preferred_element_type=f32)
        out += lax.dot_general(pick(1), flux_two, NT, preferred_element_type=f32)
        out += lax.dot_general(pick(2), flux_up, NT, preferred_element_type=f32)
        corner = jnp.broadcast_to(east[0:1, COLS - 1 : COLS], out.shape)
        return jnp.where(row_ids(out.shape) == 3, corner, out).astype(bf16)

    full, rest = chunks()

    def body(i, carry):
        rim_ref[:, pl.ds(pl.multiple_of(i * 128, 128), 128)] = piece(i * 8, 8)
        return carry

    lax.fori_loop(0, full, body, 0, unroll=2)
    rim_ref[:, full * 128 : full * 128 + rest * ROWS] = piece(full * 8, rest)
    rim_ref[:, full * 128 + rest * ROWS :] = jnp.zeros(
        (16, rim_ref.shape[1] - full * 128 - rest * ROWS), bf16
    )
    q_top = x_ref[pl.ds(ROWS - 1, FEAT, stride=ROWS), :]
    q_under = x_ref[pl.ds(ROWS - 2, FEAT, stride=ROWS), :]
    top = slice(ROWS - 1, ROWS)
    after_top = (
        keep[top] * q_top + west[top] * pltpu.roll(q_top, 1, 1) + south[top] * q_under
    )
    north_out_ref[0:FEAT, :] = (north[top] * q_top).astype(bf16)
    north_out_ref[FPAD : FPAD + FEAT, :] = (north[top] * after_top).astype(bf16)
    pad = jnp.broadcast_to(north[top], (FPAD - FEAT, COLS)).astype(bf16)
    north_out_ref[FEAT:FPAD, :] = pad
    north_out_ref[FPAD + FEAT :, :] = pad


def transport_kernel(
    table_ref, flags_ref, x_ref, east_ref, north_ref, rim_ref, south_ref, corner_ref,
    field_ref, own_ref, send_ref, mid_ref, row_ref,
):
    east, north, keep, west, south = coefficients(east_ref[...], north_ref[...], flags_ref)
    full, rest = chunks()
    row16 = row_ids((16, COLS))
    lane16 = lane_ids((16, COLS))

    def put(k):
        return jnp.where(jnp.logical_and(row16 == k, lane16 == 0), 1.0, 0.0).astype(bf16)

    def column(values, k):
        return lax.dot_general(values, put(k), TN, preferred_element_type=f32)

    def first(start, count, lanes):
        q = x_ref[pl.ds(start * ROWS, count * ROWS), :]
        rim = rim_ref[:, lanes]
        inflow = column(rim, 0)[: count * ROWS]
        after = step(q, keep, west, south).reshape(count * ROWS, COLS) + inflow
        mid_ref[pl.ds(start * ROWS, count * ROWS), :] = after

    def first_body(i, carry):
        first(i * 8, 8, pl.ds(pl.multiple_of(i * 128, 128), 128))
        return carry

    lax.fori_loop(0, full, first_body, 0, unroll=2)
    first(full * 8, rest, slice(full * 128, full * 128 + 128))
    row0 = pl.ds(0, FEAT, stride=ROWS)
    mid_ref[row0, :] = mid_ref[row0, :] + south_ref[0:FEAT, :].astype(f32)

    def second(start, count, lanes):
        q = mid_ref[pl.ds(start * ROWS, count * ROWS), :]
        rim = rim_ref[:, lanes].astype(f32)
        corner = corner_ref[:, lanes]
        moved = pltpu.roll(corner.astype(f32), 128 - (ROWS - 1), 1)
        moved = jnp.where(lane_ids((1, 128)) % ROWS == 0, moved[2:3, :] * rim[3:4, :], 0.0)
        inflow_row = (rim[1:2, :] + moved).astype(bf16)
        values = jnp.broadcast_to(inflow_row, (16, 128))
        inflow = column(values, 0)[: count * ROWS]
        after = step(q, keep, west, south).reshape(count * ROWS, COLS) + inflow
        field_ref[pl.ds(start * ROWS, count * ROWS), :] = after
        row_ref[pl.ds(start * ROWS, count * ROWS), :] = column(corner, 0)[: count * ROWS]

    def second_body(i, carry):
        second(i * 8, 8, pl.ds(pl.multiple_of(i * 128, 128), 128))
        return carry

    lax.fori_loop(0, full, second_body, 0, unroll=2)
    second(full * 8, rest, slice(full * 128, full * 128 + 128))
    south_courant = south_ref[FEAT : FEAT + 1, 0:1].astype(f32)
    extra = row_ref[pl.ds(ROWS - 1, FEAT, stride=ROWS), :] * south_courant
    field_ref[row0, :] = (
        field_ref[row0, :] + south_ref[FPAD : FPAD + FEAT, :].astype(f32) + extra
    )

    turn = table_ref[2, 0]
    to_slot = table_ref[2, 1]
    low = lane_ids((PACK, COLS)) < COLS // 2
    zeros = jnp.zeros((FPAD - FEAT, COLS), f32)

    def block(r):
        rows = pl.ds(table_ref[0, r], FEAT, stride=ROWS)
        value = jnp.concatenate([field_ref[rows, :], zeros], axis=0)
        return pltpu.roll(value, turn, 1)

    def half(value):
        return pltpu.roll(value, COLS // 2, 1)

    def pair_body(i, carry):
        kept = []
        for side in range(2):
            r = 2 * i + side
            value = block(r)
            other = half(value)
            packed = jnp.where(low, other[:PACK], value[PACK:])
            send_ref[2 * r + to_slot] = packed.astype(bf16)
            send_ref[2 * r + 1 - to_slot] = jnp.zeros((PACK, COLS), bf16)
            kept.append(value if side == 0 else other)
        low_full = lane_ids((FPAD, COLS)) < COLS // 2
        own_ref[:, pl.ds(pl.multiple_of(i * COLS, COLS), COLS)] = jnp.where(
            low_full, kept[0], kept[1]
        ).astype(bf16)
        return carry

    lax.fori_loop(0, ROWS // 2, pair_body, 0)


def swap_halves(value):
    return pltpu.roll(value, COLS // 2, 1)


def forward_kernel(
    table_ref, own_ref, recv_ref, w_one_ref, w_two_ref, w_three_ref, gain_ref,
    inputs_ref, hidden_ref, g_two_ref, slope_ref, own_out_ref, send_ref, vec_ref,
):
    from_slot = table_ref[2, 1]
    offset = table_ref[2, 2]
    low = lane_ids((PACK, COLS)) < COLS // 2
    gain = gain_ref[...]
    loss_norm = 1.0 / math.sqrt(ROWS * 8 * COLS * ROWS)
    energy_norm = 1.0 / math.sqrt(OUT)
    tile = 2 * COLS
    vec_ref[...] = jnp.zeros(vec_ref.shape, f32)

    def tile_body(t, carry):
        lanes = pl.ds(pl.multiple_of(t * tile, tile), tile)
        live_parts = []
        for g in range(2):
            i = 2 * t + g
            group = pl.ds(pl.multiple_of(i * COLS, COLS), COLS)
            first = recv_ref[4 * i + from_slot].astype(f32)
            second = recv_ref[4 * i + 2 + from_slot].astype(f32)
            inputs_ref[0:FPAD, group] = own_ref[:, group]
            inputs_ref[FPAD : FPAD + PACK, group] = jnp.where(
                low, first, swap_halves(second)
            ).astype(bf16)
            inputs_ref[FPAD + PACK :, group] = jnp.where(
                low, swap_halves(first), second
            ).astype(bf16)
            lane = lane_ids((1, COLS))
            column = lane % (COLS // 2) + offset
            cost = jnp.where(lane < COLS // 2, table_ref[1, 2 * i], table_ref[1, 2 * i + 1])
            live_parts.append(jnp.where(column < cost, 1.0, 0.0))
        live = jnp.concatenate(live_parts, axis=1)
        inputs = inputs_ref[:, lanes]
        pre_one = jnp.dot(w_one_ref[...], inputs, preferred_element_type=f32)
        sig = 1.0 / (1.0 + jnp.exp(-pre_one))
        hidden_one = (pre_one * sig).astype(bf16)
        slope_ref[:, lanes] = sig * (1.0 + pre_one * (1.0 - sig))
        hidden_ref[:, lanes] = hidden_one
        pre_two = jnp.dot(w_two_ref[...], hidden_one, preferred_element_type=f32)
        sig = 1.0 / (1.0 + jnp.exp(-pre_two))
        hidden_two = (pre_two * sig).astype(bf16)
        slope_two = sig * (1.0 + pre_two * (1.0 - sig))
        result = jnp.dot(w_three_ref[...], hidden_two, preferred_element_type=f32).astype(bf16)
        own_out_ref[:, lanes] = result[:FPAD]
        to_send = result[FPAD:].astype(f32)
        for g in range(2):
            i = 2 * t + g
            part = to_send[:, g * COLS : (g + 1) * COLS]
            other = swap_halves(part)
            zeros = jnp.zeros((PACK, COLS), bf16)
            send_ref[4 * i + from_slot] = jnp.where(low, part[:PACK], other[PACK:]).astype(bf16)
            send_ref[4 * i + 2 + from_slot] = jnp.where(
                low, other[:PACK], part[PACK:]
            ).astype(bf16)
            send_ref[4 * i + 1 - from_slot] = zeros
            send_ref[4 * i + 3 - from_slot] = zeros
        energy = jnp.sum(gain * hidden_two.astype(f32), axis=0, keepdims=True) * energy_norm
        weight = live * energy * loss_norm
        g_two_ref[:, lanes] = (gain * weight * slope_two).astype(bf16)
        high = weight.astype(bf16)
        left = weight - high.astype(f32)
        mid = left.astype(bf16)
        low_part = (left - mid.astype(f32)).astype(bf16)
        rows = row_ids((16, tile))
        stacked = jnp.where(
            rows == 0,
            high.astype(f32),
            jnp.where(rows == 1, mid.astype(f32), jnp.where(rows == 2, low_part.astype(f32), 0.0)),
        ).astype(bf16)
        vec_ref[...] += lax.dot_general(stacked, hidden_two, NT, preferred_element_type=f32)
        return carry

    lax.fori_loop(0, MINE // tile, tile_body, 0)


def backward_kernel(
    table_ref, inputs_ref, hidden_ref, g_two_ref, slope_ref, w_mid_ref, vec_ref,
    grad_ref, g_one_ref, d_in_ref,
):
    state_first = table_ref[2, 3]
    tile = 2 * COLS

    def tile_body(t, carry):
        lanes = pl.ds(pl.multiple_of(t * tile, tile), tile)
        back = jnp.dot(w_mid_ref[...], g_two_ref[:, lanes], preferred_element_type=f32)
        g_one_ref[:, lanes] = (back * slope_ref[:, lanes]).astype(bf16)
        return carry

    lax.fori_loop(0, MINE // tile, tile_body, 0)
    d_mid = lax.dot_general(hidden_ref[...], g_two_ref[...], NT, preferred_element_type=f32)
    g_one = g_one_ref[...]
    own_at = pl.multiple_of((1 - state_first) * FPAD, 8)
    recv_at = pl.multiple_of(state_first * FPAD, 8)
    d_in_ref[pl.ds(own_at, FPAD), :] = lax.dot_general(
        inputs_ref[:FPAD, :], g_one, NT, preferred_element_type=f32
    )
    d_in_ref[pl.ds(recv_at, FPAD), :] = lax.dot_general(
        inputs_ref[FPAD:, :], g_one, NT, preferred_element_type=f32
    )
    d_in = d_in_ref[...]

    def put_a(row, value):
        grad_ref[row // A_PIECE, row % A_PIECE : row % A_PIECE + 8, :] = value

    def put_b(row, value):
        grad_ref[row // B_PIECE, A_PIECE:PIECE, :] = value

    for l in range(3):
        lanes = slice(l * 128, (l + 1) * 128)
        for k in range(2 * FPAD // 8):
            put_a(l * A_ROWS + k * 8, d_in[k * 8 : k * 8 + 8, lanes])
        for k in range((A_ROWS - 2 * FPAD) // 8):
            put_a(l * A_ROWS + 2 * FPAD + k * 8, d_mid[k * 8 : k * 8 + 8, lanes])
        for k in range(B_ROWS // 8):
            put_b(l * B_ROWS + k * 8, d_mid[96 + k * 8 : 96 + k * 8 + 8, lanes])
    zeros = jnp.zeros((8, 128), f32)
    for row in range(3 * A_ROWS, OWNERS * A_PIECE, 8):
        put_a(row, zeros)
    vec = jnp.sum(vec_ref[...], axis=0, keepdims=True)
    for l in range(3):
        put_b(3 * B_ROWS + l * 8, jnp.broadcast_to(vec[:, l * 128 : (l + 1) * 128], (8, 128)))
    for row in range(3 * B_ROWS + 24, OWNERS * B_PIECE, 8):
        put_b(row, zeros)


def final_kernel(table_ref, scale_ref, field_ref, own_ref, recv_ref, out_ref):
    turn = table_ref[2, 0]
    from_slot = table_ref[2, 1]
    keep_scale = scale_ref[2]
    new_scale = scale_ref[3]
    low = lane_ids((PACK, COLS)) < COLS // 2
    low_full = lane_ids((FPAD, COLS)) < COLS // 2

    def pair_body(i, carry):
        pair = own_ref[:, pl.ds(pl.multiple_of(i * COLS, COLS), COLS)].astype(f32)
        for side in range(2):
            r = 2 * i + side
            chunk = recv_ref[2 * r + from_slot].astype(f32)
            theirs = jnp.concatenate([swap_halves(chunk), chunk], axis=0)
            mine = pair if side == 0 else swap_halves(pair)
            tend = pltpu.roll(jnp.where(low_full, mine, theirs), turn, 1)[:FEAT]
            rows = pl.ds(table_ref[0, r], FEAT, stride=ROWS)
            old = field_ref[rows, :]
            live = lane_ids((FEAT, COLS)) < table_ref[1, r]
            out_ref[rows, :] = jnp.where(live, keep_scale * old + new_scale * tend, old)
        return carry

    lax.fori_loop(0, ROWS // 2, pair_body, 0)


def shape(dims, dtype):
    return jax.ShapeDtypeStruct(dims, dtype)


def swap(value, axis):
    return lax.ppermute(value, axis, [(0, 1), (1, 0)])


def on_device(columns, east_courant, north_courant, assign, block_cost, w_in, w_mid, w_out, energy):
    band = lax.axis_index("lat")
    bands = lax.axis_size("lat")
    lon = lax.axis_index(LON)
    lons = lax.axis_size(LON)
    grp = lax.axis_index("grp")
    is_physics = grp == 1
    stored = columns.reshape(FLAT, COLS)

    dyn = (1 - grp).astype(f32)
    flags = jnp.stack(
        [dyn, (band != bands - 1).astype(f32), jnp.where(is_physics, 0.0, 1.0), jnp.where(is_physics, 1.0, 0.5)]
    )
    rim, north_out = vmem_call(
        rim_kernel,
        [shape((16, 35 * 128), bf16), shape((2 * FPAD, COLS), bf16)],
        [],
        1,
        3,
        10**8,
        3 * 10**6,
        "rim",
    )(flags, stored, east_courant, north_courant)
    from_west = lax.ppermute(rim, LON, [(i, (i + 1) % lons) for i in range(lons)])
    from_south = lax.ppermute(north_out, "lat", [(i, i + 1) for i in range(bands - 1)])
    from_corner = lax.ppermute(
        rim,
        ("lat",) + LON,
        [(b * lons + i, (b + 1) * lons + (i + 1) % lons) for b in range(bands - 1) for i in range(lons)],
    )

    targets = lax.dynamic_index_in_dim(assign, band, 0, keepdims=False)
    costs = lax.dynamic_index_in_dim(block_cost, band, 0, keepdims=False)
    owner = targets // ROWS
    ids = lax.broadcasted_iota(jnp.int32, (ROWS, ROWS), 0)
    ks = lax.broadcasted_iota(jnp.int32, (ROWS, ROWS), 1)
    here_owner = lax.dynamic_index_in_dim(owner, lon, 0, keepdims=True)
    here_cost = lax.dynamic_index_in_dim(costs, lon, 0, keepdims=True)
    match = jnp.where(is_physics, owner == lon, here_owner == ids)
    row_of = jnp.sum(jnp.where(match, jnp.where(is_physics, targets % ROWS, ks), 0), axis=1)
    cost_of = jnp.sum(jnp.where(match, jnp.where(is_physics, costs, here_cost), 0), axis=1)
    half = COLS // 2
    facts = jnp.stack([grp * half, 1 - grp, grp * half, 1 - grp]).astype(jnp.int32)
    table = jnp.stack([row_of, cost_of, jnp.pad(facts, (0, ROWS - 4))]).astype(jnp.int32)

    def halves(a, b, axis):
        first = jnp.where(is_physics, b, a)
        second = jnp.where(is_physics, a, b)
        pad = [(0, 0), (0, 0)]
        pad[axis] = (0, FPAD - FEAT)
        return jnp.concatenate([jnp.pad(first, pad), jnp.pad(second, pad)], axis=axis)

    w_in_t = w_in.T
    w_one = halves(w_in_t[:, :FEAT], w_in_t[:, FEAT:], 1)
    w_out_t = w_out.T
    w_three = halves(w_out_t[:FEAT], w_out_t[OUT - FEAT :], 0)
    gain = jnp.sum(w_out.astype(f32) * energy[None, :], axis=1, keepdims=True)

    field, own, send = vmem_call(
        transport_kernel,
        [shape((FLAT, COLS), f32), shape((FPAD, MINE), bf16), shape((2 * ROWS, PACK, COLS), bf16)],
        [pltpu.VMEM((FLAT, COLS), f32), pltpu.VMEM((FLAT, COLS), f32)],
        2,
        6,
        10**8,
        6 * 10**6,
        "transport",
    )(table, flags, stored, east_courant, north_courant, from_west, from_south, from_corner)
    recv = lax.all_to_all(send, LON + ("grp",), 0, 0, tiled=True)
    inputs, hidden, g_two, slope, own_out, send_back, vec = vmem_call(
        forward_kernel,
        [
            shape((2 * FPAD, MINE), bf16),
            shape((HID, MINE), bf16),
            shape((HID, MINE), bf16),
            shape((HID, MINE), f32),
            shape((FPAD, MINE), bf16),
            shape((2 * ROWS, PACK, COLS), bf16),
            shape((16, HID), f32),
        ],
        [],
        1,
        6,
        2 * MINE * HID * (4 * FPAD + HID),
        8 * 10**6,
        "forward",
    )(table, own, recv, w_one, w_mid.T, w_three, gain)
    back = lax.all_to_all(send_back, LON + ("grp",), 0, 0, tiled=True)
    grad = vmem_call(
        backward_kernel,
        [shape((OWNERS, PIECE, 128), f32)],
        [pltpu.VMEM((HID, MINE), bf16), pltpu.VMEM((2 * FPAD, HID), f32)],
        1,
        6,
        2 * MINE * HID * (2 * FPAD + 2 * HID),
        6 * 10**6,
        "backward",
    )(table, inputs, hidden, g_two, slope, w_mid, vec)[0]

    for axis in ("core", "x"):
        pieces = grad.shape[0] // 2
        at = lax.axis_index(axis)
        keep = lax.dynamic_slice_in_dim(grad, at * pieces, pieces)
        other = lax.dynamic_slice_in_dim(grad, (1 - at) * pieces, pieces)
        grad = keep + swap(other, axis)
    ring = ("lat", "y")
    members = bands * lax.axis_size("y")
    grad = jnp.sum(lax.all_to_all(grad, ring, 0, 0, tiled=True), axis=0)
    grad = grad + swap(grad, "grp")
    piece = jnp.where(
        is_physics, jnp.pad(grad[A_PIECE:], ((0, A_PIECE - B_PIECE), (0, 0))), grad[:A_PIECE]
    )
    piece = lax.all_to_all(
        jnp.broadcast_to(piece[None], (members,) + piece.shape), ring, 0, 0, tiled=True
    )
    for axis in ("x", "core"):
        other = swap(piece, axis)
        at_zero = lax.axis_index(axis) == 0
        piece = jnp.concatenate(
            [jnp.where(at_zero, piece, other), jnp.where(at_zero, other, piece)], axis=0
        )
    rows_a = piece.reshape(OWNERS * A_PIECE, 128)[: 3 * A_ROWS].reshape(3, A_ROWS, 128)
    rows_a = rows_a.transpose(1, 0, 2)
    mid_a = 98
    flat_a = jnp.concatenate(
        [rows_a[:FEAT], rows_a[FPAD : FPAD + FEAT], rows_a[2 * FPAD : 2 * FPAD + mid_a]]
    ).reshape(-1)
    all_b = piece[:, :B_PIECE].reshape(OWNERS * B_PIECE, 128)
    rows_b = all_b[: 3 * B_ROWS].reshape(3, B_ROWS, 128).transpose(1, 0, 2)[mid_a - 96 :]
    vec_sum = all_b[3 * B_ROWS : 3 * B_ROWS + 24 : 8].reshape(HID)
    flat_b = jnp.concatenate(
        [rows_b.reshape(-1), (vec_sum[:, None] * energy[None, :]).reshape(-1)]
    )
    grad_half = jnp.where(is_physics, flat_b, flat_a)

    new = vmem_call(
        final_kernel,
        [shape((FLAT, COLS), f32)],
        [],
        2,
        3,
        10**7,
        6 * 10**6,
        "final",
    )(table, flags, field, own_out, back)[0]
    return new.reshape(columns.shape), grad_half


def solution(mesh):
    lat, lon, grp = mesh.devices.shape
    split = Mesh(
        mesh.devices.reshape(lat, lon // 4, 2, 2, grp), ("lat", "y", "x", "core", "grp")
    )
    grid = P("lat", LON)
    columns = P("grp", None, "lat", LON)
    return jax.shard_map(
        on_device,
        mesh=split,
        in_specs=(columns, grid, grid, P(), P(), P(), P(), P(), P()),
        out_specs=(columns, P("grp")),
        check_vma=False,
    )
```

time: 438 us -> 177 us (0.40)
  waiting for transfers between devices: 295 us -> 44.5 us
  blocking collectives: 0 us -> 40.3 us
  Pallas kernels: 0 us -> 40 us
  matrix products: 32 us -> 0 us
  local copies, waits for them, and re-layouts: 33.7 us -> 12.7 us
  other arithmetic: 26.2 us -> 6.9 us
  between operations: 14.4 us -> 1.05 us
    psum x1 -> x0, waiting for transfers between devices: 260 us -> none  [on_device(): summed = lax.psum(gradient, ('lat', 'lon', 'grp'))]
    all_to_all x0 -> x2, blocking collectives: none -> 40.3 us  [the longest x1 24.6 us: on_device(): grad = jnp.sum(lax.all_to_all(grad, ring, 0, 0, tiled=True), axis=0)]
    pallas_call x0 -> x5, Pallas kernels: none -> 40 us  [the longest x1 15.1 us: on_device(): vmem_call(transport_kernel, [shape((FLAT, COLS), f32), shape((FPAD, MINE)...]
    dot_general x11 -> x0, matrix products: 32 us -> none  [the longest x1 6.55 us: network(): d_in = jnp.dot(inputs, g_one.T, preferred_element_type=jnp.float32)]
    all_to_all x2, waiting for transfers between devices: 14.3 us -> 29 us  [the longest x1 16.1 us: on_device(): recv = lax.all_to_all(send, LON + ('grp',), 0, 0, tiled=True)]
    slice x6 -> x7, local copies, waits for them, and re-layouts: 9.9 us -> 0.5 us  [the longest x2 0.34 us: on_device(): all_b[:3 * B_ROWS].reshape(3, B_ROWS, 128).transpose(1, 0, 2)[mid_a - 96:]]
    convert_element_type x2 -> x0, other arithmetic: 7.97 us -> none  [the longest x1 6.82 us: on_device(): arrived = from_behind(state_field.astype(jnp.bfloat16), 'grp', 1)]
    ppermute x6 -> x8, starting transfers between devices: 19.7 us -> 13.6 us  [the longest x5 4.14 us: swap(): return lax.ppermute(value, axis, [(0, 1), (1, 0)])]
  transfers between devices with their start and end apart: 9 -> 10, of which waited for: 5 -> 6; matrix products, arithmetic and copies ran while one was open for 12% -> 3% of each run, Pallas kernels for 0% -> 3%
where the time goes in v1:
time: 177 us; the launch traced here: 176 us
  waiting for transfers between devices  44.5 us (25%)
  blocking collectives  40.3 us (23%)
  Pallas kernels  40 us (23%)
  starting transfers between devices  31.1 us (18%)
  local copies, waits for them, and re-layouts  12.7 us (7%)
  other arithmetic  6.9 us (4%)
    all_to_all x1, blocking collectives, on_device(): grad = jnp.sum(lax.all_to_all(grad, ring, 0, 0, tiled=True), axis=0)  24.6 us
    all_to_all x1, waiting for transfers between devices, on_device(): recv = lax.all_to_all(send, LON + ('grp',), 0, 0, tiled=True)  16.1 us
    all_to_all x1, blocking collectives, on_device(): lax.all_to_all(jnp.broadcast_to(piece[None], (members,) + piece.shape), r...  15.7 us
    ppermute x5, waiting for transfers between devices, swap(): return lax.ppermute(value, axis, [(0, 1), (1, 0)])  15.4 us
    pallas_call x1, Pallas kernels, on_device(): vmem_call(transport_kernel, [shape((FLAT, COLS), f32), shape((FPAD, MINE)...  15.1 us
    all_to_all x1, waiting for transfers between devices, on_device(): back = lax.all_to_all(send_back, LON + ('grp',), 0, 0, tiled=True)  12.9 us
    pallas_call x1, Pallas kernels, on_device(): vmem_call(forward_kernel, [shape((2 * FPAD, MINE), bf16), shape((HID, MIN...  9.22 us
    all_to_all x1, starting transfers between devices, on_device(): back = lax.all_to_all(send_back, LON + ('grp',), 0, 0, tiled=True)  8.88 us
  transfers between devices with their start and end apart: 10, of which 6 were waited for; matrix products, arithmetic and copies ran while one was open for 3% of the time, Pallas kernels for 3%

profile of v1, /device:TPU:1, one launch (start us, length us, event | category | flops | bytes accessed | tf_op | source)
XLA Modules:
  0.0 176.5 jit_solution(12259701921619296903)
XLA Ops:
  0.8 1.6 copy-done
  3.8 6.0 %rim.1 = (bf16[16,4480]{1,0:T(8,128)(2,1)S(1)}, bf16[576,128]{1,0:T(8,128)(2,1)S(1)}) custom-call(f32[4]{0:T(128)S(1)} %pad_maximum_fusion.3.flags_ref.scale_ref, f32[4448,128]{1,0:T(8,128)S(1)} %bitcast.55, f32[16,128]{1,0:T(8,128)S(1)} %copy-done.7, f32[16,128]{1,0:T(8,128)S(1)} %copy-done.9), custom_call_target="tpu_custom_call" | custom-call | flops 100000000 | bytes 3000000 | tf_op jit(solution)/shard_map/rim/pallas_call | solution.py:395
  9.7 2.6 %collective-permute-start = (bf16[16,4480]{1,0:T(8,128)(2,1)S(1)}, bf16[16,4480]{1,0:T(8,128)(2,1)S(1)}, u32[]{:S(2)}, u32[]{:S(2)}) collective-permute-start(bf16[16,4480]{1,0:T(8,128)(2,1)S(1)} %get-tuple-element.14), channel_id=1, source_target_pairs={{0,2},{2,4},{4,6},{6,8},{8,10},{10,12},{12,14},{14,16},{16,18},{18... | collective-permute-start | bytes 430088 | tf_op jit(solution)/shard_map/ppermute | solution.py:405
  12.4 3.3 %collective-permute-start.2 = (bf16[16,4480]{1,0:T(8,128)(2,1)S(1)}, bf16[16,4480]{1,0:T(8,128)(2,1)S(1)}, u32[]{:S(2)}, u32[]{:S(2)}) collective-permute-start(bf16[16,4480]{1,0:T(8,128)(2,1)S(1)} %get-tuple-element.14), channel_id=1, source_target_pairs={{0,34},{2,36},{4,38},{6,40},{8,42},{10,44},{12,46},{14,48},{16,50}... | collective-permute-start | bytes 430088 | tf_op jit(solution)/shard_map/ppermute | solution.py:407
  15.7 3.5 %collective-permute-start.1 = (bf16[576,128]{1,0:T(8,128)(2,1)S(1)}, bf16[576,128]{1,0:T(8,128)(2,1)S(1)}, u32[]{:S(2)}, u32[]{:S(2)}) collective-permute-start(bf16[576,128]{1,0:T(8,128)(2,1)S(1)} %get-tuple-element.15), channel_id=1, source_target_pairs={{0,32},{32,64},{64,96},{96,128},{128,160},{160,192},{192,224},{1,3... | collective-permute-start | bytes 442376 | tf_op jit(solution)/shard_map/ppermute | solution.py:406
  19.2 0.7 add_select_fusion.1
  20.8 0.8 fusion.11
  21.7 15.1 %transport.1 = (f32[4448,128]{1,0:T(8,128)}, bf16[288,1024]{1,0:T(8,128)(2,1)S(1)}, bf16[32,144,128]{2,1,0:T(8,128)(2,1)}) custom-call(s32[3,16]{1,0:T(4,128)S(1)} %pad_add_fusion.table_ref, f32[4]{0:T(128)S(1)} %pad_maximum_fusion.3.flags_ref.scale_ref, f32[4448,128]{1,0:T(8,128)} %bitcast.54, f32[16,128]{1,0:T(8,128)S(1)} %copy-done.8, ...), custom_call_target="tpu_custom_call" | custom-call | flops 100000000 | bytes 6000000 | tf_op jit(solution)/shard_map/transport/pallas_call | solution.py:440
  36.8 8.6 %all-to-all-start = ((bf16[32,144,128]{2,1,0:T(8,128)(2,1)}), bf16[32,144,128]{2,1,0:T(8,128)(2,1)}, u32[]{:S(2)}, u32[]{:S(2)}) async-start(bf16[32,144,128]{2,1,0:T(8,128)(2,1)} %get-tuple-element.18), calls=%async_computation | async-start | bytes 2359296 | tf_op jit(solution)/shard_map/all_to_all | solution.py:450
  46.7 16.1 %all-to-all-done.recv_ref = bf16[32,144,128]{2,1,0:T(8,128)(2,1)} async-done(((bf16[32,144,128]{2,1,0:T(8,128)(2,1)}), bf16[32,144,128]{2,1,0:T(8,128)(2,1)}, u32[]{:S(2)}, u32[]{:S(2)}) %all-to-all-start) | async-done | bytes 1179680 | tf_op jit(solution)/shard_map/all_to_all | solution.py:450
  62.8 9.2 %forward.1 = (bf16[576,1024]{1,0:T(8,128)(2,1)}, bf16[384,1024]{1,0:T(8,128)(2,1)S(1)}, bf16[384,1024]{1,0:T(8,128)(2,1)}, f32[384,1024]{1,0:T(8,128)}, bf16[288...) custom-call(s32[3,16]{1,0:T(4,128)S(1)} %pad_add_fusion.table_ref, ...), custom_call_target="tpu_custom_call" | custom-call | flops 1207959552 | bytes 8000000 | tf_op jit(solution)/shard_map/forward/pallas_call | solution.py:451
  72.0 1.5 copy-done.3
  73.5 1.1 copy-done.4
  74.6 4.9 %backward.1 = f32[128,24,128]{2,1,0:T(8,128)} custom-call(s32[3,16]{1,0:T(4,128)S(1)} %pad_add_fusion.table_ref, bf16[576,1024]{1,0:T(8,128)(2,1)S(1)} %copy-done.3, bf16[384,1024]{1,0:T(8,128)(2,1)S(1)} %get-tuple-element.22.hidden_ref, bf16[384,1024]{1,0:T(8,128)(2,1)S(1)} %copy-done.4, f32[384,1024]{1,0:T(8,128)} %get-tuple-element.24.slope_ref, ...), custom_call_target="tpu_custom_call" | custom-call | flops 1056964608 | bytes 6000000 | tf_op jit(solution)/shard_map/backward/pallas_call | solution.py:470
  79.5 1.3 constant_dynamic-slice_fusion.1
  80.8 1.0 collective-permute-start.3
  81.8 1.9 %collective-permute-done.3 = f32[64,24,128]{2,1,0:T(8,128)S(1)} collective-permute-done((f32[64,24,128]{2,1,0:T(8,128)S(1)}, f32[64,24,128]{2,1,0:T(8,128)S(1)}, u32[]{:S(2)}, u32[]{:S(2)}) %collective-permute-start.3) | collective-permute-done | bytes 786464 | tf_op jit(solution)/shard_map/ppermute | solution.py:379
  84.2 10.1 %collective-permute-done.4 = f32[32,24,128]{2,1,0:T(8,128)S(1)} collective-permute-done((f32[32,24,128]{2,1,0:T(8,128)S(1)}, f32[32,24,128]{2,1,0:T(8,128)S(1)}, u32[]{:S(2)}, u32[]{:S(2)}) %collective-permute-start.4) | collective-permute-done | bytes 393248 | tf_op jit(solution)/shard_map/ppermute | solution.py:379
  94.3 24.6 %all_to_all.20 = f32[32,24,128]{2,1,0:T(8,128)S(1)} all-to-all(f32[32,24,128]{2,1,0:T(8,128)S(1)} %dynamic-slice_add_fusion.1), channel_id=1, replica_groups=mesh['lat'=8,'y'=4,'x'=2,'core'=2,'grp'=2] {'lat','y'}, dimensions={0} | all-to-all | bytes 786432 | tf_op jit(solution)/shard_map/all_to_all | solution.py:489
  118.9 0.7 collective-permute-start.5
  119.6 3.4 %collective-permute-done.5 = f32[24,128]{1,0:T(8,128)S(1)} collective-permute-done((f32[24,128]{1,0:T(8,128)S(1)}, f32[24,128]{1,0:T(8,128)S(1)}, u32[]{:S(2)}, u32[]{:S(2)}) %collective-permute-start.5) | collective-permute-done | bytes 12320 | tf_op jit(solution)/shard_map/ppermute | solution.py:379
  123.1 15.7 %all_to_all.21 = f32[32,16,128]{2,1,0:T(8,128)} all-to-all(f32[32,16,128]{2,1,0:T(8,128)S(1)} %broadcast_in_dim.27), channel_id=1, replica_groups=mesh['lat'=8,'y'=4,'x'=2,'core'=2,'grp'=2] {'lat','y'}, dimensions={0} | all-to-all | bytes 524288 | tf_op jit(solution)/shard_map/all_to_all | solution.py:494
  139.1 8.9 %all-to-all-start.1 = ((bf16[32,144,128]{2,1,0:T(8,128)(2,1)}), bf16[32,144,128]{2,1,0:T(8,128)(2,1)S(1)}, u32[]{:S(2)}, u32[]{:S(2)}) async-start(bf16[32,144,128]{2,1,0:T(8,128)(2,1)} %get-tuple-element.20), calls=%async_computation.1 | async-start | bytes 2359296 | tf_op jit(solution)/shard_map/all_to_all | solution.py:469
  148.0 1.1 broadcast_select_fusion.7
  149.1 0.7 copy-done.12
  149.8 0.8 pad_maximum_fusion.2
  150.6 1.7 collective-permute-start.7
  152.3 12.9 %all-to-all-done.1.recv_ref = bf16[32,144,128]{2,1,0:T(8,128)(2,1)S(1)} async-done(((bf16[32,144,128]{2,1,0:T(8,128)(2,1)}), bf16[32,144,128]{2,1,0:T(8,128)(2,1)S(1)}, u32[]{:S(2)}, u32[]{:S(2)}) %all-to-all-start.1) | async-done | bytes 1179680 | tf_op jit(solution)/shard_map/all_to_all | solution.py:469
  165.3 1.1 copy-done.6
  166.3 4.9 %final.1 = f32[4448,128]{1,0:T(8,128)} custom-call(s32[3,16]{1,0:T(4,128)S(1)} %pad_add_fusion.table_ref, f32[4]{0:T(128)S(1)} %pad_maximum_fusion.3.flags_ref.scale_ref, f32[4448,128]{1,0:T(8,128)S(1)} %copy-done.1, bf16[288,1024]{1,0:T(8,128)(2,1)S(1)} %copy-done.6, bf16[32,144,128]{2,1,0:T(8,128)(2,1)S(1)} %all-to-all-done.1.recv_ref), custom_call_target="tpu_custom_call" | custom-call | flops 10000000 | bytes 6000000 | tf_op jit(solution)/shard_map/final/pallas_call | solution.py:517
  171.3 1.1 broadcast_select_fusion.3
  175.4 1.1 maximum_select_fusion
  (78 shorter events, 7.4 us)
Async XLA Ops:
  0.6 21.1 %copy-start.8 = (f32[16,128]{1,0:T(8,128)S(1)}, f32[16,128]{1,0:T(8,128)}, u32[]{:S(2)}) copy-start(f32[16,128]{1,0:T(8,128)} %east_ref.3) | copy-start | bytes 24580
  0.6 21.1 %copy-start.10 = (f32[16,128]{1,0:T(8,128)S(1)}, f32[16,128]{1,0:T(8,128)}, u32[]{:S(2)}) copy-start(f32[16,128]{1,0:T(8,128)} %north_ref.3) | copy-start | bytes 24580
  0.7 1.6 copy-start
  2.4 0.7 copy-start.7
  3.1 0.7 copy-start.9
  9.7 11.9 %collective-permute-start = (bf16[16,4480]{1,0:T(8,128)(2,1)S(1)}, bf16[16,4480]{1,0:T(8,128)(2,1)S(1)}, u32[]{:S(2)}, u32[]{:S(2)}) collective-permute-start(bf16[16,4480]{1,0:T(8,128)(2,1)S(1)} %get-tuple-element.14), channel_id=1, source_target_pairs={{0,2},{2,4},{4,6},{6,8},{8,10},{10,12},{12,14},{14,16},{16,18},{18... | collective-permute-start | bytes 430088 | tf_op jit(solution)/shard_map/ppermute | solution.py:405
  12.4 9.2 %collective-permute-start.2 = (bf16[16,4480]{1,0:T(8,128)(2,1)S(1)}, bf16[16,4480]{1,0:T(8,128)(2,1)S(1)}, u32[]{:S(2)}, u32[]{:S(2)}) collective-permute-start(bf16[16,4480]{1,0:T(8,128)(2,1)S(1)} %get-tuple-element.14), channel_id=1, source_target_pairs={{0,34},{2,36},{4,38},{6,40},{8,42},{10,44},{12,46},{14,48},{16,50}... | collective-permute-start | bytes 430088 | tf_op jit(solution)/shard_map/ppermute | solution.py:407
  15.7 6.1 %collective-permute-start.1 = (bf16[576,128]{1,0:T(8,128)(2,1)S(1)}, bf16[576,128]{1,0:T(8,128)(2,1)S(1)}, u32[]{:S(2)}, u32[]{:S(2)}) collective-permute-start(bf16[576,128]{1,0:T(8,128)(2,1)S(1)} %get-tuple-element.15), channel_id=1, source_target_pairs={{0,32},{32,64},{64,96},{96,128},{128,160},{160,192},{192,224},{1,3... | collective-permute-start | bytes 442376 | tf_op jit(solution)/shard_map/ppermute | solution.py:406
  36.8 8.6 %copy-start.17 = (bf16[556,384]{1,0:T(8,128)(2,1)S(1)}, bf16[556,384]{1,0:T(8,128)(2,1)}, u32[]{:S(2)}) copy-start(bf16[556,384]{1,0:T(8,128)(2,1)} %param.14) | copy-start | bytes 1281028
  36.8 8.9 %copy-start.2 = (bf16[384,384]{1,0:T(8,128)(2,1)S(1)}, bf16[384,384]{1,0:T(8,128)(2,1)}, u32[]{:S(2)}) copy-start(bf16[384,384]{1,0:T(8,128)(2,1)} %w_mid_ref.1) | copy-start | bytes 884740
  36.8 9.1 %copy-start.16 = (bf16[384,368]{0,1:T(8,128)(2,1)S(1)}, bf16[384,368]{0,1:T(8,128)(2,1)}, u32[]{:S(2)}) copy-start(bf16[384,368]{0,1:T(8,128)(2,1)} %param.16) | copy-start | bytes 847876
  36.8 9.1 %copy-start.18 = (f32[368]{0:T(512)S(1)}, f32[368]{0:T(512)}, u32[]{:S(2)}) copy-start(f32[368]{0:T(512)} %param.17) | copy-start | bytes 4420
  36.8 25.9 %all-to-all-start = ((bf16[32,144,128]{2,1,0:T(8,128)(2,1)}), bf16[32,144,128]{2,1,0:T(8,128)(2,1)}, u32[]{:S(2)}, u32[]{:S(2)}) async-start(bf16[32,144,128]{2,1,0:T(8,128)(2,1)} %get-tuple-element.18), calls=%async_computation | async-start | bytes 2359296 | tf_op jit(solution)/shard_map/all_to_all | solution.py:450
  72.0 7.5 %copy-start.5 = (bf16[288,1024]{1,0:T(8,128)(2,1)}, bf16[288,1024]{1,0:T(8,128)(2,1)S(1)}, u32[]{:S(2)}) copy-start(bf16[288,1024]{1,0:T(8,128)(2,1)S(1)} %get-tuple-element.19.own_ref) | copy-start | bytes 1769476
  72.0 1.5 copy-start.3
  73.5 1.1 copy-start.4
  79.4 4.2 %copy-start.11 = (f32[128,24,128]{2,1,0:T(8,128)S(1)}, f32[128,24,128]{2,1,0:T(8,128)}, u32[]{:S(2)}) copy-start(f32[128,24,128]{2,1,0:T(8,128)} %backward.1) | copy-start | bytes 4718596
  80.8 2.9 %collective-permute-start.3 = (f32[64,24,128]{2,1,0:T(8,128)S(1)}, f32[64,24,128]{2,1,0:T(8,128)S(1)}, u32[]{:S(2)}, u32[]{:S(2)}) collective-permute-start(f32[64,24,128]{2,1,0:T(8,128)S(1)} %constant_dynamic-slice_fusion.1), channel_id=1, source_target_pairs={{0,2},{2,0},{1,3},{3,1},{4,6},{6,4},{5,7},{7,5},{8,10},{10,8},{9,1... | collective-permute-start | bytes 2359304 | tf_op jit(solution)/shard_map/ppermute | solution.py:379
  83.8 10.4 %collective-permute-start.4 = (f32[32,24,128]{2,1,0:T(8,128)S(1)}, f32[32,24,128]{2,1,0:T(8,128)S(1)}, u32[]{:S(2)}, u32[]{:S(2)}) collective-permute-start(f32[32,24,128]{2,1,0:T(8,128)S(1)} %constant_dynamic-slice_fusion), channel_id=1, source_target_pairs={{0,4},{4,0},{1,5},{5,1},{2,6},{6,2},{3,7},{7,3},{8,12},{12,8},{9,1... | collective-permute-start | bytes 1179656 | tf_op jit(solution)/shard_map/ppermute | solution.py:379
  118.9 4.1 %collective-permute-start.5 = (f32[24,128]{1,0:T(8,128)S(1)}, f32[24,128]{1,0:T(8,128)S(1)}, u32[]{:S(2)}, u32[]{:S(2)}) collective-permute-start(f32[24,128]{1,0:T(8,128)S(1)} %reduce_sum.39), channel_id=1, source_target_pairs={{0,1},{1,0},{2,3},{3,2},{4,5},{5,4},{6,7},{7,6},{8,9},{9,8},{10,11... | collective-permute-start | bytes 36872 | tf_op jit(solution)/shard_map/ppermute | solution.py:379
  138.8 9.2 %collective-permute-start.6 = (f32[32,16,128]{2,1,0:T(8,128)}, f32[32,16,128]{2,1,0:T(8,128)}, u32[]{:S(2)}, u32[]{:S(2)}) collective-permute-start(f32[32,16,128]{2,1,0:T(8,128)} %all_to_all.21), channel_id=1, source_target_pairs={{0,4},{4,0},{1,5},{5,1},{2,6},{6,2},{3,7},{7,3},{8,12},{12,8},{9,1... | collective-permute-start | bytes 786440 | tf_op jit(solution)/shard_map/ppermute | solution.py:379
  139.1 26.2 %copy-start.1 = (f32[4448,128]{1,0:T(8,128)S(1)}, f32[4448,128]{1,0:T(8,128)}, u32[]{:S(2)}) copy-start(f32[4448,128]{1,0:T(8,128)} %get-tuple-element.16.field_ref) | copy-start | bytes 6832132
  139.1 26.2 %all-to-all-start.1 = ((bf16[32,144,128]{2,1,0:T(8,128)(2,1)}), bf16[32,144,128]{2,1,0:T(8,128)(2,1)S(1)}, u32[]{:S(2)}, u32[]{:S(2)}) async-start(bf16[32,144,128]{2,1,0:T(8,128)(2,1)} %get-tuple-element.20), calls=%async_computation.1 | async-start | bytes 2359296 | tf_op jit(solution)/shard_map/all_to_all | solution.py:469
  149.1 0.7 copy-start.12
  149.1 1.5 copy-start.14
  150.6 20.6 %collective-permute-start.7 = (f32[64,16,128]{2,1,0:T(8,128)}, f32[64,16,128]{2,1,0:T(8,128)}, u32[]{:S(2)}, u32[]{:S(2)}) collective-permute-start(f32[64,16,128]{2,1,0:T(8,128)} %pad_maximum_fusion.2), channel_id=1, source_target_pairs={{0,2},{2,0},{1,3},{3,1},{4,6},{6,4},{5,7},{7,5},{8,10},{10,8},{9,1... | collective-permute-start | bytes 1572872 | tf_op jit(solution)/shard_map/ppermute | solution.py:379
  165.3 1.1 copy-start.6
  166.3 4.9 %copy-start.13 = (f32[32,16,128]{2,1,0:T(8,128)S(1)}, f32[32,16,128]{2,1,0:T(8,128)}, u32[]{:S(2)}) copy-start(f32[32,16,128]{2,1,0:T(8,128)} %copy-done.12) | copy-start | bytes 786436
  166.3 4.9 %copy-start.15 = (f32[32,16,128]{2,1,0:T(8,128)S(1)}, f32[32,16,128]{2,1,0:T(8,128)}, u32[]{:S(2)}) copy-start(f32[32,16,128]{2,1,0:T(8,128)} %copy-done.14) | copy-start | bytes 786436

commit v2 on v1

--- a/solution.py
+++ b/solution.py
@@ -21,7 +21,8 @@
 FLAT = FEAT * ROWS
 MINE = ROWS * COLS // 2
 LON = ("y", "x", "core")
-VMEM_LIMIT = 50 * 1024 * 1024
+LAT = ("za", "zb", "zc")
+VMEM_LIMIT = 24 * 1024 * 1024
 
 NT = (((1,), (1,)), ((), ()))
 TN = (((0,), (0,)), ((), ()))
@@ -83,38 +84,39 @@
     return out
 
 
-def rim_kernel(flags_ref, x_ref, east_ref, north_ref, rim_ref, north_out_ref):
+def tiled_column(value, lane):
+    column = jnp.broadcast_to(value[:, lane : lane + 1], (ROWS, COLS))
+    return jnp.concatenate([column] * 8, axis=0)
+
+
+def rim_kernel(flags_ref, x_ref, east_ref, north_ref, rim_ref, corner_ref, north_out_ref):
     east, north, keep, west, south = coefficients(east_ref[...], north_ref[...], flags_ref)
-    pick_rows = row_ids((16, COLS))
-    last = lane_ids((16, COLS)) == COLS - 1
-
-    def pick(k):
-        return jnp.where(jnp.logical_and(pick_rows == k, last), 1.0, 0.0).astype(bf16)
-
-    def piece(start, count):
-        q = x_ref[pl.ds(start * ROWS, count * ROWS), :]
-        shaped = q.reshape(count, ROWS, COLS)
-        after = step(q, keep, west, south)
-        flux_one = (east[None] * shaped).reshape(count * ROWS, COLS).astype(bf16)
-        flux_two = (east[None] * after).reshape(count * ROWS, COLS).astype(bf16)
-        flux_up = (north[None] * shaped).reshape(count * ROWS, COLS).astype(bf16)
-        out = lax.dot_general(pick(0), flux_one, NT, preferred_element_type=f32)
-        out += lax.dot_general(pick(1), flux_two, NT, preferred_element_type=f32)
-        out += lax.dot_general(pick(2), flux_up, NT, preferred_element_type=f32)
-        corner = jnp.broadcast_to(east[0:1, COLS - 1 : COLS], out.shape)
-        return jnp.where(row_ids(out.shape) == 3, corner, out).astype(bf16)
-
     full, rest = chunks()
-
-    def body(i, carry):
-        rim_ref[:, pl.ds(pl.multiple_of(i * 128, 128), 128)] = piece(i * 8, 8)
-        return carry
-
-    lax.fori_loop(0, full, body, 0, unroll=2)
-    rim_ref[:, full * 128 : full * 128 + rest * ROWS] = piece(full * 8, rest)
-    rim_ref[:, full * 128 + rest * ROWS :] = jnp.zeros(
-        (16, rim_ref.shape[1] - full * 128 - rest * ROWS), bf16
-    )
+    lane = lane_ids((128, COLS))
+    picked = jnp.zeros((128, COLS), f32)
+    for g in range(full):
+        turned = pltpu.roll(x_ref[g * 128 : (g + 1) * 128, :], 2 * g + 2, 1)
+        picked = jnp.where(lane // 2 == g, turned, picked)
+    tail = pltpu.roll(x_ref[full * 128 :, :], 2 * full + 2, 1)
+    tail = jnp.concatenate([tail, jnp.zeros((128 - rest * ROWS, COLS), f32)], axis=0)
+    picked = jnp.where(lane // 2 == full, tail, picked)
+
+    last = COLS - 1
+    east_last = tiled_column(east, last)
+    after = (
+        tiled_column(keep, last) * picked
+        + tiled_column(west, last) * pltpu.roll(picked, 1, 1)
+        + tiled_column(south, last) * pltpu.roll(picked, 1, 0)
+    )
+    odd = lane % 2 == 1
+    flux_one = east_last * picked
+    flux_two = pltpu.roll(east_last * after, COLS - 1, 1)
+    flux_up = pltpu.roll(tiled_column(north, last) * picked, COLS - 1, 1)
+    scalar = jnp.broadcast_to(east[0:1, last:], (128, COLS))
+    rim = jnp.where(odd, flux_one, flux_two)
+    rim_ref[...] = jnp.where(lane == last, scalar, rim).astype(bf16)
+    corner_ref[...] = jnp.where(odd, flux_one, flux_up).astype(bf16)
+
     q_top = x_ref[pl.ds(ROWS - 1, FEAT, stride=ROWS), :]
     q_under = x_ref[pl.ds(ROWS - 2, FEAT, stride=ROWS), :]
     top = slice(ROWS - 1, ROWS)
@@ -130,90 +132,75 @@
 
 def transport_kernel(
     table_ref, flags_ref, x_ref, east_ref, north_ref, rim_ref, south_ref, corner_ref,
-    field_ref, own_ref, send_ref, mid_ref, row_ref,
+    field_ref, own_ref, send_ref, mid_ref, inflow_ref,
 ):
     east, north, keep, west, south = coefficients(east_ref[...], north_ref[...], flags_ref)
     full, rest = chunks()
-    row16 = row_ids((16, COLS))
-    lane16 = lane_ids((16, COLS))
-
-    def put(k):
-        return jnp.where(jnp.logical_and(row16 == k, lane16 == 0), 1.0, 0.0).astype(bf16)
-
-    def column(values, k):
-        return lax.dot_general(values, put(k), TN, preferred_element_type=f32)
-
-    def first(start, count, lanes):
-        q = x_ref[pl.ds(start * ROWS, count * ROWS), :]
-        rim = rim_ref[:, lanes]
-        inflow = column(rim, 0)[: count * ROWS]
-        after = step(q, keep, west, south).reshape(count * ROWS, COLS) + inflow
-        mid_ref[pl.ds(start * ROWS, count * ROWS), :] = after
-
-    def first_body(i, carry):
-        first(i * 8, 8, pl.ds(pl.multiple_of(i * 128, 128), 128))
+    lane = lane_ids((128, COLS))
+    odd = lane % 2 == 1
+    rim = rim_ref[...].astype(f32)
+    corner = pltpu.roll(corner_ref[...].astype(f32), 128 - (ROWS - 1), 0)
+    east_courant = rim[0:1, COLS - 1 : COLS]
+    north_courant = south_ref[FEAT : FEAT + 1, 0:1].astype(f32)
+    lacked = corner * east_courant + pltpu.roll(corner, COLS - 1, 1) * north_courant
+    fix = jnp.logical_and(row_ids((128, COLS)) % ROWS == 0, jnp.logical_not(odd))
+    inflow_ref[...] = rim + jnp.where(fix, lacked, 0.0)
+
+    def stage(source, target, g, count, shift):
+        rows = pl.ds(pl.multiple_of(g * 128, 128), count * ROWS)
+        inflow = pltpu.roll(inflow_ref[0 : count * ROWS, :], shift, 1)
+        inflow = jnp.where(lane[: count * ROWS] == 0, inflow, 0.0)
+        after = step(source[rows, :], keep, west, south).reshape(count * ROWS, COLS)
+        target[rows, :] = after + inflow
+
+    row0 = pl.ds(0, FEAT, stride=ROWS)
+
+    def first_body(g, carry):
+        stage(x_ref, mid_ref, g, 8, COLS - 1 - 2 * g)
         return carry
 
-    lax.fori_loop(0, full, first_body, 0, unroll=2)
-    first(full * 8, rest, slice(full * 128, full * 128 + 128))
-    row0 = pl.ds(0, FEAT, stride=ROWS)
+    lax.fori_loop(0, full, first_body, 0, unroll=4)
+    stage(x_ref, mid_ref, full, rest, COLS - 1 - 2 * full)
     mid_ref[row0, :] = mid_ref[row0, :] + south_ref[0:FEAT, :].astype(f32)
 
-    def second(start, count, lanes):
-        q = mid_ref[pl.ds(start * ROWS, count * ROWS), :]
-        rim = rim_ref[:, lanes].astype(f32)
-        corner = corner_ref[:, lanes]
-        moved = pltpu.roll(corner.astype(f32), 128 - (ROWS - 1), 1)
-        moved = jnp.where(lane_ids((1, 128)) % ROWS == 0, moved[2:3, :] * rim[3:4, :], 0.0)
-        inflow_row = (rim[1:2, :] + moved).astype(bf16)
-        values = jnp.broadcast_to(inflow_row, (16, 128))
-        inflow = column(values, 0)[: count * ROWS]
-        after = step(q, keep, west, south).reshape(count * ROWS, COLS) + inflow
-        field_ref[pl.ds(start * ROWS, count * ROWS), :] = after
-        row_ref[pl.ds(start * ROWS, count * ROWS), :] = column(corner, 0)[: count * ROWS]
-
-    def second_body(i, carry):
-        second(i * 8, 8, pl.ds(pl.multiple_of(i * 128, 128), 128))
+    def second_body(g, carry):
+        stage(mid_ref, field_ref, g, 8, COLS - 2 * g)
         return carry
 
-    lax.fori_loop(0, full, second_body, 0, unroll=2)
-    second(full * 8, rest, slice(full * 128, full * 128 + 128))
-    south_courant = south_ref[FEAT : FEAT + 1, 0:1].astype(f32)
-    extra = row_ref[pl.ds(ROWS - 1, FEAT, stride=ROWS), :] * south_courant
-    field_ref[row0, :] = (
-        field_ref[row0, :] + south_ref[FPAD : FPAD + FEAT, :].astype(f32) + extra
-    )
-
-    turn = table_ref[2, 0]
+    lax.fori_loop(1, full, second_body, 0, unroll=4)
+    stage(mid_ref, field_ref, 0, 8, 0)
+    stage(mid_ref, field_ref, full, rest, COLS - 2 * full)
+    field_ref[row0, :] = field_ref[row0, :] + south_ref[FPAD : FPAD + FEAT, :].astype(f32)
+
     to_slot = table_ref[2, 1]
+    is_dyn = to_slot == 1
     low = lane_ids((PACK, COLS)) < COLS // 2
+    low_full = lane_ids((FPAD, COLS)) < COLS // 2
     zeros = jnp.zeros((FPAD - FEAT, COLS), f32)
-
-    def block(r):
-        rows = pl.ds(table_ref[0, r], FEAT, stride=ROWS)
-        value = jnp.concatenate([field_ref[rows, :], zeros], axis=0)
-        return pltpu.roll(value, turn, 1)
-
-    def half(value):
-        return pltpu.roll(value, COLS // 2, 1)
 
     def pair_body(i, carry):
         kept = []
         for side in range(2):
             r = 2 * i + side
-            value = block(r)
-            other = half(value)
+            rows = pl.ds(table_ref[0, r], FEAT, stride=ROWS)
+            here = jnp.concatenate([field_ref[rows, :], zeros], axis=0)
+            turned = pltpu.roll(here, COLS // 2, 1)
+            value = jnp.where(is_dyn, here, turned)
+            other = jnp.where(is_dyn, turned, here)
             packed = jnp.where(low, other[:PACK], value[PACK:])
             send_ref[2 * r + to_slot] = packed.astype(bf16)
             send_ref[2 * r + 1 - to_slot] = jnp.zeros((PACK, COLS), bf16)
             kept.append(value if side == 0 else other)
-        low_full = lane_ids((FPAD, COLS)) < COLS // 2
         own_ref[:, pl.ds(pl.multiple_of(i * COLS, COLS), COLS)] = jnp.where(
             low_full, kept[0], kept[1]
         ).astype(bf16)
         return carry
 
-    lax.fori_loop(0, ROWS // 2, pair_body, 0)
+    lax.fori_loop(0, ROWS // 2, pair_body, 0, unroll=2)
+
+
+def sigmoid(value):
+    return 0.5 + 0.5 * jnp.tanh(0.5 * value)
 
 
 def swap_halves(value):
@@ -255,14 +242,16 @@
         live = jnp.concatenate(live_parts, axis=1)
         inputs = inputs_ref[:, lanes]
         pre_one = jnp.dot(w_one_ref[...], inputs, preferred_element_type=f32)
-        sig = 1.0 / (1.0 + jnp.exp(-pre_one))
-        hidden_one = (pre_one * sig).astype(bf16)
-        slope_ref[:, lanes] = sig * (1.0 + pre_one * (1.0 - sig))
+        sig = sigmoid(pre_one)
+        silu = pre_one * sig
+        hidden_one = silu.astype(bf16)
+        slope_ref[:, lanes] = sig + silu * (1.0 - sig)
         hidden_ref[:, lanes] = hidden_one
         pre_two = jnp.dot(w_two_ref[...], hidden_one, preferred_element_type=f32)
-        sig = 1.0 / (1.0 + jnp.exp(-pre_two))
-        hidden_two = (pre_two * sig).astype(bf16)
-        slope_two = sig * (1.0 + pre_two * (1.0 - sig))
+        sig = sigmoid(pre_two)
+        silu = pre_two * sig
+        hidden_two = silu.astype(bf16)
+        slope_two = sig + silu * (1.0 - sig)
         result = jnp.dot(w_three_ref[...], hidden_two, preferred_element_type=f32).astype(bf16)
         own_out_ref[:, lanes] = result[:FPAD]
         to_send = result[FPAD:].astype(f32)
@@ -293,14 +282,22 @@
         vec_ref[...] += lax.dot_general(stacked, hidden_two, NT, preferred_element_type=f32)
         return carry
 
-    lax.fori_loop(0, MINE // tile, tile_body, 0)
+    lax.fori_loop(0, MINE // tile, tile_body, 0, unroll=True)
+
+
+def place(owner):
+    core, x, za, zb, zc, y = (
+        owner // 64, owner // 32 % 2, owner // 16 % 2, owner // 8 % 2, owner // 4 % 2, owner % 4
+    )
+    return core, zc * 32 + zb * 16 + za * 8 + y * 2 + x
 
 
 def backward_kernel(
     table_ref, inputs_ref, hidden_ref, g_two_ref, slope_ref, w_mid_ref, vec_ref,
-    grad_ref, g_one_ref, d_in_ref,
+    keep_ref, send_ref, g_one_ref, d_in_ref,
 ):
     state_first = table_ref[2, 3]
+    core = table_ref[2, 4]
     tile = 2 * COLS
 
     def tile_body(t, carry):
@@ -309,7 +306,7 @@
         g_one_ref[:, lanes] = (back * slope_ref[:, lanes]).astype(bf16)
         return carry
 
-    lax.fori_loop(0, MINE // tile, tile_body, 0)
+    lax.fori_loop(0, MINE // tile, tile_body, 0, unroll=True)
     d_mid = lax.dot_general(hidden_ref[...], g_two_ref[...], NT, preferred_element_type=f32)
     g_one = g_one_ref[...]
     own_at = pl.multiple_of((1 - state_first) * FPAD, 8)
@@ -320,35 +317,47 @@
     d_in_ref[pl.ds(recv_at, FPAD), :] = lax.dot_general(
         inputs_ref[FPAD:, :], g_one, NT, preferred_element_type=f32
     )
-    d_in = d_in_ref[...]
-
-    def put_a(row, value):
-        grad_ref[row // A_PIECE, row % A_PIECE : row % A_PIECE + 8, :] = value
-
-    def put_b(row, value):
-        grad_ref[row // B_PIECE, A_PIECE:PIECE, :] = value
-
-    for l in range(3):
-        lanes = slice(l * 128, (l + 1) * 128)
-        for k in range(2 * FPAD // 8):
-            put_a(l * A_ROWS + k * 8, d_in[k * 8 : k * 8 + 8, lanes])
-        for k in range((A_ROWS - 2 * FPAD) // 8):
-            put_a(l * A_ROWS + 2 * FPAD + k * 8, d_mid[k * 8 : k * 8 + 8, lanes])
-        for k in range(B_ROWS // 8):
-            put_b(l * B_ROWS + k * 8, d_mid[96 + k * 8 : 96 + k * 8 + 8, lanes])
-    zeros = jnp.zeros((8, 128), f32)
-    for row in range(3 * A_ROWS, OWNERS * A_PIECE, 8):
-        put_a(row, zeros)
-    vec = jnp.sum(vec_ref[...], axis=0, keepdims=True)
-    for l in range(3):
-        put_b(3 * B_ROWS + l * 8, jnp.broadcast_to(vec[:, l * 128 : (l + 1) * 128], (8, 128)))
-    for row in range(3 * B_ROWS + 24, OWNERS * B_PIECE, 8):
-        put_b(row, zeros)
+
+    def write(refs):
+        def put(owner, at, value):
+            half, index = place(owner)
+            refs[half][index, at : at + 8, :] = value
+
+        def put_a(row, value):
+            put(row // A_PIECE, row % A_PIECE, value)
+
+        def put_b(row, value):
+            put(row // B_PIECE, A_PIECE, value)
+
+        for l in range(3):
+            lanes = slice(l * 128, (l + 1) * 128)
+            for k in range(2 * FPAD // 8):
+                put_a(l * A_ROWS + k * 8, d_in_ref[k * 8 : k * 8 + 8, lanes])
+            for k in range((A_ROWS - 2 * FPAD) // 8):
+                put_a(l * A_ROWS + 2 * FPAD + k * 8, d_mid[k * 8 : k * 8 + 8, lanes])
+            for k in range(B_ROWS // 8):
+                put_b(l * B_ROWS + k * 8, d_mid[96 + k * 8 : 96 + k * 8 + 8, lanes])
+        zeros = jnp.zeros((8, 128), f32)
+        for row in range(3 * A_ROWS, OWNERS * A_PIECE, 8):
+            put_a(row, zeros)
+        vec = jnp.sum(vec_ref[...], axis=0, keepdims=True)
+        for l in range(3):
+            put_b(3 * B_ROWS + l * 8, jnp.broadcast_to(vec[:, l * 128 : (l + 1) * 128], (8, 128)))
+        for row in range(3 * B_ROWS + 24, OWNERS * B_PIECE, 8):
+            put_b(row, zeros)
+
+    @pl.when(core == 0)
+    def _():
+        write((keep_ref, send_ref))
+
+    @pl.when(core == 1)
+    def _():
+        write((send_ref, keep_ref))
 
 
 def final_kernel(table_ref, scale_ref, field_ref, own_ref, recv_ref, out_ref):
-    turn = table_ref[2, 0]
     from_slot = table_ref[2, 1]
+    is_dyn = from_slot == 1
     keep_scale = scale_ref[2]
     new_scale = scale_ref[3]
     low = lane_ids((PACK, COLS)) < COLS // 2
@@ -361,14 +370,15 @@
             chunk = recv_ref[2 * r + from_slot].astype(f32)
             theirs = jnp.concatenate([swap_halves(chunk), chunk], axis=0)
             mine = pair if side == 0 else swap_halves(pair)
-            tend = pltpu.roll(jnp.where(low_full, mine, theirs), turn, 1)[:FEAT]
+            tend = jnp.where(low_full, mine, theirs)[:FEAT]
+            tend = jnp.where(is_dyn, tend, swap_halves(tend))
             rows = pl.ds(table_ref[0, r], FEAT, stride=ROWS)
             old = field_ref[rows, :]
             live = lane_ids((FEAT, COLS)) < table_ref[1, r]
             out_ref[rows, :] = jnp.where(live, keep_scale * old + new_scale * tend, old)
         return carry
 
-    lax.fori_loop(0, ROWS // 2, pair_body, 0)
+    lax.fori_loop(0, ROWS // 2, pair_body, 0, unroll=2)
 
 
 def shape(dims, dtype):
@@ -380,8 +390,8 @@
 
 
 def on_device(columns, east_courant, north_courant, assign, block_cost, w_in, w_mid, w_out, energy):
-    band = lax.axis_index("lat")
-    bands = lax.axis_size("lat")
+    band = lax.axis_index(LAT)
+    bands = lax.axis_size(LAT)
     lon = lax.axis_index(LON)
     lons = lax.axis_size(LON)
     grp = lax.axis_index("grp")
@@ -392,9 +402,9 @@
     flags = jnp.stack(
         [dyn, (band != bands - 1).astype(f32), jnp.where(is_physics, 0.0, 1.0), jnp.where(is_physics, 1.0, 0.5)]
     )
-    rim, north_out = vmem_call(
+    rim, corner, north_out = vmem_call(
         rim_kernel,
-        [shape((16, 35 * 128), bf16), shape((2 * FPAD, COLS), bf16)],
+        [shape((128, COLS), bf16), shape((128, COLS), bf16), shape((2 * FPAD, COLS), bf16)],
         [],
         1,
         3,
@@ -403,10 +413,10 @@
         "rim",
     )(flags, stored, east_courant, north_courant)
     from_west = lax.ppermute(rim, LON, [(i, (i + 1) % lons) for i in range(lons)])
-    from_south = lax.ppermute(north_out, "lat", [(i, i + 1) for i in range(bands - 1)])
+    from_south = lax.ppermute(north_out, LAT, [(i, i + 1) for i in range(bands - 1)])
     from_corner = lax.ppermute(
-        rim,
-        ("lat",) + LON,
+        corner,
+        LAT + LON,
         [(b * lons + i, (b + 1) * lons + (i + 1) % lons) for b in range(bands - 1) for i in range(lons)],
     )
 
@@ -421,8 +431,8 @@
     row_of = jnp.sum(jnp.where(match, jnp.where(is_physics, targets % ROWS, ks), 0), axis=1)
     cost_of = jnp.sum(jnp.where(match, jnp.where(is_physics, costs, here_cost), 0), axis=1)
     half = COLS // 2
-    facts = jnp.stack([grp * half, 1 - grp, grp * half, 1 - grp]).astype(jnp.int32)
-    table = jnp.stack([row_of, cost_of, jnp.pad(facts, (0, ROWS - 4))]).astype(jnp.int32)
+    facts = jnp.stack([grp * half, 1 - grp, grp * half, 1 - grp, lax.axis_index("core")]).astype(jnp.int32)
+    table = jnp.stack([row_of, cost_of, jnp.pad(facts, (0, ROWS - 5))]).astype(jnp.int32)
 
     def halves(a, b, axis):
         first = jnp.where(is_physics, b, a)
@@ -440,7 +450,7 @@
     field, own, send = vmem_call(
         transport_kernel,
         [shape((FLAT, COLS), f32), shape((FPAD, MINE), bf16), shape((2 * ROWS, PACK, COLS), bf16)],
-        [pltpu.VMEM((FLAT, COLS), f32), pltpu.VMEM((FLAT, COLS), f32)],
+        [pltpu.VMEM((FLAT, COLS), f32), pltpu.VMEM((128, COLS), f32)],
         2,
         6,
         10**8,
@@ -467,35 +477,47 @@
         "forward",
     )(table, own, recv, w_one, w_mid.T, w_three, gain)
     back = lax.all_to_all(send_back, LON + ("grp",), 0, 0, tiled=True)
-    grad = vmem_call(
+    keep, other = vmem_call(
         backward_kernel,
-        [shape((OWNERS, PIECE, 128), f32)],
+        [shape((OWNERS // 2, PIECE, 128), f32)] * 2,
         [pltpu.VMEM((HID, MINE), bf16), pltpu.VMEM((2 * FPAD, HID), f32)],
         1,
         6,
         2 * MINE * HID * (2 * FPAD + 2 * HID),
         6 * 10**6,
         "backward",
-    )(table, inputs, hidden, g_two, slope, w_mid, vec)[0]
-
-    for axis in ("core", "x"):
+    )(table, inputs, hidden, g_two, slope, w_mid, vec)
+
+    grad = keep + swap(other, "core")
+    for axis in ("zc", "zb"):
         pieces = grad.shape[0] // 2
         at = lax.axis_index(axis)
+        other = lax.dynamic_slice_in_dim(grad, (1 - at) * pieces, pieces)
         keep = lax.dynamic_slice_in_dim(grad, at * pieces, pieces)
-        other = lax.dynamic_slice_in_dim(grad, (1 - at) * pieces, pieces)
         grad = keep + swap(other, axis)
-    ring = ("lat", "y")
+    grad, back = lax.optimization_barrier((grad, back))
+    pieces_b = jnp.pad(grad[:, A_PIECE:], ((0, 0), (0, A_PIECE - B_PIECE), (0, 0)))
+    pieces = jnp.stack([grad[:, :A_PIECE], pieces_b], axis=1).reshape(-1, A_PIECE, 128)
+    piece = jnp.sum(lax.all_to_all(pieces, ("za", "y", "x", "grp"), 0, 0, tiled=True), axis=0)
+    ring = LAT + ("y",)
     members = bands * lax.axis_size("y")
-    grad = jnp.sum(lax.all_to_all(grad, ring, 0, 0, tiled=True), axis=0)
-    grad = grad + swap(grad, "grp")
-    piece = jnp.where(
-        is_physics, jnp.pad(grad[A_PIECE:], ((0, A_PIECE - B_PIECE), (0, 0))), grad[:A_PIECE]
-    )
     piece = lax.all_to_all(
         jnp.broadcast_to(piece[None], (members,) + piece.shape), ring, 0, 0, tiled=True
     )
+    new = vmem_call(
+        final_kernel,
+        [shape((FLAT, COLS), f32)],
+        [],
+        2,
+        3,
+        10**7,
+        6 * 10**6,
+        "final",
+    )(table, flags, field, own_out, back)[0]
     for axis in ("x", "core"):
         other = swap(piece, axis)
+        if axis == "x":
+            other, new = lax.optimization_barrier((other, new))
         at_zero = lax.axis_index(axis) == 0
         piece = jnp.concatenate(
             [jnp.where(at_zero, piece, other), jnp.where(at_zero, other, piece)], axis=0
@@ -514,26 +536,14 @@
     )
     grad_half = jnp.where(is_physics, flat_b, flat_a)
 
-    new = vmem_call(
-        final_kernel,
-        [shape((FLAT, COLS), f32)],
-        [],
-        2,
-        3,
-        10**7,
-        6 * 10**6,
-        "final",
-    )(table, flags, field, own_out, back)[0]
     return new.reshape(columns.shape), grad_half
 
 
 def solution(mesh):
     lat, lon, grp = mesh.devices.shape
-    split = Mesh(
-        mesh.devices.reshape(lat, lon // 4, 2, 2, grp), ("lat", "y", "x", "core", "grp")
-    )
-    grid = P("lat", LON)
-    columns = P("grp", None, "lat", LON)
+    split = Mesh(mesh.devices.reshape(lat // 4, 2, 2, lon // 4, 2, 2, grp), LAT + LON + ("grp",))
+    grid = P(LAT, LON)
+    columns = P("grp", None, LAT, LON)
     return jax.shard_map(
         on_device,
         mesh=split,

time: 177 us -> 145 us (0.82)
  Pallas kernels: 40 us -> 21.6 us
  waiting for transfers between devices: 44.5 us -> 32.2 us
    all_to_all x1, waiting for transfers between devices: 12.9 us -> 0.51 us  [on_device(): back = lax.all_to_all(send_back, LON + ('grp',), 0, 0, tiled=True)]
    pallas_call x1, Pallas kernels: 15.1 us -> 7.16 us  [on_device(): vmem_call(transport_kernel, [shape((FLAT, COLS), f32), shape((FPAD, MINE)...]
    pallas_call x2, Pallas kernels: 10.8 us -> 3.78 us  [the longest x1 2.28 us: on_device(): vmem_call(backward_kernel, [shape((OWNERS // 2, PIECE, 128), f32)] * 2, [...]
    ppermute x5, starting transfers between devices: 4.14 us -> 9.85 us  [swap(): return lax.ppermute(value, axis, [(0, 1), (1, 0)])]
    all_to_all x1, starting transfers between devices: 8.88 us -> 4.72 us  [on_device(): back = lax.all_to_all(send_back, LON + ('grp',), 0, 0, tiled=True)]
    pallas_call x1, Pallas kernels: 9.22 us -> 5.7 us  [on_device(): vmem_call(forward_kernel, [shape((2 * FPAD, MINE), bf16), shape((HID, MIN...]
    all_to_all x1, blocking collectives: 24.6 us -> 22 us  [on_device(): lax.all_to_all(pieces, ('za', 'y', 'x', 'grp'), 0, 0, tiled=True)]
    all_to_all x1, blocking collectives: 15.7 us -> 18.2 us  [on_device(): lax.all_to_all(jnp.broadcast_to(piece[None], (members,) + piece.shape), r...]
where the time goes in v2:
time: 145 us; the launch traced here: 144 us
  blocking collectives  40.2 us (28%)
  waiting for transfers between devices  32.2 us (22%)
  starting transfers between devices  32 us (22%)
  Pallas kernels  21.6 us (15%)
  local copies, waits for them, and re-layouts  11.1 us (8%)
  other arithmetic  5.96 us (4%)
    all_to_all x1, blocking collectives, on_device(): lax.all_to_all(pieces, ('za', 'y', 'x', 'grp'), 0, 0, tiled=True)  22 us
    all_to_all x1, blocking collectives, on_device(): lax.all_to_all(jnp.broadcast_to(piece[None], (members,) + piece.shape), r...  18.2 us
    ppermute x5, waiting for transfers between devices, swap(): return lax.ppermute(value, axis, [(0, 1), (1, 0)])  16.1 us
    all_to_all x1, waiting for transfers between devices, on_device(): recv = lax.all_to_all(send, LON + ('grp',), 0, 0, tiled=True)  15.6 us
    ppermute x5, starting transfers between devices, swap(): return lax.ppermute(value, axis, [(0, 1), (1, 0)])  9.85 us
    all_to_all x1, starting transfers between devices, on_device(): recv = lax.all_to_all(send, LON + ('grp',), 0, 0, tiled=True)  7.68 us
    unnamed x34, local copies, waits for them, and re-layouts  7.51 us
    pallas_call x1, Pallas kernels, on_device(): vmem_call(transport_kernel, [shape((FLAT, COLS), f32), shape((FPAD, MINE)...  7.16 us
  transfers between devices with their start and end apart: 10, of which 6 were waited for; matrix products, arithmetic and copies ran while one was open for 3% of the time, Pallas kernels for 3%

profile of v2, /device:TPU:1, one launch (start us, length us, event | category | flops | bytes accessed | tf_op | source)
XLA Modules:
  0.0 144.2 jit_solution(6220848255781677851)
XLA Ops:
  0.8 1.6 %copy-done = f32[1,278,16,128]{3,2,1,0:T(8,128)S(1)} copy-done((f32[1,278,16,128]{3,2,1,0:T(8,128)S(1)}, f32[1,278,16,128]{3,2,1,0:T(8,128)}, u32[]{:S(2)}) %copy-start) | copy-done | bytes 2277400
  2.4 0.7 copy-done.7
  3.8 1.5 %rim.1 = (bf16[128,128]{1,0:T(8,128)(2,1)S(1)}, bf16[128,128]{1,0:T(8,128)(2,1)S(1)}, bf16[576,128]{1,0:T(8,128)(2,1)S(1)}) custom-call(f32[4]{0:T(128)S(1)} %pad_maximum_fusion.4.flags_ref.scale_ref, f32[4448,128]{1,0:T(8,128)S(1)} %bitcast.60, f32[16,128]{1,0:T(8,128)S(1)} %copy-done.7, f32[16,128]{1,0:T(8,128)S(1)} %copy-done.9), custom_call_target="tpu_custom_call" | custom-call | flops 100000000 | bytes 3000000 | tf_op jit(solution)/shard_map/rim/pallas_call | solution.py:405
  5.3 4.4 %collective-permute-start.1 = (bf16[576,128]{1,0:T(8,128)(2,1)S(1)}, bf16[576,128]{1,0:T(8,128)(2,1)S(1)}, u32[]{:S(2)}, u32[]{:S(2)}) collective-permute-start(bf16[576,128]{1,0:T(8,128)(2,1)S(1)} %get-tuple-element.22), channel_id=1, source_target_pairs={{0,32},{32,64},{64,96},{96,128},{128,160},{160,192},{192,224},{1,3... | collective-permute-start | bytes 442376 | tf_op jit(solution)/shard_map/ppermute | solution.py:416
  9.7 2.1 %collective-permute-start = (bf16[128,128]{1,0:T(8,128)(2,1)S(1)}, bf16[128,128]{1,0:T(8,128)(2,1)S(1)}, u32[]{:S(2)}, u32[]{:S(2)}) collective-permute-start(bf16[128,128]{1,0:T(8,128)(2,1)S(1)} %get-tuple-element.21), channel_id=1, source_target_pairs={{0,2},{2,4},{4,6},{6,8},{8,10},{10,12},{12,14},{14,16},{16,18},{18... | collective-permute-start | bytes 98312 | tf_op jit(solution)/shard_map/ppermute | solution.py:415
  11.8 3.3 %collective-permute-start.2 = (bf16[128,128]{1,0:T(8,128)(2,1)S(1)}, bf16[128,128]{1,0:T(8,128)(2,1)S(1)}, u32[]{:S(2)}, u32[]{:S(2)}) collective-permute-start(bf16[128,128]{1,0:T(8,128)(2,1)S(1)} %get-tuple-element.23), channel_id=1, source_target_pairs={{0,34},{2,36},{4,38},{6,40},{8,42},{10,44},{12,46},{14,48},{16,50}... | collective-permute-start | bytes 98312 | tf_op jit(solution)/shard_map/ppermute | solution.py:417
  15.1 0.7 add_select_fusion.1
  15.9 0.7 fusion.18
  16.6 0.8 fusion.11
  17.6 7.2 %transport.1 = (f32[4448,128]{1,0:T(8,128)S(1)}, bf16[288,1024]{1,0:T(8,128)(2,1)S(1)}, bf16[32,144,128]{2,1,0:T(8,128)(2,1)}) custom-call(s32[3,16]{1,0:T(4,128)S(1)} %pad_add_fusion.table_ref, f32[4]{0:T(128)S(1)} %pad_maximum_fusion.4.flags_ref.scale_ref, f32[4448,128]{1,0:T(8,128)S(1)} %bitcast.61, f32[16,128]{1,0:T(8,128)S(1)} %copy-done.8, ...), custom_call_target="tpu_custom_call" | custom-call | flops 100000000 | bytes 6000000 | tf_op jit(solution)/shard_map/transport/pallas_call | solution.py:450
  24.7 1.4 copy-done.2
  26.1 7.7 %all-to-all-start = ((bf16[32,144,128]{2,1,0:T(8,128)(2,1)}), bf16[32,144,128]{2,1,0:T(8,128)(2,1)S(1)}, u32[]{:S(2)}, u32[]{:S(2)}) async-start(bf16[32,144,128]{2,1,0:T(8,128)(2,1)} %get-tuple-element.25), calls=%async_computation | async-start | bytes 2359296 | tf_op jit(solution)/shard_map/all_to_all | solution.py:460
  35.5 15.6 %all-to-all-done.recv_ref = bf16[32,144,128]{2,1,0:T(8,128)(2,1)S(1)} async-done(((bf16[32,144,128]{2,1,0:T(8,128)(2,1)}), bf16[32,144,128]{2,1,0:T(8,128)(2,1)S(1)}, u32[]{:S(2)}, u32[]{:S(2)}) %all-to-all-start) | async-done | bytes 1179680 | tf_op jit(solution)/shard_map/all_to_all | solution.py:460
  51.1 1.1 copy-done.12
  52.1 5.7 %forward.1 = (bf16[576,1024]{1,0:T(8,128)(2,1)S(1)}, bf16[384,1024]{1,0:T(8,128)(2,1)S(1)}, bf16[384,1024]{1,0:T(8,128)(2,1)S(1)}, f32[384,1024]{1,0:T(8,128)S(1...) custom-call(s32[3,16]{1,0:T(4,128)S(1)} %pad_add_fusion.table_ref, ...), custom_call_target="tpu_custom_call" | custom-call | flops 1207959552 | bytes 8000000 | tf_op jit(solution)/shard_map/forward/pallas_call | solution.py:461
  57.8 2.3 %backward.1 = (f32[64,24,128]{2,1,0:T(8,128)S(1)}, f32[64,24,128]{2,1,0:T(8,128)S(1)}) custom-call(s32[3,16]{1,0:T(4,128)S(1)} %pad_add_fusion.table_ref, bf16[576,1024]{1,0:T(8,128)(2,1)S(1)} %get-tuple-element.26.inputs_ref, bf16[384,1024]{1,0:T(8,128)(2,1)S(1)} %get-tuple-element.27.hidden_ref, bf16[384,1024]{1,0:T(8,128)(2,1)S(1)} %get-tuple-element.28.g_two_ref, ...), custom_call_target="tpu_custom_call" | custom-call | flops 1056964608 | bytes 6000000 | tf_op jit(solution)/shard_map/backward/pallas_call | solution.py:480
  60.1 1.0 collective-permute-start.3
  61.1 1.9 %collective-permute-done.3 = f32[64,24,128]{2,1,0:T(8,128)S(1)} collective-permute-done((f32[64,24,128]{2,1,0:T(8,128)S(1)}, f32[64,24,128]{2,1,0:T(8,128)S(1)}, u32[]{:S(2)}, u32[]{:S(2)}) %collective-permute-start.3) | collective-permute-done | bytes 786464 | tf_op jit(solution)/shard_map/ppermute | solution.py:389
  63.2 1.7 %collective-permute-start.4 = (f32[32,24,128]{2,1,0:T(8,128)S(1)}, f32[32,24,128]{2,1,0:T(8,128)S(1)}, u32[]{:S(2)}, u32[]{:S(2)}) collective-permute-start(f32[32,24,128]{2,1,0:T(8,128)S(1)} %constant_dynamic-slice_fusion.1), channel_id=1, source_target_pairs={{0,32},{32,0},{1,33},{33,1},{2,34},{34,2},{3,35},{35,3},{4,36},{36... | collective-permute-start | bytes 1179656 | tf_op jit(solution)/shard_map/ppermute | solution.py:389
  64.9 4.7 %all-to-all-start.1 = ((bf16[32,144,128]{2,1,0:T(8,128)(2,1)}), bf16[32,144,128]{2,1,0:T(8,128)(2,1)S(1)}, u32[]{:S(2)}, u32[]{:S(2)}) async-start(bf16[32,144,128]{2,1,0:T(8,128)(2,1)} %get-tuple-element.33), calls=%async_computation.1 | async-start | bytes 2359296 | tf_op jit(solution)/shard_map/all_to_all | solution.py:479
  69.6 4.3 %collective-permute-done.4 = f32[32,24,128]{2,1,0:T(8,128)S(1)} collective-permute-done((f32[32,24,128]{2,1,0:T(8,128)S(1)}, f32[32,24,128]{2,1,0:T(8,128)S(1)}, u32[]{:S(2)}, u32[]{:S(2)}) %collective-permute-start.4) | collective-permute-done | bytes 393248 | tf_op jit(solution)/shard_map/ppermute | solution.py:389
  74.0 4.0 %collective-permute-start.5 = (f32[16,24,128]{2,1,0:T(8,128)S(1)}, f32[16,24,128]{2,1,0:T(8,128)S(1)}, u32[]{:S(2)}, u32[]{:S(2)}) collective-permute-start(f32[16,24,128]{2,1,0:T(8,128)S(1)} %constant_dynamic-slice_fusion), channel_id=1, source_target_pairs={{0,64},{64,0},{1,65},{65,1},{2,66},{66,2},{3,67},{67,3},{4,68},{68... | collective-permute-start | bytes 589832 | tf_op jit(solution)/shard_map/ppermute | solution.py:389
  78.0 8.4 %collective-permute-done.5 = f32[16,24,128]{2,1,0:T(8,128)S(1)} collective-permute-done((f32[16,24,128]{2,1,0:T(8,128)S(1)}, f32[16,24,128]{2,1,0:T(8,128)S(1)}, u32[]{:S(2)}, u32[]{:S(2)}) %collective-permute-start.5) | collective-permute-done | bytes 196640 | tf_op jit(solution)/shard_map/ppermute | solution.py:389
  87.0 22.0 %all_to_all.20 = f32[32,16,128]{2,1,0:T(8,128)} all-to-all(f32[32,16,128]{2,1,0:T(8,128)S(1)} %bitcast.70), channel_id=1, replica_groups=mesh['za'=2,'zb'=2,'zc'=2,'y'=4,'x'=2,'core'=2,'grp'=2] {'za','y','x','g..., dimensions={0} | all-to-all | bytes 524288 | tf_op jit(solution)/shard_map/all_to_all | solution.py:501
  109.0 1.0 reduce_sum.39
  110.0 18.2 %all_to_all.21 = f32[32,16,128]{2,1,0:T(8,128)} all-to-all(f32[32,16,128]{2,1,0:T(8,128)S(1)} %broadcast_in_dim.27), channel_id=1, replica_groups=mesh['za'=2,'zb'=2,'zc'=2,'y'=4,'x'=2,'core'=2,'grp'=2] {'za','zb','zc',..., dimensions={0} | all-to-all | bytes 524288 | tf_op jit(solution)/shard_map/all_to_all | solution.py:504
  128.2 1.1 copy-done.6
  129.2 5.0 %final.1 = f32[4448,128]{1,0:T(8,128)} custom-call(s32[3,16]{1,0:T(4,128)S(1)} %pad_add_fusion.table_ref, f32[4]{0:T(128)S(1)} %pad_maximum_fusion.4.flags_ref.scale_ref, f32[4448,128]{1,0:T(8,128)S(1)} %copy-done.3, bf16[288,1024]{1,0:T(8,128)(2,1)S(1)} %copy-done.6, bf16[32,144,128]{2,1,0:T(8,128)(2,1)S(1)} %all-to-all-done.1.recv_ref), custom_call_target="tpu_custom_call" | custom-call | flops 10000000 | bytes 6000000 | tf_op jit(solution)/shard_map/final/pallas_call | solution.py:507
  134.2 1.1 broadcast_select_fusion.7
  135.3 3.2 %collective-permute-start.7 = (f32[64,16,128]{2,1,0:T(8,128)S(1)}, f32[64,16,128]{2,1,0:T(8,128)S(1)}, u32[]{:S(2)}, u32[]{:S(2)}) collective-permute-start(f32[64,16,128]{2,1,0:T(8,128)S(1)} %pad_maximum_fusion.2), channel_id=1, source_target_pairs={{0,2},{2,0},{1,3},{3,1},{4,6},{6,4},{5,7},{7,5},{8,10},{10,8},{9,1... | collective-permute-start | bytes 1572872 | tf_op jit(solution)/shard_map/ppermute | solution.py:389
  138.5 1.5 %collective-permute-done.7 = f32[64,16,128]{2,1,0:T(8,128)S(1)} collective-permute-done((f32[64,16,128]{2,1,0:T(8,128)S(1)}, f32[64,16,128]{2,1,0:T(8,128)S(1)}, u32[]{:S(2)}, u32[]{:S(2)}) %collective-permute-start.7) | collective-permute-done | bytes 524320 | tf_op jit(solution)/shard_map/ppermute | solution.py:389
  143.1 1.1 maximum_select_fusion
  (74 shorter events, 6.3 us)
Async XLA Ops:
  0.6 16.9 %copy-start.8 = (f32[16,128]{1,0:T(8,128)S(1)}, f32[16,128]{1,0:T(8,128)}, u32[]{:S(2)}) copy-start(f32[16,128]{1,0:T(8,128)} %east_ref.3) | copy-start | bytes 24580
  0.6 16.9 %copy-start.10 = (f32[16,128]{1,0:T(8,128)S(1)}, f32[16,128]{1,0:T(8,128)}, u32[]{:S(2)}) copy-start(f32[16,128]{1,0:T(8,128)} %north_ref.3) | copy-start | bytes 24580
  0.8 1.6 %copy-start = (f32[1,278,16,128]{3,2,1,0:T(8,128)S(1)}, f32[1,278,16,128]{3,2,1,0:T(8,128)}, u32[]{:S(2)}) copy-start(f32[1,278,16,128]{3,2,1,0:T(8,128)} %param.9) | copy-start | bytes 6832132
  2.4 0.7 copy-start.7
  3.1 0.7 copy-start.9
  3.8 13.8 %copy-start.1 = (f32[1,278,16,128]{3,2,1,0:T(8,128)S(1)}, f32[1,278,16,128]{3,2,1,0:T(8,128)}, u32[]{:S(2)}) copy-start(f32[1,278,16,128]{3,2,1,0:T(8,128)} %param.9) | copy-start | bytes 6832132
  5.3 12.2 %collective-permute-start.1 = (bf16[576,128]{1,0:T(8,128)(2,1)S(1)}, bf16[576,128]{1,0:T(8,128)(2,1)S(1)}, u32[]{:S(2)}, u32[]{:S(2)}) collective-permute-start(bf16[576,128]{1,0:T(8,128)(2,1)S(1)} %get-tuple-element.22), channel_id=1, source_target_pairs={{0,32},{32,64},{64,96},{96,128},{128,160},{160,192},{192,224},{1,3... | collective-permute-start | bytes 442376 | tf_op jit(solution)/shard_map/ppermute | solution.py:416
  9.7 7.8 %collective-permute-start = (bf16[128,128]{1,0:T(8,128)(2,1)S(1)}, bf16[128,128]{1,0:T(8,128)(2,1)S(1)}, u32[]{:S(2)}, u32[]{:S(2)}) collective-permute-start(bf16[128,128]{1,0:T(8,128)(2,1)S(1)} %get-tuple-element.21), channel_id=1, source_target_pairs={{0,2},{2,4},{4,6},{6,8},{8,10},{10,12},{12,14},{14,16},{16,18},{18... | collective-permute-start | bytes 98312 | tf_op jit(solution)/shard_map/ppermute | solution.py:415
  11.8 5.7 %collective-permute-start.2 = (bf16[128,128]{1,0:T(8,128)(2,1)S(1)}, bf16[128,128]{1,0:T(8,128)(2,1)S(1)}, u32[]{:S(2)}, u32[]{:S(2)}) collective-permute-start(bf16[128,128]{1,0:T(8,128)(2,1)S(1)} %get-tuple-element.23), channel_id=1, source_target_pairs={{0,34},{2,36},{4,38},{6,40},{8,42},{10,44},{12,46},{14,48},{16,50}... | collective-permute-start | bytes 98312 | tf_op jit(solution)/shard_map/ppermute | solution.py:417
  24.7 1.4 copy-start.2
  26.1 7.7 %copy-start.11 = (bf16[288,1024]{1,0:T(8,128)(2,1)}, bf16[288,1024]{1,0:T(8,128)(2,1)S(1)}, u32[]{:S(2)}) copy-start(bf16[288,1024]{1,0:T(8,128)(2,1)S(1)} %get-tuple-element.24.own_ref) | copy-start | bytes 1769476
  26.1 7.7 %copy-start.14 = (bf16[556,384]{1,0:T(8,128)(2,1)S(1)}, bf16[556,384]{1,0:T(8,128)(2,1)}, u32[]{:S(2)}) copy-start(bf16[556,384]{1,0:T(8,128)(2,1)} %param.14) | copy-start | bytes 1281028
  26.1 8.0 %copy-start.4 = (bf16[384,384]{1,0:T(8,128)(2,1)S(1)}, bf16[384,384]{1,0:T(8,128)(2,1)}, u32[]{:S(2)}) copy-start(bf16[384,384]{1,0:T(8,128)(2,1)} %w_mid_ref.1) | copy-start | bytes 884740
  26.1 25.0 %all-to-all-start = ((bf16[32,144,128]{2,1,0:T(8,128)(2,1)}), bf16[32,144,128]{2,1,0:T(8,128)(2,1)S(1)}, u32[]{:S(2)}, u32[]{:S(2)}) async-start(bf16[32,144,128]{2,1,0:T(8,128)(2,1)} %get-tuple-element.25), calls=%async_computation | async-start | bytes 2359296 | tf_op jit(solution)/shard_map/all_to_all | solution.py:460
  33.8 1.0 copy-start.13
  33.8 1.0 copy-start.15
  51.1 1.1 copy-start.12
  57.8 2.3 %copy-start.5 = (bf16[288,1024]{1,0:T(8,128)(2,1)}, bf16[288,1024]{1,0:T(8,128)(2,1)S(1)}, u32[]{:S(2)}) copy-start(bf16[288,1024]{1,0:T(8,128)(2,1)S(1)} %get-tuple-element.36.own_ref) | copy-start | bytes 1769476
  60.1 2.9 %collective-permute-start.3 = (f32[64,24,128]{2,1,0:T(8,128)S(1)}, f32[64,24,128]{2,1,0:T(8,128)S(1)}, u32[]{:S(2)}, u32[]{:S(2)}) collective-permute-start(f32[64,24,128]{2,1,0:T(8,128)S(1)} %get-tuple-element.32), channel_id=1, source_target_pairs={{0,2},{2,0},{1,3},{3,1},{4,6},{6,4},{5,7},{7,5},{8,10},{10,8},{9,1... | collective-permute-start | bytes 2359304 | tf_op jit(solution)/shard_map/ppermute | solution.py:389
  63.2 10.7 %collective-permute-start.4 = (f32[32,24,128]{2,1,0:T(8,128)S(1)}, f32[32,24,128]{2,1,0:T(8,128)S(1)}, u32[]{:S(2)}, u32[]{:S(2)}) collective-permute-start(f32[32,24,128]{2,1,0:T(8,128)S(1)} %constant_dynamic-slice_fusion.1), channel_id=1, source_target_pairs={{0,32},{32,0},{1,33},{33,1},{2,34},{34,2},{3,35},{35,3},{4,36},{36... | collective-permute-start | bytes 1179656 | tf_op jit(solution)/shard_map/ppermute | solution.py:389
  64.9 22.0 %all-to-all-start.1 = ((bf16[32,144,128]{2,1,0:T(8,128)(2,1)}), bf16[32,144,128]{2,1,0:T(8,128)(2,1)S(1)}, u32[]{:S(2)}, u32[]{:S(2)}) async-start(bf16[32,144,128]{2,1,0:T(8,128)(2,1)} %get-tuple-element.33), calls=%async_computation.1 | async-start | bytes 2359296 | tf_op jit(solution)/shard_map/all_to_all | solution.py:479
  74.0 12.3 %collective-permute-start.5 = (f32[16,24,128]{2,1,0:T(8,128)S(1)}, f32[16,24,128]{2,1,0:T(8,128)S(1)}, u32[]{:S(2)}, u32[]{:S(2)}) collective-permute-start(f32[16,24,128]{2,1,0:T(8,128)S(1)} %constant_dynamic-slice_fusion), channel_id=1, source_target_pairs={{0,64},{64,0},{1,65},{65,1},{2,66},{66,2},{3,67},{67,3},{4,68},{68... | collective-permute-start | bytes 589832 | tf_op jit(solution)/shard_map/ppermute | solution.py:389
  86.9 41.3 %copy-start.3 = (f32[4448,128]{1,0:T(8,128)S(1)}, f32[4448,128]{1,0:T(8,128)}, u32[]{:S(2)}) copy-start(f32[4448,128]{1,0:T(8,128)} %copy-done.2) | copy-start | bytes 6832132
  128.2 6.0 %collective-permute-start.6 = (f32[32,16,128]{2,1,0:T(8,128)}, f32[32,16,128]{2,1,0:T(8,128)}, u32[]{:S(2)}, u32[]{:S(2)}) collective-permute-start(f32[32,16,128]{2,1,0:T(8,128)} %all_to_all.21), channel_id=1, source_target_pairs={{0,4},{4,0},{1,5},{5,1},{2,6},{6,2},{3,7},{7,3},{8,12},{12,8},{9,1... | collective-permute-start | bytes 786440 | tf_op jit(solution)/shard_map/ppermute | solution.py:389
  128.2 1.1 copy-start.6
  135.3 4.7 %collective-permute-start.7 = (f32[64,16,128]{2,1,0:T(8,128)S(1)}, f32[64,16,128]{2,1,0:T(8,128)S(1)}, u32[]{:S(2)}, u32[]{:S(2)}) collective-permute-start(f32[64,16,128]{2,1,0:T(8,128)S(1)} %pad_maximum_fusion.2), channel_id=1, source_target_pairs={{0,2},{2,0},{1,3},{3,1},{4,6},{6,4},{5,7},{7,5},{8,10},{10,8},{9,1... | collective-permute-start | bytes 1572872 | tf_op jit(solution)/shard_map/ppermute | solution.py:389

commit v3 on v2

--- a/solution.py
+++ b/solution.py
@@ -22,7 +22,8 @@
 MINE = ROWS * COLS // 2
 LON = ("y", "x", "core")
 LAT = ("za", "zb", "zc")
-VMEM_LIMIT = 24 * 1024 * 1024
+MIB = 1024 * 1024
+ALL_VMEM = 60
 
 NT = (((1,), (1,)), ((), ()))
 TN = (((0,), (0,)), ((), ()))
@@ -35,15 +36,16 @@
 PIECE = A_PIECE + B_PIECE
 
 
-def vmem_call(kernel, outs, scratch, n_smem, n_vmem, flops, size, name):
+def vmem_call(kernel, outs, scratch, places, flops, size, name, limit, out_places=None):
+    spaces = {"s": pltpu.SMEM, "v": pltpu.VMEM, "h": pltpu.HBM}
+    out_places = out_places or "v" * len(outs)
     return pl.pallas_call(
         kernel,
         out_shape=outs,
-        in_specs=[pl.BlockSpec(memory_space=pltpu.SMEM)] * n_smem
-        + [pl.BlockSpec(memory_space=pltpu.VMEM)] * n_vmem,
-        out_specs=jax.tree.map(lambda _: pl.BlockSpec(memory_space=pltpu.VMEM), outs),
+        in_specs=[pl.BlockSpec(memory_space=spaces[p]) for p in places],
+        out_specs=[pl.BlockSpec(memory_space=spaces[p]) for p in out_places],
         scratch_shapes=scratch,
-        compiler_params=pltpu.CompilerParams(vmem_limit_bytes=VMEM_LIMIT),
+        compiler_params=pltpu.CompilerParams(vmem_limit_bytes=limit * MIB),
         cost_estimate=pl.CostEstimate(flops=flops, bytes_accessed=size, transcendentals=0),
         name=name,
     )
@@ -62,9 +64,7 @@
     return full, FEAT - full * 8
 
 
-def coefficients(east, north, flags_ref):
-    dyn = flags_ref[0]
-    not_top = flags_ref[1]
+def coefficients(east, north, dyn, not_top):
     rows = row_ids(north.shape)
     north = jnp.where(rows == ROWS - 1, north * not_top, north) * dyn
     east = east * dyn
@@ -74,27 +74,78 @@
     return east, north, keep, west, south
 
 
-def step(q, keep, west, south):
-    shaped = q.reshape(-1, ROWS, COLS)
-    out = (
-        keep[None] * shaped
-        + west[None] * pltpu.roll(shaped, 1, 2)
-        + south[None] * pltpu.roll(shaped, 1, 1)
-    )
-    return out
-
-
 def tiled_column(value, lane):
     column = jnp.broadcast_to(value[:, lane : lane + 1], (ROWS, COLS))
     return jnp.concatenate([column] * 8, axis=0)
 
 
-def rim_kernel(flags_ref, x_ref, east_ref, north_ref, rim_ref, corner_ref, north_out_ref):
-    east, north, keep, west, south = coefficients(east_ref[...], north_ref[...], flags_ref)
+def block_table(is_physics, lon, facts, targets, costs, own_targets, own_costs):
+    ids = lax.broadcasted_iota(jnp.int32, (ROWS, ROWS), 0)
+    ks = lax.broadcasted_iota(jnp.int32, (ROWS, ROWS), 1)
+    own_targets = jnp.broadcast_to(own_targets, (ROWS, ROWS))
+    own_costs = jnp.broadcast_to(own_costs, (ROWS, ROWS))
+    at_home = own_targets // ROWS == ids
+    at_slot = targets // ROWS == lon
+    rows = jnp.where(
+        is_physics, jnp.where(at_slot, targets % ROWS, 0), jnp.where(at_home, ks, 0)
+    )
+    costs = jnp.where(is_physics, jnp.where(at_slot, costs, 0), jnp.where(at_home, own_costs, 0))
+    rows = jnp.sum(rows, axis=1, keepdims=True)
+    costs = jnp.sum(costs, axis=1, keepdims=True)
+    lane = lane_ids((ROWS, COLS))
+    table = jnp.where(lane == 0, rows, jnp.where(lane == 1, costs, 0))
+    for k, fact in enumerate(facts):
+        table = jnp.where(lane == 2 + k, fact, table)
+    return table
+
+
+GROUPS = -(-FEAT // 8)
+X_CUTS = tuple(range(0, FLAT, 1024)) + (FLAT,)
+
+
+def rim_kernel(
+    x_hbm, east_hbm, north_hbm, assign_hbm, cost_hbm,
+    rim_ref, corner_ref, north_out_ref, table_ref,
+    x_ref, east_ref, north_ref, assign_ref, cost_ref, sems,
+):
+    band = lax.axis_index(LAT)
+    lon = lax.axis_index(LON)
+    grp = lax.axis_index("grp")
+    core = lax.axis_index("core")
+    not_top = jnp.where(band != lax.axis_size(LAT) - 1, 1, 0)
+    copies = [
+        pltpu.make_async_copy(x_hbm.at[pl.ds(a, b - a)], x_ref.at[pl.ds(a, b - a)], sems.at[i])
+        for i, (a, b) in enumerate(zip(X_CUTS[:-1], X_CUTS[1:]))
+    ]
+    n = len(copies)
+    small = [
+        pltpu.make_async_copy(east_hbm, east_ref, sems.at[n]),
+        pltpu.make_async_copy(north_hbm, north_ref, sems.at[n + 1]),
+        pltpu.make_async_copy(assign_hbm.at[band], assign_ref, sems.at[n + 2]),
+        pltpu.make_async_copy(cost_hbm.at[band], cost_ref, sems.at[n + 3]),
+    ]
+    for copy in small + copies:
+        copy.start()
+    for copy in small:
+        copy.wait()
+    table_ref[...] = block_table(
+        grp == 1,
+        lon,
+        (not_top, 1 - grp, grp * (COLS // 2), core),
+        assign_ref[...],
+        cost_ref[...],
+        assign_ref[pl.ds(lon, 1), :],
+        cost_ref[pl.ds(lon, 1), :],
+    )
+    east, north, keep, west, south = coefficients(
+        east_ref[...], north_ref[...], (1 - grp).astype(f32), not_top.astype(f32)
+    )
     full, rest = chunks()
     lane = lane_ids((128, COLS))
     picked = jnp.zeros((128, COLS), f32)
     for g in range(full):
+        if g % 8 == 0:
+            copies[g // 8].wait()
         turned = pltpu.roll(x_ref[g * 128 : (g + 1) * 128, :], 2 * g + 2, 1)
         picked = jnp.where(lane // 2 == g, turned, picked)
     tail = pltpu.roll(x_ref[full * 128 :, :], 2 * full + 2, 1)
@@ -131,72 +182,100 @@
 
 
 def transport_kernel(
-    table_ref, flags_ref, x_ref, east_ref, north_ref, rim_ref, south_ref, corner_ref,
-    field_ref, own_ref, send_ref, mid_ref, inflow_ref,
+    table_ref, x_hbm, east_ref, north_ref, rim_ref, south_ref, corner_ref,
+    field_hbm, own_hbm, send_hbm,
+    x_ref, field_ref, inflow_ref, rims_ref, south32_ref, own_ref, send_ref, sems,
 ):
-    east, north, keep, west, south = coefficients(east_ref[...], north_ref[...], flags_ref)
-    full, rest = chunks()
+    x_in = [
+        pltpu.make_async_copy(
+            x_hbm.at[pl.ds(a, b - a)], x_ref.at[pl.ds(a, b - a)], sems.at[1 + ROWS + ROWS // 2 + i]
+        )
+        for i, (a, b) in enumerate(zip(X_CUTS[:-1], X_CUTS[1:]))
+    ]
+    for copy in x_in:
+        copy.start()
+    x_ref[FLAT:, :] = jnp.zeros((x_ref.shape[0] - FLAT, COLS), f32)
+    field_ref[:, GROUPS * 8 :, :] = jnp.zeros((ROWS, FPAD - GROUPS * 8, COLS), f32)
+    south32_ref[...] = south_ref[...].astype(f32)
+    to_slot = table_ref[0, 3]
+    is_dyn = to_slot == 1
+    east, north, keep, west, south = coefficients(
+        east_ref[...], north_ref[...], to_slot.astype(f32), table_ref[0, 2].astype(f32)
+    )
+    west = jnp.where(lane_ids(west.shape) == 0, 1.0, west)
+    keep, west, south = (value.reshape(ROWS, 1, COLS) for value in (keep, west, south))
     lane = lane_ids((128, COLS))
-    odd = lane % 2 == 1
     rim = rim_ref[...].astype(f32)
     corner = pltpu.roll(corner_ref[...].astype(f32), 128 - (ROWS - 1), 0)
     east_courant = rim[0:1, COLS - 1 : COLS]
-    north_courant = south_ref[FEAT : FEAT + 1, 0:1].astype(f32)
+    north_courant = south32_ref[FEAT : FEAT + 1, 0:1]
     lacked = corner * east_courant + pltpu.roll(corner, COLS - 1, 1) * north_courant
-    fix = jnp.logical_and(row_ids((128, COLS)) % ROWS == 0, jnp.logical_not(odd))
+    fix = jnp.logical_and(row_ids((128, COLS)) % ROWS == 0, lane % 2 == 0)
     inflow_ref[...] = rim + jnp.where(fix, lacked, 0.0)
-
-    def stage(source, target, g, count, shift):
-        rows = pl.ds(pl.multiple_of(g * 128, 128), count * ROWS)
-        inflow = pltpu.roll(inflow_ref[0 : count * ROWS, :], shift, 1)
-        inflow = jnp.where(lane[: count * ROWS] == 0, inflow, 0.0)
-        after = step(source[rows, :], keep, west, south).reshape(count * ROWS, COLS)
-        target[rows, :] = after + inflow
-
-    row0 = pl.ds(0, FEAT, stride=ROWS)
-
-    def first_body(g, carry):
-        stage(x_ref, mid_ref, g, 8, COLS - 1 - 2 * g)
+    for k in range(ROWS):
+        rims_ref[k] = inflow_ref[pl.ds(k, 8, stride=ROWS), :]
+    last = lane_ids((ROWS, 8, COLS)) == COLS - 1
+
+    def transported(q, shift, from_south):
+        inflow = pltpu.roll(rims_ref[...], shift, 2)
+        shifted = pltpu.roll(jnp.where(last, inflow, q), 1, 2)
+        under = jnp.concatenate([q[ROWS - 1 :], q[: ROWS - 1]], axis=0)
+        after = keep * q + west * shifted + south * under
+        return jnp.concatenate([after[:1] + from_south[None], after[1:]], axis=0)
+
+    def group(g, carry):
+        rows = x_ref[pl.ds(pl.multiple_of(g * 128, 128), 128), :].reshape(8, ROWS, COLS)
+        features = pl.ds(pl.multiple_of(g * 8, 8), 8)
+        q = jnp.swapaxes(rows, 0, 1)
+        q = transported(q, COLS - 2 - 2 * g, south32_ref[features, :])
+        over = pl.ds(pl.multiple_of(FPAD + g * 8, 8), 8)
+        field_ref[:, features, :] = transported(q, COLS - 1 - 2 * g, south32_ref[over, :])
         return carry
 
-    lax.fori_loop(0, full, first_body, 0, unroll=4)
-    stage(x_ref, mid_ref, full, rest, COLS - 1 - 2 * full)
-    mid_ref[row0, :] = mid_ref[row0, :] + south_ref[0:FEAT, :].astype(f32)
-
-    def second_body(g, carry):
-        stage(mid_ref, field_ref, g, 8, COLS - 2 * g)
-        return carry
-
-    lax.fori_loop(1, full, second_body, 0, unroll=4)
-    stage(mid_ref, field_ref, 0, 8, 0)
-    stage(mid_ref, field_ref, full, rest, COLS - 2 * full)
-    field_ref[row0, :] = field_ref[row0, :] + south_ref[FPAD : FPAD + FEAT, :].astype(f32)
-
-    to_slot = table_ref[2, 1]
-    is_dyn = to_slot == 1
+    field_out = []
+    n_cuts = len(x_in)
+    for i, copy in enumerate(x_in):
+        copy.wait()
+        first, end = 8 * i, min(8 * i + 8, GROUPS)
+        lax.fori_loop(first, end, group, 0, unroll=4 if end - first == 8 else True)
+        part = pl.ds(8 * first, 8 * (end - first) if end < GROUPS else FPAD - 8 * first)
+        field_out.append(
+            pltpu.make_async_copy(
+                field_ref.at[:, part], field_hbm.at[:, part], sems.at[1 + ROWS + ROWS // 2 + n_cuts + i]
+            )
+        )
+        field_out[-1].start()
+
     low = lane_ids((PACK, COLS)) < COLS // 2
     low_full = lane_ids((FPAD, COLS)) < COLS // 2
-    zeros = jnp.zeros((FPAD - FEAT, COLS), f32)
 
     def pair_body(i, carry):
         kept = []
         for side in range(2):
             r = 2 * i + side
-            rows = pl.ds(table_ref[0, r], FEAT, stride=ROWS)
-            here = jnp.concatenate([field_ref[rows, :], zeros], axis=0)
+            here = field_ref[table_ref[r, 0]]
             turned = pltpu.roll(here, COLS // 2, 1)
             value = jnp.where(is_dyn, here, turned)
             other = jnp.where(is_dyn, turned, here)
             packed = jnp.where(low, other[:PACK], value[PACK:])
-            send_ref[2 * r + to_slot] = packed.astype(bf16)
-            send_ref[2 * r + 1 - to_slot] = jnp.zeros((PACK, COLS), bf16)
+            send_ref[r] = packed.astype(bf16)
+            pltpu.make_async_copy(
+                send_ref.at[r], send_hbm.at[2 * r + to_slot], sems.at[1 + r]
+            ).start()
             kept.append(value if side == 0 else other)
-        own_ref[:, pl.ds(pl.multiple_of(i * COLS, COLS), COLS)] = jnp.where(
-            low_full, kept[0], kept[1]
-        ).astype(bf16)
+        own_ref[i] = jnp.where(low_full, kept[0], kept[1]).astype(bf16)
+        pltpu.make_async_copy(own_ref.at[i], own_hbm.at[i], sems.at[1 + ROWS + i]).start()
         return carry
 
     lax.fori_loop(0, ROWS // 2, pair_body, 0, unroll=2)
+    for copy in field_out:
+        copy.wait()
+    for r in range(ROWS):
+        pltpu.make_async_copy(
+            send_ref.at[r], send_hbm.at[2 * r + to_slot], sems.at[1 + r]
+        ).wait()
+    for i in range(ROWS // 2):
+        pltpu.make_async_copy(own_ref.at[i], own_hbm.at[i], sems.at[1 + ROWS + i]).wait()
 
 
 def sigmoid(value):
@@ -211,8 +290,8 @@
     table_ref, own_ref, recv_ref, w_one_ref, w_two_ref, w_three_ref, gain_ref,
     inputs_ref, hidden_ref, g_two_ref, slope_ref, own_out_ref, send_ref, vec_ref,
 ):
-    from_slot = table_ref[2, 1]
-    offset = table_ref[2, 2]
+    from_slot = table_ref[0, 3]
+    offset = table_ref[0, 4]
     low = lane_ids((PACK, COLS)) < COLS // 2
     gain = gain_ref[...]
     loss_norm = 1.0 / math.sqrt(ROWS * 8 * COLS * ROWS)
@@ -220,15 +299,15 @@
     tile = 2 * COLS
     vec_ref[...] = jnp.zeros(vec_ref.shape, f32)
 
-    def tile_body(t, carry):
-        lanes = pl.ds(pl.multiple_of(t * tile, tile), tile)
+    for t in range(MINE // tile):
+        lanes = slice(t * tile, (t + 1) * tile)
         live_parts = []
         for g in range(2):
             i = 2 * t + g
-            group = pl.ds(pl.multiple_of(i * COLS, COLS), COLS)
+            group = slice(i * COLS, (i + 1) * COLS)
             first = recv_ref[4 * i + from_slot].astype(f32)
             second = recv_ref[4 * i + 2 + from_slot].astype(f32)
-            inputs_ref[0:FPAD, group] = own_ref[:, group]
+            inputs_ref[0:FPAD, group] = own_ref[i]
             inputs_ref[FPAD : FPAD + PACK, group] = jnp.where(
                 low, first, swap_halves(second)
             ).astype(bf16)
@@ -237,7 +316,7 @@
             ).astype(bf16)
             lane = lane_ids((1, COLS))
             column = lane % (COLS // 2) + offset
-            cost = jnp.where(lane < COLS // 2, table_ref[1, 2 * i], table_ref[1, 2 * i + 1])
+            cost = jnp.where(lane < COLS // 2, table_ref[2 * i, 1], table_ref[2 * i + 1, 1])
             live_parts.append(jnp.where(column < cost, 1.0, 0.0))
         live = jnp.concatenate(live_parts, axis=1)
         inputs = inputs_ref[:, lanes]
@@ -280,9 +359,6 @@
             jnp.where(rows == 1, mid.astype(f32), jnp.where(rows == 2, low_part.astype(f32), 0.0)),
         ).astype(bf16)
         vec_ref[...] += lax.dot_general(stacked, hidden_two, NT, preferred_element_type=f32)
-        return carry
-
-    lax.fori_loop(0, MINE // tile, tile_body, 0, unroll=True)
 
 
 def place(owner):
@@ -296,8 +372,8 @@
     table_ref, inputs_ref, hidden_ref, g_two_ref, slope_ref, w_mid_ref, vec_ref,
     keep_ref, send_ref, g_one_ref, d_in_ref,
 ):
-    state_first = table_ref[2, 3]
-    core = table_ref[2, 4]
+    state_first = table_ref[0, 3]
+    core = table_ref[0, 5]
     tile = 2 * COLS
 
     def tile_body(t, carry):
@@ -355,12 +431,11 @@
         write((send_ref, keep_ref))
 
 
-def final_kernel(table_ref, scale_ref, field_ref, own_ref, recv_ref, out_ref):
-    from_slot = table_ref[2, 1]
+def final_kernel(table_ref, field_ref, own_ref, recv_ref, out_ref, new_ref):
+    from_slot = table_ref[0, 3]
     is_dyn = from_slot == 1
-    keep_scale = scale_ref[2]
-    new_scale = scale_ref[3]
-    low = lane_ids((PACK, COLS)) < COLS // 2
+    keep_scale = jnp.where(is_dyn, 1.0, 0.0)
+    new_scale = jnp.where(is_dyn, 0.5, 1.0)
     low_full = lane_ids((FPAD, COLS)) < COLS // 2
 
     def pair_body(i, carry):
@@ -370,15 +445,24 @@
             chunk = recv_ref[2 * r + from_slot].astype(f32)
             theirs = jnp.concatenate([swap_halves(chunk), chunk], axis=0)
             mine = pair if side == 0 else swap_halves(pair)
-            tend = jnp.where(low_full, mine, theirs)[:FEAT]
+            tend = jnp.where(low_full, mine, theirs)
             tend = jnp.where(is_dyn, tend, swap_halves(tend))
-            rows = pl.ds(table_ref[0, r], FEAT, stride=ROWS)
-            old = field_ref[rows, :]
-            live = lane_ids((FEAT, COLS)) < table_ref[1, r]
-            out_ref[rows, :] = jnp.where(live, keep_scale * old + new_scale * tend, old)
+            old = field_ref[table_ref[r, 0]]
+            live = lane_ids((FPAD, COLS)) < table_ref[r, 1]
+            new_ref[table_ref[r, 0]] = jnp.where(live, keep_scale * old + new_scale * tend, old)
         return carry
 
     lax.fori_loop(0, ROWS // 2, pair_body, 0, unroll=2)
+    full, rest = chunks()
+
+    def group(g, carry):
+        value = jnp.swapaxes(new_ref[:, pl.ds(pl.multiple_of(g * 8, 8), 8), :], 0, 1)
+        out_ref[pl.ds(pl.multiple_of(g * 128, 128), 128), :] = value.reshape(128, COLS)
+        return carry
+
+    lax.fori_loop(0, full, group, 0, unroll=2)
+    value = jnp.swapaxes(new_ref[:, full * 8 : full * 8 + 8, :], 0, 1).reshape(128, COLS)
+    out_ref[full * 128 :, :] = value[: rest * ROWS]
 
 
 def shape(dims, dtype):
@@ -390,28 +474,34 @@
 
 
 def on_device(columns, east_courant, north_courant, assign, block_cost, w_in, w_mid, w_out, energy):
-    band = lax.axis_index(LAT)
     bands = lax.axis_size(LAT)
-    lon = lax.axis_index(LON)
     lons = lax.axis_size(LON)
-    grp = lax.axis_index("grp")
-    is_physics = grp == 1
+    is_physics = lax.axis_index("grp") == 1
     stored = columns.reshape(FLAT, COLS)
 
-    dyn = (1 - grp).astype(f32)
-    flags = jnp.stack(
-        [dyn, (band != bands - 1).astype(f32), jnp.where(is_physics, 0.0, 1.0), jnp.where(is_physics, 1.0, 0.5)]
-    )
-    rim, corner, north_out = vmem_call(
+    n_copies = len(X_CUTS) - 1 + 4
+    rim, corner, north_out, table = vmem_call(
         rim_kernel,
-        [shape((128, COLS), bf16), shape((128, COLS), bf16), shape((2 * FPAD, COLS), bf16)],
-        [],
-        1,
-        3,
+        [
+            shape((128, COLS), bf16),
+            shape((128, COLS), bf16),
+            shape((2 * FPAD, COLS), bf16),
+            shape((ROWS, COLS), jnp.int32),
+        ],
+        [
+            pltpu.VMEM((FLAT, COLS), f32),
+            pltpu.VMEM((ROWS, COLS), f32),
+            pltpu.VMEM((ROWS, COLS), f32),
+            pltpu.VMEM((ROWS, ROWS), jnp.int32),
+            pltpu.VMEM((ROWS, ROWS), jnp.int32),
+            pltpu.SemaphoreType.DMA((n_copies,)),
+        ],
+        "hhhhh",
         10**8,
         3 * 10**6,
         "rim",
-    )(flags, stored, east_courant, north_courant)
+        ALL_VMEM,
+    )(stored, east_courant, north_courant, assign, block_cost)
     from_west = lax.ppermute(rim, LON, [(i, (i + 1) % lons) for i in range(lons)])
     from_south = lax.ppermute(north_out, LAT, [(i, i + 1) for i in range(bands - 1)])
     from_corner = lax.ppermute(
@@ -420,20 +510,6 @@
         [(b * lons + i, (b + 1) * lons + (i + 1) % lons) for b in range(bands - 1) for i in range(lons)],
     )
 
-    targets = lax.dynamic_index_in_dim(assign, band, 0, keepdims=False)
-    costs = lax.dynamic_index_in_dim(block_cost, band, 0, keepdims=False)
-    owner = targets // ROWS
-    ids = lax.broadcasted_iota(jnp.int32, (ROWS, ROWS), 0)
-    ks = lax.broadcasted_iota(jnp.int32, (ROWS, ROWS), 1)
-    here_owner = lax.dynamic_index_in_dim(owner, lon, 0, keepdims=True)
-    here_cost = lax.dynamic_index_in_dim(costs, lon, 0, keepdims=True)
-    match = jnp.where(is_physics, owner == lon, here_owner == ids)
-    row_of = jnp.sum(jnp.where(match, jnp.where(is_physics, targets % ROWS, ks), 0), axis=1)
-    cost_of = jnp.sum(jnp.where(match, jnp.where(is_physics, costs, here_cost), 0), axis=1)
-    half = COLS // 2
-    facts = jnp.stack([grp * half, 1 - grp, grp * half, 1 - grp, lax.axis_index("core")]).astype(jnp.int32)
-    table = jnp.stack([row_of, cost_of, jnp.pad(facts, (0, ROWS - 5))]).astype(jnp.int32)
-
     def halves(a, b, axis):
         first = jnp.where(is_physics, b, a)
         second = jnp.where(is_physics, a, b)
@@ -449,14 +525,28 @@
 
     field, own, send = vmem_call(
         transport_kernel,
-        [shape((FLAT, COLS), f32), shape((FPAD, MINE), bf16), shape((2 * ROWS, PACK, COLS), bf16)],
-        [pltpu.VMEM((FLAT, COLS), f32), pltpu.VMEM((128, COLS), f32)],
-        2,
-        6,
+        [
+            shape((ROWS, FPAD, COLS), f32),
+            shape((ROWS // 2, FPAD, COLS), bf16),
+            shape((2 * ROWS, PACK, COLS), bf16),
+        ],
+        [
+            pltpu.VMEM((GROUPS * 128, COLS), f32),
+            pltpu.VMEM((ROWS, FPAD, COLS), f32),
+            pltpu.VMEM((128, COLS), f32),
+            pltpu.VMEM((ROWS, 8, COLS), f32),
+            pltpu.VMEM((2 * FPAD, COLS), f32),
+            pltpu.VMEM((ROWS // 2, FPAD, COLS), bf16),
+            pltpu.VMEM((ROWS, PACK, COLS), bf16),
+            pltpu.SemaphoreType.DMA((1 + ROWS + ROWS // 2 + 2 * (len(X_CUTS) - 1),)),
+        ],
+        "shvvvvv",
         10**8,
         6 * 10**6,
         "transport",
-    )(table, flags, stored, east_courant, north_courant, from_west, from_south, from_corner)
+        ALL_VMEM,
+        "hhh",
+    )(table, stored, east_courant, north_courant, from_west, from_south, from_corner)
     recv = lax.all_to_all(send, LON + ("grp",), 0, 0, tiled=True)
     inputs, hidden, g_two, slope, own_out, send_back, vec = vmem_call(
         forward_kernel,
@@ -470,22 +560,22 @@
             shape((16, HID), f32),
         ],
         [],
-        1,
-        6,
+        "svvvvvv",
         2 * MINE * HID * (4 * FPAD + HID),
         8 * 10**6,
         "forward",
+        16,
     )(table, own, recv, w_one, w_mid.T, w_three, gain)
     back = lax.all_to_all(send_back, LON + ("grp",), 0, 0, tiled=True)
     keep, other = vmem_call(
         backward_kernel,
         [shape((OWNERS // 2, PIECE, 128), f32)] * 2,
         [pltpu.VMEM((HID, MINE), bf16), pltpu.VMEM((2 * FPAD, HID), f32)],
-        1,
-        6,
+        "svvvvvv",
         2 * MINE * HID * (2 * FPAD + 2 * HID),
         6 * 10**6,
         "backward",
+        16,
     )(table, inputs, hidden, g_two, slope, w_mid, vec)
 
     grad = keep + swap(other, "core")
@@ -494,7 +584,7 @@
         at = lax.axis_index(axis)
         other = lax.dynamic_slice_in_dim(grad, (1 - at) * pieces, pieces)
         keep = lax.dynamic_slice_in_dim(grad, at * pieces, pieces)
-        grad = keep + swap(other, axis)
+        grad = keep + swap(other.astype(bf16), axis).astype(f32)
     grad, back = lax.optimization_barrier((grad, back))
     pieces_b = jnp.pad(grad[:, A_PIECE:], ((0, 0), (0, A_PIECE - B_PIECE), (0, 0)))
     pieces = jnp.stack([grad[:, :A_PIECE], pieces_b], axis=1).reshape(-1, A_PIECE, 128)
@@ -507,13 +597,13 @@
     new = vmem_call(
         final_kernel,
         [shape((FLAT, COLS), f32)],
-        [],
-        2,
-        3,
+        [pltpu.VMEM((ROWS, FPAD, COLS), f32)],
+        "svvv",
         10**7,
         6 * 10**6,
         "final",
-    )(table, flags, field, own_out, back)[0]
+        16,
+    )(table, field, own_out, back)[0]
     for axis in ("x", "core"):
         other = swap(piece, axis)
         if axis == "x":

time: 145 us -> 138 us (0.952)
  local copies, waits for them, and re-layouts: 11.1 us -> 5.56 us
  waiting for transfers between devices: 32.2 us -> 28.8 us
  starting transfers between devices: 32 us -> 35 us
  other arithmetic: 5.96 us -> 4.31 us
  Pallas kernels: 21.6 us -> 23.2 us
    ppermute x5, waiting for transfers between devices: 16.1 us -> 11.4 us  [swap(): return lax.ppermute(value, axis, [(0, 1), (1, 0)])]
    unnamed x34 -> x28, local copies, waits for them, and re-layouts: 7.51 us -> 2.77 us
    ppermute x5, starting transfers between devices: 9.85 us -> 12.8 us  [swap(): return lax.ppermute(value, axis, [(0, 1), (1, 0)])]
    all_to_all x1, blocking collectives: 18.2 us -> 15.3 us  [on_device(): lax.all_to_all(jnp.broadcast_to(piece[None], (members,) + piece.shape), r...]
    all_to_all x1, blocking collectives: 22 us -> 24.1 us  [on_device(): lax.all_to_all(pieces, ('za', 'y', 'x', 'grp'), 0, 0, tiled=True)]
    pallas_call x1, Pallas kernels: 1.5 us -> 3.02 us  [on_device(): vmem_call(rim_kernel, [shape((128, COLS), bf16), shape((128, COLS), bf16)...]
  transfers between devices with their start and end apart: 10 -> 10, of which waited for: 6 -> 7; matrix products, arithmetic and copies ran while one was open for 3% -> 1% of each run, Pallas kernels for 3% -> 3%
where the time goes in v3:
time: 138 us; the launch traced here: 137 us
  blocking collectives  39.5 us (29%)
  starting transfers between devices  35 us (25%)
  waiting for transfers between devices  28.8 us (21%)
  Pallas kernels  23.2 us (17%)
  local copies, waits for them, and re-layouts  5.56 us (4%)
  other arithmetic  4.31 us (3%)
    all_to_all x1, blocking collectives, on_device(): lax.all_to_all(pieces, ('za', 'y', 'x', 'grp'), 0, 0, tiled=True)  24.1 us
    all_to_all x1, waiting for transfers between devices, on_device(): recv = lax.all_to_all(send, LON + ('grp',), 0, 0, tiled=True)  15.6 us
    all_to_all x1, blocking collectives, on_device(): lax.all_to_all(jnp.broadcast_to(piece[None], (members,) + piece.shape), r...  15.3 us
    ppermute x5, starting transfers between devices, swap(): return lax.ppermute(value, axis, [(0, 1), (1, 0)])  12.8 us
    ppermute x5, waiting for transfers between devices, swap(): return lax.ppermute(value, axis, [(0, 1), (1, 0)])  11.4 us
    all_to_all x1, starting transfers between devices, on_device(): recv = lax.all_to_all(send, LON + ('grp',), 0, 0, tiled=True)  8.25 us
    pallas_call x1, Pallas kernels, on_device(): vmem_call(transport_kernel, [shape((ROWS, FPAD, COLS), f32), shape((ROWS...  7.8 us
    pallas_call x1, Pallas kernels, on_device(): vmem_call(forward_kernel, [shape((2 * FPAD, MINE), bf16), shape((HID, MIN...  5.76 us
  transfers between devices with their start and end apart: 10, of which 7 were waited for; matrix products, arithmetic and copies ran while one was open for 1% of the time, Pallas kernels for 3%

profile of v3, /device:TPU:1, one launch (start us, length us, event | category | flops | bytes accessed | tf_op | source)
XLA Modules:
  0.0 137.4 jit_solution(7590388720502197341)
XLA Ops:
  0.6 3.0 %rim.1 = (bf16[128,128]{1,0:T(8,128)(2,1)}, bf16[128,128]{1,0:T(8,128)(2,1)}, bf16[576,128]{1,0:T(8,128)(2,1)}, s32[16,128]{1,0:T(8,128)}) custom-call(f32[4448,128]{1,0:T(8,128)} %bitcast.21, f32[16,128]{1,0:T(8,128)} %east_ref.1, f32[16,128]{1,0:T(8,128)} %north_ref.1, s32[8,16,16]{2,1,0:T(8,128)} %assign_hbm.1, s32[8,16,16]{2,1,0:T(8,128)} %cost_hbm.1), custom_call_target="tpu_custom_call" | custom-call | flops 100000000 | bytes 3000000 | tf_op jit(solution)/shard_map/rim/pallas_call | solution.py:483
  3.7 4.4 %collective-permute-start.1 = (bf16[576,128]{1,0:T(8,128)(2,1)}, bf16[576,128]{1,0:T(8,128)(2,1)S(1)}, u32[]{:S(2)}, u32[]{:S(2)}) collective-permute-start(bf16[576,128]{1,0:T(8,128)(2,1)} %get-tuple-element.24), channel_id=1, source_target_pairs={{0,32},{32,64},{64,96},{96,128},{128,160},{160,192},{192,224},{1,3... | collective-permute-start | bytes 442376 | tf_op jit(solution)/shard_map/ppermute | solution.py:506
  8.0 2.1 %collective-permute-start = (bf16[128,128]{1,0:T(8,128)(2,1)}, bf16[128,128]{1,0:T(8,128)(2,1)S(1)}, u32[]{:S(2)}, u32[]{:S(2)}) collective-permute-start(bf16[128,128]{1,0:T(8,128)(2,1)} %get-tuple-element.23), channel_id=1, source_target_pairs={{0,2},{2,4},{4,6},{6,8},{8,10},{10,12},{12,14},{14,16},{16,18},{18... | collective-permute-start | bytes 98312 | tf_op jit(solution)/shard_map/ppermute | solution.py:505
  10.2 3.3 %collective-permute-start.2 = (bf16[128,128]{1,0:T(8,128)(2,1)}, bf16[128,128]{1,0:T(8,128)(2,1)S(1)}, u32[]{:S(2)}, u32[]{:S(2)}) collective-permute-start(bf16[128,128]{1,0:T(8,128)(2,1)} %get-tuple-element.25), channel_id=1, source_target_pairs={{0,34},{2,36},{4,38},{6,40},{8,42},{10,44},{12,46},{14,48},{16,50}... | collective-permute-start | bytes 98312 | tf_op jit(solution)/shard_map/ppermute | solution.py:507
  13.5 1.3 collective-permute-done.2.corner_ref
  14.8 0.6 copy-done.10
  15.4 7.8 %transport.1 = (f32[16,288,128]{2,1,0:T(8,128)}, bf16[8,288,128]{2,1,0:T(8,128)(2,1)}, bf16[32,144,128]{2,1,0:T(8,128)(2,1)}) custom-call(s32[16,128]{1,0:T(8,128)} %get-tuple-element.22.table_ref, f32[4448,128]{1,0:T(8,128)} %bitcast.22, f32[16,128]{1,0:T(8,128)} %east_ref.1, f32[16,128]{1,0:T(8,128)} %north_ref.1, bf16[128,128]{1,0:T(8,128)(2,1)} %copy-done.9, ...), custom_call_target="tpu_custom_call" | custom-call | flops 100000000 | bytes 6000000 | tf_op jit(solution)/shard_map/transport/pallas_call | solution.py:526
  23.3 8.2 %all-to-all-start = ((bf16[32,144,128]{2,1,0:T(8,128)(2,1)}), bf16[32,144,128]{2,1,0:T(8,128)(2,1)S(1)}, u32[]{:S(2)}, u32[]{:S(2)}) async-start(bf16[32,144,128]{2,1,0:T(8,128)(2,1)} %get-tuple-element.27), calls=%async_computation | async-start | bytes 2359296 | tf_op jit(solution)/shard_map/all_to_all | solution.py:550
  32.1 0.4 copy-done.6
  33.2 15.6 %all-to-all-done.recv_ref = bf16[32,144,128]{2,1,0:T(8,128)(2,1)S(1)} async-done(((bf16[32,144,128]{2,1,0:T(8,128)(2,1)}), bf16[32,144,128]{2,1,0:T(8,128)(2,1)S(1)}, u32[]{:S(2)}, u32[]{:S(2)}) %all-to-all-start) | async-done | bytes 1179680 | tf_op jit(solution)/shard_map/all_to_all | solution.py:550
  48.8 5.8 %forward.1 = (bf16[576,1024]{1,0:T(8,128)(2,1)S(1)}, bf16[384,1024]{1,0:T(8,128)(2,1)S(1)}, bf16[384,1024]{1,0:T(8,128)(2,1)S(1)}, f32[384,1024]{1,0:T(8,128)S(1...) custom-call(s32[16,128]{1,0:T(8,128)S(1)} %copy-done.4, ...), custom_call_target="tpu_custom_call" | custom-call | flops 1207959552 | bytes 8000000 | tf_op jit(solution)/shard_map/forward/pallas_call | solution.py:551
  54.6 2.4 %backward.1 = (f32[64,24,128]{2,1,0:T(8,128)S(1)}, f32[64,24,128]{2,1,0:T(8,128)S(1)}) custom-call(s32[16,128]{1,0:T(8,128)S(1)} %copy-done.4, bf16[576,1024]{1,0:T(8,128)(2,1)S(1)} %get-tuple-element.28.inputs_ref, bf16[384,1024]{1,0:T(8,128)(2,1)S(1)} %get-tuple-element.29.hidden_ref, bf16[384,1024]{1,0:T(8,128)(2,1)S(1)} %get-tuple-element.30.g_two_ref, ...), custom_call_target="tpu_custom_call" | custom-call | flops 1056964608 | bytes 6000000 | tf_op jit(solution)/shard_map/backward/pallas_call | solution.py:570
  57.0 1.0 collective-permute-start.3
  58.0 4.2 %all-to-all-start.1 = ((bf16[32,144,128]{2,1,0:T(8,128)(2,1)}), bf16[32,144,128]{2,1,0:T(8,128)(2,1)S(1)}, u32[]{:S(2)}, u32[]{:S(2)}) async-start(bf16[32,144,128]{2,1,0:T(8,128)(2,1)} %get-tuple-element.35), calls=%async_computation.1 | async-start | bytes 2359296 | tf_op jit(solution)/shard_map/all_to_all | solution.py:569
  62.3 2.3 %collective-permute-start.4 = (bf16[32,24,128]{2,1,0:T(8,128)(2,1)S(1)}, bf16[32,24,128]{2,1,0:T(8,128)(2,1)S(1)}, u32[]{:S(2)}, u32[]{:S(2)}) collective-permute-start(bf16[32,24,128]{2,1,0:T(8,128)(2,1)S(1)} %dynamic-slice_convert_fusion), channel_id=1, source_target_pairs={{0,32},{32,0},{1,33},{33,1},{2,34},{34,2},{3,35},{35,3},{4,36},{36... | collective-permute-start | bytes 589832 | tf_op jit(solution)/shard_map/ppermute | solution.py:473
  64.5 5.1 %collective-permute-done.4 = bf16[32,24,128]{2,1,0:T(8,128)(2,1)S(1)} collective-permute-done((bf16[32,24,128]{2,1,0:T(8,128)(2,1)S(1)}, bf16[32,24,128]{2,1,0:T(8,128)(2,1)S(1)}, u32[]{:S(2)}, u32[]{:S(2)}) %collective-permute-start.4) | collective-permute-done | bytes 196640 | tf_op jit(solution)/shard_map/ppermute | solution.py:473
  69.7 4.5 %collective-permute-start.5 = (bf16[16,24,128]{2,1,0:T(8,128)(2,1)S(1)}, bf16[16,24,128]{2,1,0:T(8,128)(2,1)S(1)}, u32[]{:S(2)}, u32[]{:S(2)}) collective-permute-start(bf16[16,24,128]{2,1,0:T(8,128)(2,1)S(1)} %dynamic-slice_convert_fusion.1), channel_id=1, source_target_pairs={{0,64},{64,0},{1,65},{65,1},{2,66},{66,2},{3,67},{67,3},{4,68},{68... | collective-permute-start | bytes 294920 | tf_op jit(solution)/shard_map/ppermute | solution.py:473
  74.2 4.6 %collective-permute-done.5 = bf16[16,24,128]{2,1,0:T(8,128)(2,1)S(1)} collective-permute-done((bf16[16,24,128]{2,1,0:T(8,128)(2,1)S(1)}, bf16[16,24,128]{2,1,0:T(8,128)(2,1)S(1)}, u32[]{:S(2)}, u32[]{:S(2)}) %collective-permute-start.5) | collective-permute-done | bytes 98336 | tf_op jit(solution)/shard_map/ppermute | solution.py:473
  78.8 0.6 all-to-all-done.1.recv_ref
  79.5 24.1 %all_to_all.20 = f32[32,16,128]{2,1,0:T(8,128)} all-to-all(f32[32,16,128]{2,1,0:T(8,128)S(1)} %bitcast.30), channel_id=1, replica_groups=mesh['za'=2,'zb'=2,'zc'=2,'y'=4,'x'=2,'core'=2,'grp'=2] {'za','y','x','g..., dimensions={0} | all-to-all | bytes 524288 | tf_op jit(solution)/shard_map/all_to_all | solution.py:591
  103.6 1.0 reduce_sum.19
  104.7 15.3 %all_to_all.21 = f32[32,16,128]{2,1,0:T(8,128)} all-to-all(f32[32,16,128]{2,1,0:T(8,128)S(1)} %broadcast_in_dim.5), channel_id=1, replica_groups=mesh['za'=2,'zb'=2,'zc'=2,'y'=4,'x'=2,'core'=2,'grp'=2] {'za','zb','zc',..., dimensions={0} | all-to-all | bytes 524288 | tf_op jit(solution)/shard_map/all_to_all | solution.py:594
  120.1 1.1 copy-done.3
  121.1 4.3 %final.1 = f32[4448,128]{1,0:T(8,128)} custom-call(s32[16,128]{1,0:T(8,128)S(1)} %copy-done.4, f32[16,288,128]{2,1,0:T(8,128)S(1)} %copy-done, bf16[288,1024]{1,0:T(8,128)(2,1)S(1)} %copy-done.3, bf16[32,144,128]{2,1,0:T(8,128)(2,1)S(1)} %all-to-all-done.1.recv_ref), custom_call_target="tpu_custom_call" | custom-call | flops 10000000 | bytes 6000000 | tf_op jit(solution)/shard_map/final/pallas_call | solution.py:597
  125.5 1.1 broadcast_select_fusion.7
  126.7 5.0 %collective-permute-start.7 = (f32[64,16,128]{2,1,0:T(8,128)S(1)}, f32[64,16,128]{2,1,0:T(8,128)S(1)}, u32[]{:S(2)}, u32[]{:S(2)}) collective-permute-start(f32[64,16,128]{2,1,0:T(8,128)S(1)} %pad_maximum_fusion.2), channel_id=1, source_target_pairs={{0,2},{2,0},{1,3},{3,1},{4,6},{6,4},{5,7},{7,5},{8,10},{10,8},{9,1... | collective-permute-start | bytes 1572872 | tf_op jit(solution)/shard_map/ppermute | solution.py:473
  131.7 1.5 %collective-permute-done.7 = f32[64,16,128]{2,1,0:T(8,128)S(1)} collective-permute-done((f32[64,16,128]{2,1,0:T(8,128)S(1)}, f32[64,16,128]{2,1,0:T(8,128)S(1)}, u32[]{:S(2)}, u32[]{:S(2)}) %collective-permute-start.7) | collective-permute-done | bytes 524320 | tf_op jit(solution)/shard_map/ppermute | solution.py:473
  133.6 0.3 copy.22
  134.6 0.6 mul.46
  135.4 0.5 copy.24
  135.9 0.5 reshape.48
  136.4 1.1 maximum_select_fusion
  (60 shorter events, 2.9 us)
Async XLA Ops:
  3.7 11.1 %collective-permute-start.1 = (bf16[576,128]{1,0:T(8,128)(2,1)}, bf16[576,128]{1,0:T(8,128)(2,1)S(1)}, u32[]{:S(2)}, u32[]{:S(2)}) collective-permute-start(bf16[576,128]{1,0:T(8,128)(2,1)} %get-tuple-element.24), channel_id=1, source_target_pairs={{0,32},{32,64},{64,96},{96,128},{128,160},{160,192},{192,224},{1,3... | collective-permute-start | bytes 442376 | tf_op jit(solution)/shard_map/ppermute | solution.py:506
  8.0 5.4 %collective-permute-start = (bf16[128,128]{1,0:T(8,128)(2,1)}, bf16[128,128]{1,0:T(8,128)(2,1)S(1)}, u32[]{:S(2)}, u32[]{:S(2)}) collective-permute-start(bf16[128,128]{1,0:T(8,128)(2,1)} %get-tuple-element.23), channel_id=1, source_target_pairs={{0,2},{2,4},{4,6},{6,8},{8,10},{10,12},{12,14},{14,16},{16,18},{18... | collective-permute-start | bytes 98312 | tf_op jit(solution)/shard_map/ppermute | solution.py:505
  10.2 4.6 %collective-permute-start.2 = (bf16[128,128]{1,0:T(8,128)(2,1)}, bf16[128,128]{1,0:T(8,128)(2,1)S(1)}, u32[]{:S(2)}, u32[]{:S(2)}) collective-permute-start(bf16[128,128]{1,0:T(8,128)(2,1)} %get-tuple-element.25), channel_id=1, source_target_pairs={{0,34},{2,36},{4,38},{6,40},{8,42},{10,44},{12,46},{14,48},{16,50}... | collective-permute-start | bytes 98312 | tf_op jit(solution)/shard_map/ppermute | solution.py:507
  13.5 1.3 copy-start.9
  14.8 0.6 copy-start.10
  14.8 0.7 copy-start.8
  23.2 8.3 %copy-start.7 = (bf16[556,384]{1,0:T(8,128)(2,1)S(1)}, bf16[556,384]{1,0:T(8,128)(2,1)}, u32[]{:S(2)}) copy-start(bf16[556,384]{1,0:T(8,128)(2,1)} %param.14) | copy-start | bytes 1281028
  23.3 8.6 %copy-start.1 = (bf16[384,384]{1,0:T(8,128)(2,1)S(1)}, bf16[384,384]{1,0:T(8,128)(2,1)}, u32[]{:S(2)}) copy-start(bf16[384,384]{1,0:T(8,128)(2,1)} %w_mid_ref.1) | copy-start | bytes 884740
  23.3 25.5 %all-to-all-start = ((bf16[32,144,128]{2,1,0:T(8,128)(2,1)}), bf16[32,144,128]{2,1,0:T(8,128)(2,1)S(1)}, u32[]{:S(2)}, u32[]{:S(2)}) async-start(bf16[32,144,128]{2,1,0:T(8,128)(2,1)} %get-tuple-element.27), calls=%async_computation | async-start | bytes 2359296 | tf_op jit(solution)/shard_map/all_to_all | solution.py:550
  31.5 1.0 copy-start.6
  31.5 1.0 copy-start.11
  32.9 15.9 %copy-start.4 = (s32[16,128]{1,0:T(8,128)S(1)}, s32[16,128]{1,0:T(8,128)}, u32[]{:S(2)}) copy-start(s32[16,128]{1,0:T(8,128)} %get-tuple-element.22.table_ref) | copy-start | bytes 24580
  32.9 15.9 %copy-start.5 = (bf16[8,288,128]{2,1,0:T(8,128)(2,1)S(1)}, bf16[8,288,128]{2,1,0:T(8,128)(2,1)}, u32[]{:S(2)}) copy-start(bf16[8,288,128]{2,1,0:T(8,128)(2,1)} %get-tuple-element.26.own_ref) | copy-start | bytes 1769476
  54.6 2.4 %copy-start.2 = (bf16[288,1024]{1,0:T(8,128)(2,1)}, bf16[288,1024]{1,0:T(8,128)(2,1)S(1)}, u32[]{:S(2)}) copy-start(bf16[288,1024]{1,0:T(8,128)(2,1)S(1)} %get-tuple-element.38.own_ref) | copy-start | bytes 1769476
  57.0 5.2 %collective-permute-start.3 = (f32[64,24,128]{2,1,0:T(8,128)S(1)}, f32[64,24,128]{2,1,0:T(8,128)S(1)}, u32[]{:S(2)}, u32[]{:S(2)}) collective-permute-start(f32[64,24,128]{2,1,0:T(8,128)S(1)} %get-tuple-element.34), channel_id=1, source_target_pairs={{0,2},{2,0},{1,3},{3,1},{4,6},{6,4},{5,7},{7,5},{8,10},{10,8},{9,1... | collective-permute-start | bytes 2359304 | tf_op jit(solution)/shard_map/ppermute | solution.py:473
  58.0 21.4 %all-to-all-start.1 = ((bf16[32,144,128]{2,1,0:T(8,128)(2,1)}), bf16[32,144,128]{2,1,0:T(8,128)(2,1)S(1)}, u32[]{:S(2)}, u32[]{:S(2)}) async-start(bf16[32,144,128]{2,1,0:T(8,128)(2,1)} %get-tuple-element.35), calls=%async_computation.1 | async-start | bytes 2359296 | tf_op jit(solution)/shard_map/all_to_all | solution.py:569
  62.3 7.4 %collective-permute-start.4 = (bf16[32,24,128]{2,1,0:T(8,128)(2,1)S(1)}, bf16[32,24,128]{2,1,0:T(8,128)(2,1)S(1)}, u32[]{:S(2)}, u32[]{:S(2)}) collective-permute-start(bf16[32,24,128]{2,1,0:T(8,128)(2,1)S(1)} %dynamic-slice_convert_fusion), channel_id=1, source_target_pairs={{0,32},{32,0},{1,33},{33,1},{2,34},{34,2},{3,35},{35,3},{4,36},{36... | collective-permute-start | bytes 589832 | tf_op jit(solution)/shard_map/ppermute | solution.py:473
  69.7 9.0 %collective-permute-start.5 = (bf16[16,24,128]{2,1,0:T(8,128)(2,1)S(1)}, bf16[16,24,128]{2,1,0:T(8,128)(2,1)S(1)}, u32[]{:S(2)}, u32[]{:S(2)}) collective-permute-start(bf16[16,24,128]{2,1,0:T(8,128)(2,1)S(1)} %dynamic-slice_convert_fusion.1), channel_id=1, source_target_pairs={{0,64},{64,0},{1,65},{65,1},{2,66},{66,2},{3,67},{67,3},{4,68},{68... | collective-permute-start | bytes 294920 | tf_op jit(solution)/shard_map/ppermute | solution.py:473
  79.4 40.7 %copy-start = (f32[16,288,128]{2,1,0:T(8,128)S(1)}, f32[16,288,128]{2,1,0:T(8,128)}, u32[]{:S(2)}) copy-start(f32[16,288,128]{2,1,0:T(8,128)} %get-tuple-element.37.field_ref) | copy-start | bytes 7077892
  120.0 5.5 %collective-permute-start.6 = (f32[32,16,128]{2,1,0:T(8,128)}, f32[32,16,128]{2,1,0:T(8,128)}, u32[]{:S(2)}, u32[]{:S(2)}) collective-permute-start(f32[32,16,128]{2,1,0:T(8,128)} %all_to_all.21), channel_id=1, source_target_pairs={{0,4},{4,0},{1,5},{5,1},{2,6},{6,2},{3,7},{7,3},{8,12},{12,8},{9,1... | collective-permute-start | bytes 786440 | tf_op jit(solution)/shard_map/ppermute | solution.py:473
  120.1 1.1 copy-start.3
  126.7 6.5 %collective-permute-start.7 = (f32[64,16,128]{2,1,0:T(8,128)S(1)}, f32[64,16,128]{2,1,0:T(8,128)S(1)}, u32[]{:S(2)}, u32[]{:S(2)}) collective-permute-start(f32[64,16,128]{2,1,0:T(8,128)S(1)} %pad_maximum_fusion.2), channel_id=1, source_target_pairs={{0,2},{2,0},{1,3},{3,1},{4,6},{6,4},{5,7},{7,5},{8,10},{10,8},{9,1... | collective-permute-start | bytes 1572872 | tf_op jit(solution)/shard_map/ppermute | solution.py:473
  133.6 0.7 copy-start.12

commit v4 on v3

--- a/solution.py
+++ b/solution.py
@@ -131,7 +131,7 @@
     table_ref[...] = block_table(
         grp == 1,
         lon,
-        (not_top, 1 - grp, grp * (COLS // 2), core),
+        (not_top, 1 - grp, grp * (COLS // 2), core, lax.axis_index("x")),
         assign_ref[...],
         cost_ref[...],
         assign_ref[pl.ds(lon, 1), :],
@@ -202,7 +202,6 @@
     east, north, keep, west, south = coefficients(
         east_ref[...], north_ref[...], to_slot.astype(f32), table_ref[0, 2].astype(f32)
     )
-    west = jnp.where(lane_ids(west.shape) == 0, 1.0, west)
     keep, west, south = (value.reshape(ROWS, 1, COLS) for value in (keep, west, south))
     lane = lane_ids((128, COLS))
     rim = rim_ref[...].astype(f32)
@@ -214,22 +213,29 @@
     inflow_ref[...] = rim + jnp.where(fix, lacked, 0.0)
     for k in range(ROWS):
         rims_ref[k] = inflow_ref[pl.ds(k, 8, stride=ROWS), :]
-    last = lane_ids((ROWS, 8, COLS)) == COLS - 1
-
-    def transported(q, shift, from_south):
-        inflow = pltpu.roll(rims_ref[...], shift, 2)
-        shifted = pltpu.roll(jnp.where(last, inflow, q), 1, 2)
+    both = rims_ref[...]
+    one = pltpu.roll(both, COLS - 1, 2)
+    below = jnp.concatenate([one[ROWS - 1 :], one[: ROWS - 1]], axis=0)
+    rims_ref[...] = jnp.where(
+        lane_ids((ROWS, 8, COLS)) % 2 == 1,
+        west[:, :, 1:2] * both,
+        both + keep[:, :, 0:1] * one + south[:, :, 0:1] * below,
+    )
+    reached = lane_ids((ROWS, 8, COLS)) < 2
+
+    def transported(q, from_south):
         under = jnp.concatenate([q[ROWS - 1 :], q[: ROWS - 1]], axis=0)
-        after = keep * q + west * shifted + south * under
+        after = keep * q + west * pltpu.roll(q, 1, 2) + south * under
         return jnp.concatenate([after[:1] + from_south[None], after[1:]], axis=0)
 
     def group(g, carry):
-        rows = x_ref[pl.ds(pl.multiple_of(g * 128, 128), 128), :].reshape(8, ROWS, COLS)
         features = pl.ds(pl.multiple_of(g * 8, 8), 8)
-        q = jnp.swapaxes(rows, 0, 1)
-        q = transported(q, COLS - 2 - 2 * g, south32_ref[features, :])
         over = pl.ds(pl.multiple_of(FPAD + g * 8, 8), 8)
-        field_ref[:, features, :] = transported(q, COLS - 1 - 2 * g, south32_ref[over, :])
+        q = jnp.stack([x_ref[pl.ds(g * 128 + k, 8, stride=ROWS), :] for k in range(ROWS)])
+        q = transported(q, south32_ref[features, :])
+        q = transported(q, south32_ref[over, :])
+        inflow = pltpu.roll(rims_ref[...], lax.rem(COLS - 2 * g, COLS), 2)
+        field_ref[:, features, :] = q + jnp.where(reached, inflow, 0.0)
         return carry
 
     field_out = []
@@ -296,69 +302,66 @@
     gain = gain_ref[...]
     loss_norm = 1.0 / math.sqrt(ROWS * 8 * COLS * ROWS)
     energy_norm = 1.0 / math.sqrt(OUT)
-    tile = 2 * COLS
+    tile = MINE
     vec_ref[...] = jnp.zeros(vec_ref.shape, f32)
 
-    for t in range(MINE // tile):
-        lanes = slice(t * tile, (t + 1) * tile)
-        live_parts = []
-        for g in range(2):
-            i = 2 * t + g
-            group = slice(i * COLS, (i + 1) * COLS)
-            first = recv_ref[4 * i + from_slot].astype(f32)
-            second = recv_ref[4 * i + 2 + from_slot].astype(f32)
-            inputs_ref[0:FPAD, group] = own_ref[i]
-            inputs_ref[FPAD : FPAD + PACK, group] = jnp.where(
-                low, first, swap_halves(second)
-            ).astype(bf16)
-            inputs_ref[FPAD + PACK :, group] = jnp.where(
-                low, swap_halves(first), second
-            ).astype(bf16)
-            lane = lane_ids((1, COLS))
-            column = lane % (COLS // 2) + offset
-            cost = jnp.where(lane < COLS // 2, table_ref[2 * i, 1], table_ref[2 * i + 1, 1])
-            live_parts.append(jnp.where(column < cost, 1.0, 0.0))
-        live = jnp.concatenate(live_parts, axis=1)
-        inputs = inputs_ref[:, lanes]
-        pre_one = jnp.dot(w_one_ref[...], inputs, preferred_element_type=f32)
-        sig = sigmoid(pre_one)
-        silu = pre_one * sig
-        hidden_one = silu.astype(bf16)
-        slope_ref[:, lanes] = sig + silu * (1.0 - sig)
-        hidden_ref[:, lanes] = hidden_one
-        pre_two = jnp.dot(w_two_ref[...], hidden_one, preferred_element_type=f32)
-        sig = sigmoid(pre_two)
-        silu = pre_two * sig
-        hidden_two = silu.astype(bf16)
-        slope_two = sig + silu * (1.0 - sig)
-        result = jnp.dot(w_three_ref[...], hidden_two, preferred_element_type=f32).astype(bf16)
-        own_out_ref[:, lanes] = result[:FPAD]
-        to_send = result[FPAD:].astype(f32)
-        for g in range(2):
-            i = 2 * t + g
-            part = to_send[:, g * COLS : (g + 1) * COLS]
-            other = swap_halves(part)
-            zeros = jnp.zeros((PACK, COLS), bf16)
-            send_ref[4 * i + from_slot] = jnp.where(low, part[:PACK], other[PACK:]).astype(bf16)
-            send_ref[4 * i + 2 + from_slot] = jnp.where(
-                low, other[:PACK], part[PACK:]
-            ).astype(bf16)
-            send_ref[4 * i + 1 - from_slot] = zeros
-            send_ref[4 * i + 3 - from_slot] = zeros
-        energy = jnp.sum(gain * hidden_two.astype(f32), axis=0, keepdims=True) * energy_norm
-        weight = live * energy * loss_norm
-        g_two_ref[:, lanes] = (gain * weight * slope_two).astype(bf16)
-        high = weight.astype(bf16)
-        left = weight - high.astype(f32)
-        mid = left.astype(bf16)
-        low_part = (left - mid.astype(f32)).astype(bf16)
-        rows = row_ids((16, tile))
-        stacked = jnp.where(
-            rows == 0,
-            high.astype(f32),
-            jnp.where(rows == 1, mid.astype(f32), jnp.where(rows == 2, low_part.astype(f32), 0.0)),
+    lanes = slice(0, MINE)
+    live_parts = []
+    for i in range(ROWS // 2):
+        group = slice(i * COLS, (i + 1) * COLS)
+        first = recv_ref[4 * i + from_slot].astype(f32)
+        second = recv_ref[4 * i + 2 + from_slot].astype(f32)
+        inputs_ref[0:FPAD, group] = own_ref[i]
+        inputs_ref[FPAD : FPAD + PACK, group] = jnp.where(
+            low, first, swap_halves(second)
         ).astype(bf16)
-        vec_ref[...] += lax.dot_general(stacked, hidden_two, NT, preferred_element_type=f32)
+        inputs_ref[FPAD + PACK :, group] = jnp.where(
+            low, swap_halves(first), second
+        ).astype(bf16)
+        lane = lane_ids((1, COLS))
+        column = lane % (COLS // 2) + offset
+        cost = jnp.where(lane < COLS // 2, table_ref[2 * i, 1], table_ref[2 * i + 1, 1])
+        live_parts.append(jnp.where(column < cost, 1.0, 0.0))
+    live = jnp.concatenate(live_parts, axis=1)
+    inputs = inputs_ref[:, lanes]
+    pre_one = jnp.dot(w_one_ref[...], inputs, preferred_element_type=f32)
+    sig = sigmoid(pre_one)
+    silu = pre_one * sig
+    hidden_one = silu.astype(bf16)
+    slope_ref[:, lanes] = sig + silu * (1.0 - sig)
+    hidden_ref[:, lanes] = hidden_one
+    pre_two = jnp.dot(w_two_ref[...], hidden_one, preferred_element_type=f32)
+    sig = sigmoid(pre_two)
+    silu = pre_two * sig
+    hidden_two = silu.astype(bf16)
+    slope_two = sig + silu * (1.0 - sig)
+    result = jnp.dot(w_three_ref[...], hidden_two, preferred_element_type=f32).astype(bf16)
+    own_out_ref[:, lanes] = result[:FPAD]
+    to_send = result[FPAD:].astype(f32)
+    for i in range(ROWS // 2):
+        part = to_send[:, i * COLS : (i + 1) * COLS]
+        other = swap_halves(part)
+        zeros = jnp.zeros((PACK, COLS), bf16)
+        send_ref[4 * i + from_slot] = jnp.where(low, part[:PACK], other[PACK:]).astype(bf16)
+        send_ref[4 * i + 2 + from_slot] = jnp.where(
+            low, other[:PACK], part[PACK:]
+        ).astype(bf16)
+        send_ref[4 * i + 1 - from_slot] = zeros
+        send_ref[4 * i + 3 - from_slot] = zeros
+    energy = jnp.sum(gain * hidden_two.astype(f32), axis=0, keepdims=True) * energy_norm
+    weight = live * energy * loss_norm
+    g_two_ref[:, lanes] = (gain * weight * slope_two).astype(bf16)
+    high = weight.astype(bf16)
+    left = weight - high.astype(f32)
+    mid = left.astype(bf16)
+    low_part = (left - mid.astype(f32)).astype(bf16)
+    rows = row_ids((16, tile))
+    stacked = jnp.where(
+        rows == 0,
+        high.astype(f32),
+        jnp.where(rows == 1, mid.astype(f32), jnp.where(rows == 2, low_part.astype(f32), 0.0)),
+    ).astype(bf16)
+    vec_ref[...] += lax.dot_general(stacked, hidden_two, NT, preferred_element_type=f32)
 
 
 def place(owner):
@@ -463,6 +466,64 @@
     lax.fori_loop(0, full, group, 0, unroll=2)
     value = jnp.swapaxes(new_ref[:, full * 8 : full * 8 + 8, :], 0, 1).reshape(128, COLS)
     out_ref[full * 128 :, :] = value[: rest * ROWS]
+
+
+MID_A = 98
+PERIOD = 23
+OUT_AT = 3 * (HID - MID_A)
+
+
+def gather_kernel(
+    table_ref, mine_ref, x_other_ref, core_other_ref, far_ref, energy_ref, out_ref, all_ref, vec_ref
+):
+    is_dyn = table_ref[0, 3] == 1
+    core = table_ref[0, 5]
+    x = table_ref[0, 6]
+    all_ref[2 * core + x] = mine_ref[...]
+    all_ref[2 * core + 1 - x] = x_other_ref[...]
+    all_ref[2 * (1 - core) + x] = core_other_ref[...]
+    all_ref[2 * (1 - core) + 1 - x] = far_ref[...]
+
+    def rows_at(row, count):
+        quarter = OWNERS // 4 * A_PIECE
+        parts = []
+        while count:
+            here = min(count, quarter - row % quarter)
+            parts.append(all_ref[row // quarter, row % quarter : row % quarter + here, :])
+            row, count = row + here, count - here
+        return parts[0] if len(parts) == 1 else jnp.concatenate(parts, axis=0)
+
+    @pl.when(is_dyn)
+    def _():
+        for l in range(3):
+            for first, source, count in ((0, 0, FEAT), (FEAT, FPAD, FEAT), (2 * FEAT, 2 * FPAD, MID_A)):
+                out_ref[pl.ds(3 * first + l, count, stride=3), :] = rows_at(
+                    l * A_ROWS + source, count
+                )
+
+    @pl.when(jnp.logical_not(is_dyn))
+    def _():
+        skip = MID_A - 96
+        for l in range(3):
+            for m in range(B_ROWS // 8):
+                value = rows_at((l * B_ROWS // 8 + m) * A_PIECE, 8)
+                value = value[skip:] if m == 0 else value
+                first = 0 if m == 0 else 8 * m - skip
+                out_ref[pl.ds(3 * first + l, value.shape[0], stride=3), :] = value
+        for l in range(3):
+            value = rows_at((3 * B_ROWS // 8 + l) * A_PIECE, 8)
+            value = jnp.concatenate([value] * 16, axis=0)
+            vec_ref[l * 128 : (l + 1) * 128, :] = value.T
+        vec_ref[HID:, :] = jnp.zeros((8, 128), f32)
+        lane = lane_ids((HID // 8, 128))
+        for k in range(PERIOD):
+            h, start = 128 * k // OUT, 128 * k
+            bound = OUT * (h + 1) - start
+            value = vec_ref[pl.ds(h, HID // 8, stride=8), :]
+            if bound < 128:
+                after = vec_ref[pl.ds(h + 1, HID // 8, stride=8), :]
+                value = jnp.where(lane < bound, value, after)
+            out_ref[pl.ds(OUT_AT + k, HID // 8, stride=PERIOD), :] = value * energy_ref[k : k + 1, :]
 
 
 def shape(dims, dtype):
@@ -604,29 +665,23 @@
         "final",
         16,
     )(table, field, own_out, back)[0]
-    for axis in ("x", "core"):
-        other = swap(piece, axis)
-        if axis == "x":
-            other, new = lax.optimization_barrier((other, new))
-        at_zero = lax.axis_index(axis) == 0
-        piece = jnp.concatenate(
-            [jnp.where(at_zero, piece, other), jnp.where(at_zero, other, piece)], axis=0
-        )
-    rows_a = piece.reshape(OWNERS * A_PIECE, 128)[: 3 * A_ROWS].reshape(3, A_ROWS, 128)
-    rows_a = rows_a.transpose(1, 0, 2)
-    mid_a = 98
-    flat_a = jnp.concatenate(
-        [rows_a[:FEAT], rows_a[FPAD : FPAD + FEAT], rows_a[2 * FPAD : 2 * FPAD + mid_a]]
-    ).reshape(-1)
-    all_b = piece[:, :B_PIECE].reshape(OWNERS * B_PIECE, 128)
-    rows_b = all_b[: 3 * B_ROWS].reshape(3, B_ROWS, 128).transpose(1, 0, 2)[mid_a - 96 :]
-    vec_sum = all_b[3 * B_ROWS : 3 * B_ROWS + 24 : 8].reshape(HID)
-    flat_b = jnp.concatenate(
-        [rows_b.reshape(-1), (vec_sum[:, None] * energy[None, :]).reshape(-1)]
-    )
-    grad_half = jnp.where(is_physics, flat_b, flat_a)
-
-    return new.reshape(columns.shape), grad_half
+    core_other = swap(piece, "core")
+    x_other = swap(piece, "x")
+    x_other, new = lax.optimization_barrier((x_other, new))
+    far = swap(x_other, "core")
+    energy_rows = jnp.tile(energy, 8).reshape(PERIOD, 128)
+    quarter = (OWNERS // 4 * A_PIECE, 128)
+    grad_half = vmem_call(
+        gather_kernel,
+        [shape((3 * (2 * FEAT + MID_A), 128), f32)],
+        [pltpu.VMEM((4,) + quarter, f32), pltpu.VMEM((HID + 8, 128), f32)],
+        "svvvvv",
+        10**7,
+        2 * 10**6,
+        "gather",
+        16,
+    )(table, *(value.reshape(quarter) for value in (piece, x_other, core_other, far)), energy_rows)[0]
+    return new.reshape(columns.shape), grad_half.reshape(-1)
 
 
 def solution(mesh):

time: 138 us -> 132 us (0.957)
  other arithmetic: 4.31 us -> 1.73 us
  local copies, waits for them, and re-layouts: 5.56 us -> 2.99 us
    select_n x3 -> x0, other arithmetic: 2.23 us -> none  [the longest x2 1.14 us: on_device(): jnp.where(at_zero, piece, other)]
    pallas_call x0 -> x1, Pallas kernels: none -> 2.14 us  [on_device(): vmem_call(gather_kernel, [shape((3 * (2 * FEAT + MID_A), 128), f32)], [pl...]
    pallas_call x1, Pallas kernels: 5.76 us -> 4.37 us  [on_device(): vmem_call(forward_kernel, [shape((2 * FPAD, MINE), bf16), shape((HID, MIN...]
    ppermute x5 -> x6, waiting for transfers between devices: 11.4 us -> 11 us  [swap(): return lax.ppermute(value, axis, [(0, 1), (1, 0)])]
    ppermute x5 -> x6, starting transfers between devices: 12.8 us -> 12.7 us  [swap(): return lax.ppermute(value, axis, [(0, 1), (1, 0)])]
  transfers between devices with their start and end apart: 10 -> 11, of which waited for: 7 -> 7; matrix products, arithmetic and copies ran while one was open for 1% -> 1% of each run, Pallas kernels for 3% -> 3%
where the time goes in v4:
time: 132 us
  blocking collectives  39.5 us (30%)
  starting transfers between devices  34.9 us (26%)
  waiting for transfers between devices  28.6 us (22%)
  Pallas kernels  23.3 us (18%)
  local copies, waits for them, and re-layouts  2.99 us (2%)
  other arithmetic  1.73 us (1%)
    all_to_all x1, blocking collectives, on_device(): lax.all_to_all(pieces, ('za', 'y', 'x', 'grp'), 0, 0, tiled=True)  24.1 us
    all_to_all x1, waiting for transfers between devices, on_device(): recv = lax.all_to_all(send, LON + ('grp',), 0, 0, tiled=True)  15.6 us
    all_to_all x1, blocking collectives, on_device(): lax.all_to_all(jnp.broadcast_to(piece[None], (members,) + piece.shape), r...  15.3 us
    ppermute x6, starting transfers between devices, swap(): return lax.ppermute(value, axis, [(0, 1), (1, 0)])  12.7 us
    ppermute x6, waiting for transfers between devices, swap(): return lax.ppermute(value, axis, [(0, 1), (1, 0)])  11 us
    all_to_all x1, starting transfers between devices, on_device(): recv = lax.all_to_all(send, LON + ('grp',), 0, 0, tiled=True)  8.25 us
    pallas_call x1, Pallas kernels, on_device(): vmem_call(transport_kernel, [shape((ROWS, FPAD, COLS), f32), shape((ROWS...  7.11 us
    ppermute x1, starting transfers between devices, on_device(): lax.ppermute(north_out, LAT, [(i, i + 1) for i in range(bands - 1)])  4.38 us
  transfers between devices with their start and end apart: 11, of which 7 were waited for; matrix products, arithmetic and copies ran while one was open for 1% of the time, Pallas kernels for 3%

profile of v4, /device:TPU:1, one launch (start us, length us, event | category | flops | bytes accessed | tf_op | source)
XLA Modules:
  0.0 131.9 jit_solution(1896031497492718306)
XLA Ops:
  0.6 3.0 %rim.1 = (bf16[128,128]{1,0:T(8,128)(2,1)}, bf16[128,128]{1,0:T(8,128)(2,1)}, bf16[576,128]{1,0:T(8,128)(2,1)}, s32[16,128]{1,0:T(8,128)}) custom-call(f32[4448,128]{1,0:T(8,128)} %bitcast.18, f32[16,128]{1,0:T(8,128)} %east_ref.1, f32[16,128]{1,0:T(8,128)} %north_ref.1, s32[8,16,16]{2,1,0:T(8,128)} %assign_hbm.1, s32[8,16,16]{2,1,0:T(8,128)} %cost_hbm.1), custom_call_target="tpu_custom_call" | custom-call | flops 100000000 | bytes 3000000 | tf_op jit(solution)/shard_map/rim/pallas_call | solution.py:544
  3.7 4.4 %collective-permute-start.1 = (bf16[576,128]{1,0:T(8,128)(2,1)}, bf16[576,128]{1,0:T(8,128)(2,1)S(1)}, u32[]{:S(2)}, u32[]{:S(2)}) collective-permute-start(bf16[576,128]{1,0:T(8,128)(2,1)} %get-tuple-element.24), channel_id=1, source_target_pairs={{0,32},{32,64},{64,96},{96,128},{128,160},{160,192},{192,224},{1,3... | collective-permute-start | bytes 442376 | tf_op jit(solution)/shard_map/ppermute | solution.py:567
  8.0 2.1 %collective-permute-start = (bf16[128,128]{1,0:T(8,128)(2,1)}, bf16[128,128]{1,0:T(8,128)(2,1)S(1)}, u32[]{:S(2)}, u32[]{:S(2)}) collective-permute-start(bf16[128,128]{1,0:T(8,128)(2,1)} %get-tuple-element.23), channel_id=1, source_target_pairs={{0,2},{2,4},{4,6},{6,8},{8,10},{10,12},{12,14},{14,16},{16,18},{18... | collective-permute-start | bytes 98312 | tf_op jit(solution)/shard_map/ppermute | solution.py:566
  10.2 3.3 %collective-permute-start.2 = (bf16[128,128]{1,0:T(8,128)(2,1)}, bf16[128,128]{1,0:T(8,128)(2,1)S(1)}, u32[]{:S(2)}, u32[]{:S(2)}) collective-permute-start(bf16[128,128]{1,0:T(8,128)(2,1)} %get-tuple-element.25), channel_id=1, source_target_pairs={{0,34},{2,36},{4,38},{6,40},{8,42},{10,44},{12,46},{14,48},{16,50}... | collective-permute-start | bytes 98312 | tf_op jit(solution)/shard_map/ppermute | solution.py:568
  13.5 1.3 collective-permute-done.2.corner_ref
  14.8 0.6 copy-done.10
  15.4 7.1 %transport.1 = (f32[16,288,128]{2,1,0:T(8,128)}, bf16[8,288,128]{2,1,0:T(8,128)(2,1)}, bf16[32,144,128]{2,1,0:T(8,128)(2,1)}) custom-call(s32[16,128]{1,0:T(8,128)} %get-tuple-element.22.table_ref, f32[4448,128]{1,0:T(8,128)} %bitcast.19, f32[16,128]{1,0:T(8,128)} %east_ref.1, f32[16,128]{1,0:T(8,128)} %north_ref.1, bf16[128,128]{1,0:T(8,128)(2,1)} %copy-done.9, ...), custom_call_target="tpu_custom_call" | custom-call | flops 100000000 | bytes 6000000 | tf_op jit(solution)/shard_map/transport/pallas_call | solution.py:587
  22.6 8.2 %all-to-all-start = ((bf16[32,144,128]{2,1,0:T(8,128)(2,1)}), bf16[32,144,128]{2,1,0:T(8,128)(2,1)S(1)}, u32[]{:S(2)}, u32[]{:S(2)}) async-start(bf16[32,144,128]{2,1,0:T(8,128)(2,1)} %get-tuple-element.27), calls=%async_computation | async-start | bytes 2359296 | tf_op jit(solution)/shard_map/all_to_all | solution.py:611
  30.9 0.3 copy.13
  31.1 0.2 copy.14
  31.4 0.4 copy-done.6
  32.4 0.2 fusion.4.w_one_ref
  32.5 15.6 %all-to-all-done.recv_ref = bf16[32,144,128]{2,1,0:T(8,128)(2,1)S(1)} async-done(((bf16[32,144,128]{2,1,0:T(8,128)(2,1)}), bf16[32,144,128]{2,1,0:T(8,128)(2,1)S(1)}, u32[]{:S(2)}, u32[]{:S(2)}) %all-to-all-start) | async-done | bytes 1179680 | tf_op jit(solution)/shard_map/all_to_all | solution.py:611
  48.1 4.4 %forward.1 = (bf16[576,1024]{1,0:T(8,128)(2,1)S(1)}, bf16[384,1024]{1,0:T(8,128)(2,1)S(1)}, bf16[384,1024]{1,0:T(8,128)(2,1)S(1)}, f32[384,1024]{1,0:T(8,128)S(1...) custom-call(s32[16,128]{1,0:T(8,128)S(1)} %copy-done.4, ...), custom_call_target="tpu_custom_call" | custom-call | flops 1207959552 | bytes 8000000 | tf_op jit(solution)/shard_map/forward/pallas_call | solution.py:612
  52.5 2.4 %backward.1 = (f32[64,24,128]{2,1,0:T(8,128)S(1)}, f32[64,24,128]{2,1,0:T(8,128)S(1)}) custom-call(s32[16,128]{1,0:T(8,128)S(1)} %copy-done.4, bf16[576,1024]{1,0:T(8,128)(2,1)S(1)} %get-tuple-element.28.inputs_ref, bf16[384,1024]{1,0:T(8,128)(2,1)S(1)} %get-tuple-element.29.hidden_ref, bf16[384,1024]{1,0:T(8,128)(2,1)S(1)} %get-tuple-element.30.g_two_ref, ...), custom_call_target="tpu_custom_call" | custom-call | flops 1056964608 | bytes 6000000 | tf_op jit(solution)/shard_map/backward/pallas_call | solution.py:631
  54.9 1.0 collective-permute-start.3
  55.9 4.2 %all-to-all-start.1 = ((bf16[32,144,128]{2,1,0:T(8,128)(2,1)}), bf16[32,144,128]{2,1,0:T(8,128)(2,1)S(1)}, u32[]{:S(2)}, u32[]{:S(2)}) async-start(bf16[32,144,128]{2,1,0:T(8,128)(2,1)} %get-tuple-element.35), calls=%async_computation.1 | async-start | bytes 2359296 | tf_op jit(solution)/shard_map/all_to_all | solution.py:630
  60.2 2.3 %collective-permute-start.4 = (bf16[32,24,128]{2,1,0:T(8,128)(2,1)S(1)}, bf16[32,24,128]{2,1,0:T(8,128)(2,1)S(1)}, u32[]{:S(2)}, u32[]{:S(2)}) collective-permute-start(bf16[32,24,128]{2,1,0:T(8,128)(2,1)S(1)} %dynamic-slice_convert_fusion), channel_id=1, source_target_pairs={{0,32},{32,0},{1,33},{33,1},{2,34},{34,2},{3,35},{35,3},{4,36},{36... | collective-permute-start | bytes 589832 | tf_op jit(solution)/shard_map/ppermute | solution.py:534
  62.5 5.1 %collective-permute-done.4 = bf16[32,24,128]{2,1,0:T(8,128)(2,1)S(1)} collective-permute-done((bf16[32,24,128]{2,1,0:T(8,128)(2,1)S(1)}, bf16[32,24,128]{2,1,0:T(8,128)(2,1)S(1)}, u32[]{:S(2)}, u32[]{:S(2)}) %collective-permute-start.4) | collective-permute-done | bytes 196640 | tf_op jit(solution)/shard_map/ppermute | solution.py:534
  67.7 4.3 %collective-permute-start.5 = (bf16[16,24,128]{2,1,0:T(8,128)(2,1)S(1)}, bf16[16,24,128]{2,1,0:T(8,128)(2,1)S(1)}, u32[]{:S(2)}, u32[]{:S(2)}) collective-permute-start(bf16[16,24,128]{2,1,0:T(8,128)(2,1)S(1)} %dynamic-slice_convert_fusion.1), channel_id=1, source_target_pairs={{0,64},{64,0},{1,65},{65,1},{2,66},{66,2},{3,67},{67,3},{4,68},{68... | collective-permute-start | bytes 294920 | tf_op jit(solution)/shard_map/ppermute | solution.py:534
  72.0 4.6 %collective-permute-done.5 = bf16[16,24,128]{2,1,0:T(8,128)(2,1)S(1)} collective-permute-done((bf16[16,24,128]{2,1,0:T(8,128)(2,1)S(1)}, bf16[16,24,128]{2,1,0:T(8,128)(2,1)S(1)}, u32[]{:S(2)}, u32[]{:S(2)}) %collective-permute-start.5) | collective-permute-done | bytes 98336 | tf_op jit(solution)/shard_map/ppermute | solution.py:534
  76.6 0.8 all-to-all-done.1.recv_ref
  77.4 24.1 %all_to_all.20 = f32[32,16,128]{2,1,0:T(8,128)} all-to-all(f32[32,16,128]{2,1,0:T(8,128)S(1)} %bitcast.23), channel_id=1, replica_groups=mesh['za'=2,'zb'=2,'zc'=2,'y'=4,'x'=2,'core'=2,'grp'=2] {'za','y','x','g..., dimensions={0} | all-to-all | bytes 524288 | tf_op jit(solution)/shard_map/all_to_all | solution.py:652
  101.6 1.0 reduce_sum.19
  102.6 15.3 %all_to_all.21 = f32[32,16,128]{2,1,0:T(8,128)} all-to-all(f32[32,16,128]{2,1,0:T(8,128)S(1)} %broadcast_in_dim.5), channel_id=1, replica_groups=mesh['za'=2,'zb'=2,'zc'=2,'y'=4,'x'=2,'core'=2,'grp'=2] {'za','zb','zc',..., dimensions={0} | all-to-all | bytes 524288 | tf_op jit(solution)/shard_map/all_to_all | solution.py:655
  118.0 1.1 copy-done.3
  119.1 4.3 %final.1 = f32[4448,128]{1,0:T(8,128)} custom-call(s32[16,128]{1,0:T(8,128)S(1)} %copy-done.4, f32[16,288,128]{2,1,0:T(8,128)S(1)} %copy-done, bf16[288,1024]{1,0:T(8,128)(2,1)S(1)} %copy-done.3, bf16[32,144,128]{2,1,0:T(8,128)(2,1)S(1)} %all-to-all-done.1.recv_ref), custom_call_target="tpu_custom_call" | custom-call | flops 10000000 | bytes 6000000 | tf_op jit(solution)/shard_map/final/pallas_call | solution.py:658
  123.3 4.0 %collective-permute-start.7 = (f32[32,16,128]{2,1,0:T(8,128)}, f32[32,16,128]{2,1,0:T(8,128)S(1)}, u32[]{:S(2)}, u32[]{:S(2)}) collective-permute-start(f32[32,16,128]{2,1,0:T(8,128)} %all_to_all.21), channel_id=1, source_target_pairs={{0,2},{2,0},{1,3},{3,1},{4,6},{6,4},{5,7},{7,5},{8,10},{10,8},{9,1... | collective-permute-start | bytes 786440 | tf_op jit(solution)/shard_map/ppermute | solution.py:534
  127.4 1.0 collective-permute-start.8
  128.5 0.3 collective-permute-done.7
  128.7 1.0 collective-permute-done.8
  129.7 2.1 %gather.1 = f32[1962,128]{1,0:T(8,128)} custom-call(s32[16,128]{1,0:T(8,128)S(1)} %copy-done.4, f32[512,128]{1,0:T(8,128)} %bitcast.8.mine_ref, f32[512,128]{1,0:T(8,128)} %bitcast.9.x_other_ref, f32[512,128]{1,0:T(8,128)S(1)} %bitcast.16, f32[512,128]{1,0:T(8,128)S(1)} %bitcast.17, f32[23,128]{1,0:T(8,128)S(1)} %reshape_tile.3.energy_ref), custom_call_target="tpu_custom_call" | custom-call | flops 10000000 | bytes 2000000 | tf_op jit(solution)/shard_map/gather/pallas_call | solution.py:674
  (45 shorter events, 1.1 us)
Async XLA Ops:
  3.7 11.1 %collective-permute-start.1 = (bf16[576,128]{1,0:T(8,128)(2,1)}, bf16[576,128]{1,0:T(8,128)(2,1)S(1)}, u32[]{:S(2)}, u32[]{:S(2)}) collective-permute-start(bf16[576,128]{1,0:T(8,128)(2,1)} %get-tuple-element.24), channel_id=1, source_target_pairs={{0,32},{32,64},{64,96},{96,128},{128,160},{160,192},{192,224},{1,3... | collective-permute-start | bytes 442376 | tf_op jit(solution)/shard_map/ppermute | solution.py:567
  8.0 5.4 %collective-permute-start = (bf16[128,128]{1,0:T(8,128)(2,1)}, bf16[128,128]{1,0:T(8,128)(2,1)S(1)}, u32[]{:S(2)}, u32[]{:S(2)}) collective-permute-start(bf16[128,128]{1,0:T(8,128)(2,1)} %get-tuple-element.23), channel_id=1, source_target_pairs={{0,2},{2,4},{4,6},{6,8},{8,10},{10,12},{12,14},{14,16},{16,18},{18... | collective-permute-start | bytes 98312 | tf_op jit(solution)/shard_map/ppermute | solution.py:566
  10.2 4.6 %collective-permute-start.2 = (bf16[128,128]{1,0:T(8,128)(2,1)}, bf16[128,128]{1,0:T(8,128)(2,1)S(1)}, u32[]{:S(2)}, u32[]{:S(2)}) collective-permute-start(bf16[128,128]{1,0:T(8,128)(2,1)} %get-tuple-element.25), channel_id=1, source_target_pairs={{0,34},{2,36},{4,38},{6,40},{8,42},{10,44},{12,46},{14,48},{16,50}... | collective-permute-start | bytes 98312 | tf_op jit(solution)/shard_map/ppermute | solution.py:568
  13.5 1.3 %copy-start.9 = (bf16[128,128]{1,0:T(8,128)(2,1)}, bf16[128,128]{1,0:T(8,128)(2,1)S(1)}, u32[]{:S(2)}) copy-start(bf16[128,128]{1,0:T(8,128)(2,1)S(1)} %collective-permute-done.rim_ref) | copy-start | bytes 98308
  14.8 0.6 copy-start.10
  14.8 0.7 copy-start.8
  22.6 8.3 %copy-start.7 = (bf16[556,384]{1,0:T(8,128)(2,1)S(1)}, bf16[556,384]{1,0:T(8,128)(2,1)}, u32[]{:S(2)}) copy-start(bf16[556,384]{1,0:T(8,128)(2,1)} %param.14) | copy-start | bytes 1281028
  22.6 8.6 %copy-start.1 = (bf16[384,384]{1,0:T(8,128)(2,1)S(1)}, bf16[384,384]{1,0:T(8,128)(2,1)}, u32[]{:S(2)}) copy-start(bf16[384,384]{1,0:T(8,128)(2,1)} %w_mid_ref.1) | copy-start | bytes 884740
  22.6 25.5 %all-to-all-start = ((bf16[32,144,128]{2,1,0:T(8,128)(2,1)}), bf16[32,144,128]{2,1,0:T(8,128)(2,1)S(1)}, u32[]{:S(2)}, u32[]{:S(2)}) async-start(bf16[32,144,128]{2,1,0:T(8,128)(2,1)} %get-tuple-element.27), calls=%async_computation | async-start | bytes 2359296 | tf_op jit(solution)/shard_map/all_to_all | solution.py:611
  30.8 1.0 copy-start.6
  30.8 1.0 copy-start.11
  32.2 15.9 %copy-start.4 = (s32[16,128]{1,0:T(8,128)S(1)}, s32[16,128]{1,0:T(8,128)}, u32[]{:S(2)}) copy-start(s32[16,128]{1,0:T(8,128)} %get-tuple-element.22.table_ref) | copy-start | bytes 24580
  32.2 15.9 %copy-start.5 = (bf16[8,288,128]{2,1,0:T(8,128)(2,1)S(1)}, bf16[8,288,128]{2,1,0:T(8,128)(2,1)}, u32[]{:S(2)}) copy-start(bf16[8,288,128]{2,1,0:T(8,128)(2,1)} %get-tuple-element.26.own_ref) | copy-start | bytes 1769476
  52.5 2.4 %copy-start.2 = (bf16[288,1024]{1,0:T(8,128)(2,1)}, bf16[288,1024]{1,0:T(8,128)(2,1)S(1)}, u32[]{:S(2)}) copy-start(bf16[288,1024]{1,0:T(8,128)(2,1)S(1)} %get-tuple-element.38.own_ref) | copy-start | bytes 1769476
  54.9 5.2 %collective-permute-start.3 = (f32[64,24,128]{2,1,0:T(8,128)S(1)}, f32[64,24,128]{2,1,0:T(8,128)S(1)}, u32[]{:S(2)}, u32[]{:S(2)}) collective-permute-start(f32[64,24,128]{2,1,0:T(8,128)S(1)} %get-tuple-element.34), channel_id=1, source_target_pairs={{0,2},{2,0},{1,3},{3,1},{4,6},{6,4},{5,7},{7,5},{8,10},{10,8},{9,1... | collective-permute-start | bytes 2359304 | tf_op jit(solution)/shard_map/ppermute | solution.py:534
  55.9 21.5 %all-to-all-start.1 = ((bf16[32,144,128]{2,1,0:T(8,128)(2,1)}), bf16[32,144,128]{2,1,0:T(8,128)(2,1)S(1)}, u32[]{:S(2)}, u32[]{:S(2)}) async-start(bf16[32,144,128]{2,1,0:T(8,128)(2,1)} %get-tuple-element.35), calls=%async_computation.1 | async-start | bytes 2359296 | tf_op jit(solution)/shard_map/all_to_all | solution.py:630
  60.2 7.4 %collective-permute-start.4 = (bf16[32,24,128]{2,1,0:T(8,128)(2,1)S(1)}, bf16[32,24,128]{2,1,0:T(8,128)(2,1)S(1)}, u32[]{:S(2)}, u32[]{:S(2)}) collective-permute-start(bf16[32,24,128]{2,1,0:T(8,128)(2,1)S(1)} %dynamic-slice_convert_fusion), channel_id=1, source_target_pairs={{0,32},{32,0},{1,33},{33,1},{2,34},{34,2},{3,35},{35,3},{4,36},{36... | collective-permute-start | bytes 589832 | tf_op jit(solution)/shard_map/ppermute | solution.py:534
  67.7 8.9 %collective-permute-start.5 = (bf16[16,24,128]{2,1,0:T(8,128)(2,1)S(1)}, bf16[16,24,128]{2,1,0:T(8,128)(2,1)S(1)}, u32[]{:S(2)}, u32[]{:S(2)}) collective-permute-start(bf16[16,24,128]{2,1,0:T(8,128)(2,1)S(1)} %dynamic-slice_convert_fusion.1), channel_id=1, source_target_pairs={{0,64},{64,0},{1,65},{65,1},{2,66},{66,2},{3,67},{67,3},{4,68},{68... | collective-permute-start | bytes 294920 | tf_op jit(solution)/shard_map/ppermute | solution.py:534
  77.4 40.6 %copy-start = (f32[16,288,128]{2,1,0:T(8,128)S(1)}, f32[16,288,128]{2,1,0:T(8,128)}, u32[]{:S(2)}) copy-start(f32[16,288,128]{2,1,0:T(8,128)} %get-tuple-element.37.field_ref) | copy-start | bytes 7077892
  117.9 9.4 %collective-permute-start.6 = (f32[32,16,128]{2,1,0:T(8,128)}, f32[32,16,128]{2,1,0:T(8,128)}, u32[]{:S(2)}, u32[]{:S(2)}) collective-permute-start(f32[32,16,128]{2,1,0:T(8,128)} %all_to_all.21), channel_id=1, source_target_pairs={{0,4},{4,0},{1,5},{5,1},{2,6},{6,2},{3,7},{7,3},{8,12},{12,8},{9,1... | collective-permute-start | bytes 786440 | tf_op jit(solution)/shard_map/ppermute | solution.py:534
  118.0 1.1 copy-start.3
  119.1 9.3 %copy-start.12 = (f32[368]{0:T(512)S(1)}, f32[368]{0:T(512)}, u32[]{:S(2)}) copy-start(f32[368]{0:T(512)} %param.17) | copy-start | bytes 4420
  123.3 5.4 %collective-permute-start.7 = (f32[32,16,128]{2,1,0:T(8,128)}, f32[32,16,128]{2,1,0:T(8,128)S(1)}, u32[]{:S(2)}, u32[]{:S(2)}) collective-permute-start(f32[32,16,128]{2,1,0:T(8,128)} %all_to_all.21), channel_id=1, source_target_pairs={{0,2},{2,0},{1,3},{3,1},{4,6},{6,4},{5,7},{7,5},{8,10},{10,8},{9,1... | collective-permute-start | bytes 786440 | tf_op jit(solution)/shard_map/ppermute | solution.py:534
  127.4 2.4 %collective-permute-start.8 = (f32[32,16,128]{2,1,0:T(8,128)}, f32[32,16,128]{2,1,0:T(8,128)S(1)}, u32[]{:S(2)}, u32[]{:S(2)}) collective-permute-start(f32[32,16,128]{2,1,0:T(8,128)} %collective-permute-done.6), channel_id=1, source_target_pairs={{0,2},{2,0},{1,3},{3,1},{4,6},{6,4},{5,7},{7,5},{8,10},{10,8},{9,1... | collective-permute-start | bytes 786440 | tf_op jit(solution)/shard_map/ppermute | solution.py:534

commit v5 on v4

--- a/solution.py
+++ b/solution.py
@@ -174,11 +174,9 @@
     after_top = (
         keep[top] * q_top + west[top] * pltpu.roll(q_top, 1, 1) + south[top] * q_under
     )
-    north_out_ref[0:FEAT, :] = (north[top] * q_top).astype(bf16)
-    north_out_ref[FPAD : FPAD + FEAT, :] = (north[top] * after_top).astype(bf16)
-    pad = jnp.broadcast_to(north[top], (FPAD - FEAT, COLS)).astype(bf16)
-    north_out_ref[FEAT:FPAD, :] = pad
-    north_out_ref[FPAD + FEAT :, :] = pad
+    pad = jnp.broadcast_to(north[top], (FPAD - FEAT, COLS))
+    for at, flux in ((0, north[top] * q_top), (FPAD, north[top] * after_top)):
+        north_out_ref[at : at + FPAD, :] = jnp.concatenate([flux, pad], axis=0).astype(bf16)
 
 
 def transport_kernel(
@@ -243,7 +241,7 @@
     for i, copy in enumerate(x_in):
         copy.wait()
         first, end = 8 * i, min(8 * i + 8, GROUPS)
-        lax.fori_loop(first, end, group, 0, unroll=4 if end - first == 8 else True)
+        lax.fori_loop(first, end, group, 0, unroll=True)
         part = pl.ds(8 * first, 8 * (end - first) if end < GROUPS else FPAD - 8 * first)
         field_out.append(
             pltpu.make_async_copy(
@@ -645,8 +643,10 @@
         at = lax.axis_index(axis)
         other = lax.dynamic_slice_in_dim(grad, (1 - at) * pieces, pieces)
         keep = lax.dynamic_slice_in_dim(grad, at * pieces, pieces)
-        grad = keep + swap(other.astype(bf16), axis).astype(f32)
-    grad, back = lax.optimization_barrier((grad, back))
+        other = swap(other.astype(bf16), axis)
+        if axis == "zb":
+            other, back = lax.optimization_barrier((other, back))
+        grad = keep + other.astype(f32)
     pieces_b = jnp.pad(grad[:, A_PIECE:], ((0, 0), (0, A_PIECE - B_PIECE), (0, 0)))
     pieces = jnp.stack([grad[:, :A_PIECE], pieces_b], axis=1).reshape(-1, A_PIECE, 128)
     piece = jnp.sum(lax.all_to_all(pieces, ("za", "y", "x", "grp"), 0, 0, tiled=True), axis=0)

time: 132 us -> 133 us (level)
  no operation moved by 1% of the time
where the time goes in v5:
time: 133 us; the launch traced here: 132 us
  blocking collectives  39.5 us (30%)
  starting transfers between devices  35 us (26%)
  waiting for transfers between devices  28.5 us (21%)
  Pallas kernels  23.3 us (18%)
  local copies, waits for them, and re-layouts  2.99 us (2%)
  other arithmetic  1.73 us (1%)
    all_to_all x1, blocking collectives, on_device(): lax.all_to_all(pieces, ('za', 'y', 'x', 'grp'), 0, 0, tiled=True)  24.2 us
    all_to_all x1, waiting for transfers between devices, on_device(): recv = lax.all_to_all(send, LON + ('grp',), 0, 0, tiled=True)  15.6 us
    all_to_all x1, blocking collectives, on_device(): lax.all_to_all(jnp.broadcast_to(piece[None], (members,) + piece.shape), r...  15.4 us
    ppermute x6, starting transfers between devices, swap(): return lax.ppermute(value, axis, [(0, 1), (1, 0)])  12.8 us
    ppermute x6, waiting for transfers between devices, swap(): return lax.ppermute(value, axis, [(0, 1), (1, 0)])  11 us
    all_to_all x1, starting transfers between devices, on_device(): recv = lax.all_to_all(send, LON + ('grp',), 0, 0, tiled=True)  8.25 us
    pallas_call x1, Pallas kernels, on_device(): vmem_call(transport_kernel, [shape((ROWS, FPAD, COLS), f32), shape((ROWS...  7.15 us
    ppermute x1, starting transfers between devices, on_device(): lax.ppermute(north_out, LAT, [(i, i + 1) for i in range(bands - 1)])  4.38 us
  transfers between devices with their start and end apart: 11, of which 7 were waited for; matrix products, arithmetic and copies ran while one was open for 1% of the time, Pallas kernels for 3%

profile of v5, /device:TPU:1, one launch (start us, length us, event | category | flops | bytes accessed | tf_op | source)
XLA Modules:
  0.0 132.0 jit_solution(2521987608782286502)
XLA Ops:
  0.6 3.0 %rim.1 = (bf16[128,128]{1,0:T(8,128)(2,1)}, bf16[128,128]{1,0:T(8,128)(2,1)}, bf16[576,128]{1,0:T(8,128)(2,1)}, s32[16,128]{1,0:T(8,128)}) custom-call(f32[4448,128]{1,0:T(8,128)} %bitcast.18, f32[16,128]{1,0:T(8,128)} %east_ref.1, f32[16,128]{1,0:T(8,128)} %north_ref.1, s32[8,16,16]{2,1,0:T(8,128)} %assign_hbm.1, s32[8,16,16]{2,1,0:T(8,128)} %cost_hbm.1), custom_call_target="tpu_custom_call" | custom-call | flops 100000000 | bytes 3000000 | tf_op jit(solution)/shard_map/rim/pallas_call | solution.py:542
  3.7 4.4 %collective-permute-start.1 = (bf16[576,128]{1,0:T(8,128)(2,1)}, bf16[576,128]{1,0:T(8,128)(2,1)S(1)}, u32[]{:S(2)}, u32[]{:S(2)}) collective-permute-start(bf16[576,128]{1,0:T(8,128)(2,1)} %get-tuple-element.24), channel_id=1, source_target_pairs={{0,32},{32,64},{64,96},{96,128},{128,160},{160,192},{192,224},{1,3... | collective-permute-start | bytes 442376 | tf_op jit(solution)/shard_map/ppermute | solution.py:565
  8.0 2.1 %collective-permute-start = (bf16[128,128]{1,0:T(8,128)(2,1)}, bf16[128,128]{1,0:T(8,128)(2,1)S(1)}, u32[]{:S(2)}, u32[]{:S(2)}) collective-permute-start(bf16[128,128]{1,0:T(8,128)(2,1)} %get-tuple-element.23), channel_id=1, source_target_pairs={{0,2},{2,4},{4,6},{6,8},{8,10},{10,12},{12,14},{14,16},{16,18},{18... | collective-permute-start | bytes 98312 | tf_op jit(solution)/shard_map/ppermute | solution.py:564
  10.2 3.3 %collective-permute-start.2 = (bf16[128,128]{1,0:T(8,128)(2,1)}, bf16[128,128]{1,0:T(8,128)(2,1)S(1)}, u32[]{:S(2)}, u32[]{:S(2)}) collective-permute-start(bf16[128,128]{1,0:T(8,128)(2,1)} %get-tuple-element.25), channel_id=1, source_target_pairs={{0,34},{2,36},{4,38},{6,40},{8,42},{10,44},{12,46},{14,48},{16,50}... | collective-permute-start | bytes 98312 | tf_op jit(solution)/shard_map/ppermute | solution.py:566
  13.5 1.3 collective-permute-done.2.corner_ref
  14.8 0.6 copy-done.10
  15.4 7.1 %transport.1 = (f32[16,288,128]{2,1,0:T(8,128)}, bf16[8,288,128]{2,1,0:T(8,128)(2,1)}, bf16[32,144,128]{2,1,0:T(8,128)(2,1)}) custom-call(s32[16,128]{1,0:T(8,128)} %get-tuple-element.22.table_ref, f32[4448,128]{1,0:T(8,128)} %bitcast.19, f32[16,128]{1,0:T(8,128)} %east_ref.1, f32[16,128]{1,0:T(8,128)} %north_ref.1, bf16[128,128]{1,0:T(8,128)(2,1)} %copy-done.9, ...), custom_call_target="tpu_custom_call" | custom-call | flops 100000000 | bytes 6000000 | tf_op jit(solution)/shard_map/transport/pallas_call | solution.py:585
  22.6 8.2 %all-to-all-start = ((bf16[32,144,128]{2,1,0:T(8,128)(2,1)}), bf16[32,144,128]{2,1,0:T(8,128)(2,1)S(1)}, u32[]{:S(2)}, u32[]{:S(2)}) async-start(bf16[32,144,128]{2,1,0:T(8,128)(2,1)} %get-tuple-element.27), calls=%async_computation | async-start | bytes 2359296 | tf_op jit(solution)/shard_map/all_to_all | solution.py:609
  30.9 0.3 copy.13
  31.2 0.2 copy.14
  31.4 0.4 copy-done.6
  32.4 0.2 fusion.4.w_one_ref
  32.6 15.6 %all-to-all-done.recv_ref = bf16[32,144,128]{2,1,0:T(8,128)(2,1)S(1)} async-done(((bf16[32,144,128]{2,1,0:T(8,128)(2,1)}), bf16[32,144,128]{2,1,0:T(8,128)(2,1)S(1)}, u32[]{:S(2)}, u32[]{:S(2)}) %all-to-all-start) | async-done | bytes 1179680 | tf_op jit(solution)/shard_map/all_to_all | solution.py:609
  48.1 4.4 %forward.1 = (bf16[576,1024]{1,0:T(8,128)(2,1)S(1)}, bf16[384,1024]{1,0:T(8,128)(2,1)S(1)}, bf16[384,1024]{1,0:T(8,128)(2,1)S(1)}, f32[384,1024]{1,0:T(8,128)S(1...) custom-call(s32[16,128]{1,0:T(8,128)S(1)} %copy-done.4, ...), custom_call_target="tpu_custom_call" | custom-call | flops 1207959552 | bytes 8000000 | tf_op jit(solution)/shard_map/forward/pallas_call | solution.py:610
  52.5 2.4 %backward.1 = (f32[64,24,128]{2,1,0:T(8,128)S(1)}, f32[64,24,128]{2,1,0:T(8,128)S(1)}) custom-call(s32[16,128]{1,0:T(8,128)S(1)} %copy-done.4, bf16[576,1024]{1,0:T(8,128)(2,1)S(1)} %get-tuple-element.28.inputs_ref, bf16[384,1024]{1,0:T(8,128)(2,1)S(1)} %get-tuple-element.29.hidden_ref, bf16[384,1024]{1,0:T(8,128)(2,1)S(1)} %get-tuple-element.30.g_two_ref, ...), custom_call_target="tpu_custom_call" | custom-call | flops 1056964608 | bytes 6000000 | tf_op jit(solution)/shard_map/backward/pallas_call | solution.py:629
  54.9 1.0 collective-permute-start.3
  55.9 4.2 %all-to-all-start.1 = ((bf16[32,144,128]{2,1,0:T(8,128)(2,1)}), bf16[32,144,128]{2,1,0:T(8,128)(2,1)S(1)}, u32[]{:S(2)}, u32[]{:S(2)}) async-start(bf16[32,144,128]{2,1,0:T(8,128)(2,1)} %get-tuple-element.35), calls=%async_computation.1 | async-start | bytes 2359296 | tf_op jit(solution)/shard_map/all_to_all | solution.py:628
  60.2 2.4 %collective-permute-start.4 = (bf16[32,24,128]{2,1,0:T(8,128)(2,1)S(1)}, bf16[32,24,128]{2,1,0:T(8,128)(2,1)S(1)}, u32[]{:S(2)}, u32[]{:S(2)}) collective-permute-start(bf16[32,24,128]{2,1,0:T(8,128)(2,1)S(1)} %dynamic-slice_convert_fusion), channel_id=1, source_target_pairs={{0,32},{32,0},{1,33},{33,1},{2,34},{34,2},{3,35},{35,3},{4,36},{36... | collective-permute-start | bytes 589832 | tf_op jit(solution)/shard_map/ppermute | solution.py:532
  62.7 5.1 %collective-permute-done.4 = bf16[32,24,128]{2,1,0:T(8,128)(2,1)S(1)} collective-permute-done((bf16[32,24,128]{2,1,0:T(8,128)(2,1)S(1)}, bf16[32,24,128]{2,1,0:T(8,128)(2,1)S(1)}, u32[]{:S(2)}, u32[]{:S(2)}) %collective-permute-start.4) | collective-permute-done | bytes 196640 | tf_op jit(solution)/shard_map/ppermute | solution.py:532
  67.9 4.3 %collective-permute-start.5 = (bf16[16,24,128]{2,1,0:T(8,128)(2,1)S(1)}, bf16[16,24,128]{2,1,0:T(8,128)(2,1)S(1)}, u32[]{:S(2)}, u32[]{:S(2)}) collective-permute-start(bf16[16,24,128]{2,1,0:T(8,128)(2,1)S(1)} %dynamic-slice_convert_fusion.1), channel_id=1, source_target_pairs={{0,64},{64,0},{1,65},{65,1},{2,66},{66,2},{3,67},{67,3},{4,68},{68... | collective-permute-start | bytes 294920 | tf_op jit(solution)/shard_map/ppermute | solution.py:532
  72.2 4.6 %collective-permute-done.5 = bf16[16,24,128]{2,1,0:T(8,128)(2,1)S(1)} collective-permute-done((bf16[16,24,128]{2,1,0:T(8,128)(2,1)S(1)}, bf16[16,24,128]{2,1,0:T(8,128)(2,1)S(1)}, u32[]{:S(2)}, u32[]{:S(2)}) %collective-permute-start.5) | collective-permute-done | bytes 98336 | tf_op jit(solution)/shard_map/ppermute | solution.py:532
  76.7 0.6 all-to-all-done.1.recv_ref
  77.5 24.2 %all_to_all.20 = f32[32,16,128]{2,1,0:T(8,128)} all-to-all(f32[32,16,128]{2,1,0:T(8,128)S(1)} %bitcast.23), channel_id=1, replica_groups=mesh['za'=2,'zb'=2,'zc'=2,'y'=4,'x'=2,'core'=2,'grp'=2] {'za','y','x','g..., dimensions={0} | all-to-all | bytes 524288 | tf_op jit(solution)/shard_map/all_to_all | solution.py:652
  101.6 1.0 reduce_sum.19
  102.6 15.4 %all_to_all.21 = f32[32,16,128]{2,1,0:T(8,128)} all-to-all(f32[32,16,128]{2,1,0:T(8,128)S(1)} %broadcast_in_dim.5), channel_id=1, replica_groups=mesh['za'=2,'zb'=2,'zc'=2,'y'=4,'x'=2,'core'=2,'grp'=2] {'za','zb','zc',..., dimensions={0} | all-to-all | bytes 524288 | tf_op jit(solution)/shard_map/all_to_all | solution.py:655
  118.1 1.1 copy-done.3
  119.1 4.3 %final.1 = f32[4448,128]{1,0:T(8,128)} custom-call(s32[16,128]{1,0:T(8,128)S(1)} %copy-done.4, f32[16,288,128]{2,1,0:T(8,128)S(1)} %copy-done, bf16[288,1024]{1,0:T(8,128)(2,1)S(1)} %copy-done.3, bf16[32,144,128]{2,1,0:T(8,128)(2,1)S(1)} %all-to-all-done.1.recv_ref), custom_call_target="tpu_custom_call" | custom-call | flops 10000000 | bytes 6000000 | tf_op jit(solution)/shard_map/final/pallas_call | solution.py:658
  123.4 4.0 %collective-permute-start.7 = (f32[32,16,128]{2,1,0:T(8,128)}, f32[32,16,128]{2,1,0:T(8,128)S(1)}, u32[]{:S(2)}, u32[]{:S(2)}) collective-permute-start(f32[32,16,128]{2,1,0:T(8,128)} %all_to_all.21), channel_id=1, source_target_pairs={{0,2},{2,0},{1,3},{3,1},{4,6},{6,4},{5,7},{7,5},{8,10},{10,8},{9,1... | collective-permute-start | bytes 786440 | tf_op jit(solution)/shard_map/ppermute | solution.py:532
  127.4 1.0 collective-permute-start.8
  128.5 0.3 collective-permute-done.7
  128.8 1.0 collective-permute-done.8
  129.8 2.1 %gather.1 = f32[1962,128]{1,0:T(8,128)} custom-call(s32[16,128]{1,0:T(8,128)S(1)} %copy-done.4, f32[512,128]{1,0:T(8,128)} %bitcast.8.mine_ref, f32[512,128]{1,0:T(8,128)} %bitcast.9.x_other_ref, f32[512,128]{1,0:T(8,128)S(1)} %bitcast.16, f32[512,128]{1,0:T(8,128)S(1)} %bitcast.17, f32[23,128]{1,0:T(8,128)S(1)} %reshape_tile.3.energy_ref), custom_call_target="tpu_custom_call" | custom-call | flops 10000000 | bytes 2000000 | tf_op jit(solution)/shard_map/gather/pallas_call | solution.py:674
  (45 shorter events, 1.1 us)
Async XLA Ops:
  3.7 11.1 %collective-permute-start.1 = (bf16[576,128]{1,0:T(8,128)(2,1)}, bf16[576,128]{1,0:T(8,128)(2,1)S(1)}, u32[]{:S(2)}, u32[]{:S(2)}) collective-permute-start(bf16[576,128]{1,0:T(8,128)(2,1)} %get-tuple-element.24), channel_id=1, source_target_pairs={{0,32},{32,64},{64,96},{96,128},{128,160},{160,192},{192,224},{1,3... | collective-permute-start | bytes 442376 | tf_op jit(solution)/shard_map/ppermute | solution.py:565
  8.0 5.4 %collective-permute-start = (bf16[128,128]{1,0:T(8,128)(2,1)}, bf16[128,128]{1,0:T(8,128)(2,1)S(1)}, u32[]{:S(2)}, u32[]{:S(2)}) collective-permute-start(bf16[128,128]{1,0:T(8,128)(2,1)} %get-tuple-element.23), channel_id=1, source_target_pairs={{0,2},{2,4},{4,6},{6,8},{8,10},{10,12},{12,14},{14,16},{16,18},{18... | collective-permute-start | bytes 98312 | tf_op jit(solution)/shard_map/ppermute | solution.py:564
  10.2 4.6 %collective-permute-start.2 = (bf16[128,128]{1,0:T(8,128)(2,1)}, bf16[128,128]{1,0:T(8,128)(2,1)S(1)}, u32[]{:S(2)}, u32[]{:S(2)}) collective-permute-start(bf16[128,128]{1,0:T(8,128)(2,1)} %get-tuple-element.25), channel_id=1, source_target_pairs={{0,34},{2,36},{4,38},{6,40},{8,42},{10,44},{12,46},{14,48},{16,50}... | collective-permute-start | bytes 98312 | tf_op jit(solution)/shard_map/ppermute | solution.py:566
  13.5 1.3 %copy-start.9 = (bf16[128,128]{1,0:T(8,128)(2,1)}, bf16[128,128]{1,0:T(8,128)(2,1)S(1)}, u32[]{:S(2)}) copy-start(bf16[128,128]{1,0:T(8,128)(2,1)S(1)} %collective-permute-done.rim_ref) | copy-start | bytes 98308
  14.8 0.6 copy-start.10
  14.8 0.7 copy-start.8
  22.6 8.3 %copy-start.7 = (bf16[556,384]{1,0:T(8,128)(2,1)S(1)}, bf16[556,384]{1,0:T(8,128)(2,1)}, u32[]{:S(2)}) copy-start(bf16[556,384]{1,0:T(8,128)(2,1)} %param.14) | copy-start | bytes 1281028
  22.6 8.6 %copy-start.1 = (bf16[384,384]{1,0:T(8,128)(2,1)S(1)}, bf16[384,384]{1,0:T(8,128)(2,1)}, u32[]{:S(2)}) copy-start(bf16[384,384]{1,0:T(8,128)(2,1)} %w_mid_ref.1) | copy-start | bytes 884740
  22.6 25.5 %all-to-all-start = ((bf16[32,144,128]{2,1,0:T(8,128)(2,1)}), bf16[32,144,128]{2,1,0:T(8,128)(2,1)S(1)}, u32[]{:S(2)}, u32[]{:S(2)}) async-start(bf16[32,144,128]{2,1,0:T(8,128)(2,1)} %get-tuple-element.27), calls=%async_computation | async-start | bytes 2359296 | tf_op jit(solution)/shard_map/all_to_all | solution.py:609
  30.9 1.0 copy-start.6
  30.9 1.0 copy-start.11
  32.2 15.9 %copy-start.4 = (s32[16,128]{1,0:T(8,128)S(1)}, s32[16,128]{1,0:T(8,128)}, u32[]{:S(2)}) copy-start(s32[16,128]{1,0:T(8,128)} %get-tuple-element.22.table_ref) | copy-start | bytes 24580
  32.2 15.9 %copy-start.5 = (bf16[8,288,128]{2,1,0:T(8,128)(2,1)S(1)}, bf16[8,288,128]{2,1,0:T(8,128)(2,1)}, u32[]{:S(2)}) copy-start(bf16[8,288,128]{2,1,0:T(8,128)(2,1)} %get-tuple-element.26.own_ref) | copy-start | bytes 1769476
  52.5 2.4 %copy-start.2 = (bf16[288,1024]{1,0:T(8,128)(2,1)}, bf16[288,1024]{1,0:T(8,128)(2,1)S(1)}, u32[]{:S(2)}) copy-start(bf16[288,1024]{1,0:T(8,128)(2,1)S(1)} %get-tuple-element.38.own_ref) | copy-start | bytes 1769476
  54.9 5.2 %collective-permute-start.3 = (f32[64,24,128]{2,1,0:T(8,128)S(1)}, f32[64,24,128]{2,1,0:T(8,128)S(1)}, u32[]{:S(2)}, u32[]{:S(2)}) collective-permute-start(f32[64,24,128]{2,1,0:T(8,128)S(1)} %get-tuple-element.34), channel_id=1, source_target_pairs={{0,2},{2,0},{1,3},{3,1},{4,6},{6,4},{5,7},{7,5},{8,10},{10,8},{9,1... | collective-permute-start | bytes 2359304 | tf_op jit(solution)/shard_map/ppermute | solution.py:532
  55.9 21.5 %all-to-all-start.1 = ((bf16[32,144,128]{2,1,0:T(8,128)(2,1)}), bf16[32,144,128]{2,1,0:T(8,128)(2,1)S(1)}, u32[]{:S(2)}, u32[]{:S(2)}) async-start(bf16[32,144,128]{2,1,0:T(8,128)(2,1)} %get-tuple-element.35), calls=%async_computation.1 | async-start | bytes 2359296 | tf_op jit(solution)/shard_map/all_to_all | solution.py:628
  60.2 7.6 %collective-permute-start.4 = (bf16[32,24,128]{2,1,0:T(8,128)(2,1)S(1)}, bf16[32,24,128]{2,1,0:T(8,128)(2,1)S(1)}, u32[]{:S(2)}, u32[]{:S(2)}) collective-permute-start(bf16[32,24,128]{2,1,0:T(8,128)(2,1)S(1)} %dynamic-slice_convert_fusion), channel_id=1, source_target_pairs={{0,32},{32,0},{1,33},{33,1},{2,34},{34,2},{3,35},{35,3},{4,36},{36... | collective-permute-start | bytes 589832 | tf_op jit(solution)/shard_map/ppermute | solution.py:532
  67.9 8.9 %collective-permute-start.5 = (bf16[16,24,128]{2,1,0:T(8,128)(2,1)S(1)}, bf16[16,24,128]{2,1,0:T(8,128)(2,1)S(1)}, u32[]{:S(2)}, u32[]{:S(2)}) collective-permute-start(bf16[16,24,128]{2,1,0:T(8,128)(2,1)S(1)} %dynamic-slice_convert_fusion.1), channel_id=1, source_target_pairs={{0,64},{64,0},{1,65},{65,1},{2,66},{66,2},{3,67},{67,3},{4,68},{68... | collective-permute-start | bytes 294920 | tf_op jit(solution)/shard_map/ppermute | solution.py:532
  77.4 40.7 %copy-start = (f32[16,288,128]{2,1,0:T(8,128)S(1)}, f32[16,288,128]{2,1,0:T(8,128)}, u32[]{:S(2)}) copy-start(f32[16,288,128]{2,1,0:T(8,128)} %get-tuple-element.37.field_ref) | copy-start | bytes 7077892
  118.0 9.4 %collective-permute-start.6 = (f32[32,16,128]{2,1,0:T(8,128)}, f32[32,16,128]{2,1,0:T(8,128)}, u32[]{:S(2)}, u32[]{:S(2)}) collective-permute-start(f32[32,16,128]{2,1,0:T(8,128)} %all_to_all.21), channel_id=1, source_target_pairs={{0,4},{4,0},{1,5},{5,1},{2,6},{6,2},{3,7},{7,3},{8,12},{12,8},{9,1... | collective-permute-start | bytes 786440 | tf_op jit(solution)/shard_map/ppermute | solution.py:532
  118.1 1.1 copy-start.3
  119.1 9.3 %copy-start.12 = (f32[368]{0:T(512)S(1)}, f32[368]{0:T(512)}, u32[]{:S(2)}) copy-start(f32[368]{0:T(512)} %param.17) | copy-start | bytes 4420
  123.4 5.4 %collective-permute-start.7 = (f32[32,16,128]{2,1,0:T(8,128)}, f32[32,16,128]{2,1,0:T(8,128)S(1)}, u32[]{:S(2)}, u32[]{:S(2)}) collective-permute-start(f32[32,16,128]{2,1,0:T(8,128)} %all_to_all.21), channel_id=1, source_target_pairs={{0,2},{2,0},{1,3},{3,1},{4,6},{6,4},{5,7},{7,5},{8,10},{10,8},{9,1... | collective-permute-start | bytes 786440 | tf_op jit(solution)/shard_map/ppermute | solution.py:532
  127.4 2.4 %collective-permute-start.8 = (f32[32,16,128]{2,1,0:T(8,128)}, f32[32,16,128]{2,1,0:T(8,128)S(1)}, u32[]{:S(2)}, u32[]{:S(2)}) collective-permute-start(f32[32,16,128]{2,1,0:T(8,128)} %collective-permute-done.6), channel_id=1, source_target_pairs={{0,2},{2,0},{1,3},{3,1},{4,6},{6,4},{5,7},{7,5},{8,10},{10,8},{9,1... | collective-permute-start | bytes 786440 | tf_op jit(solution)/shard_map/ppermute | solution.py:532
